TPU v7x, 32 devices: a whole 2x2x4 slice. The times are simulated.
32 devices in a mesh: tm: 4 (over y, x), line: 8 (over z, core).
Axes of the slice: x: 2, y: 2, z: 4, core: 2. Of those that a mesh axis runs over, the one named last changes fastest.
Arguments:
- station_traces: bfloat16 [256, 16384], P('line', 'tm'), may hold values from -6 to 6
- shot_onset_ticks: int32 [64], P('line'), may hold values from 0 to 16383, as said below
- span_place_index: int32 [64], P('line'), may hold values from 0 to 31, as said below
- spectral_keep_flags: int32 [64, 512], replicated, may hold values 0 or 1
Outputs:
- deblended: bfloat16 [128, 256, 1024], P('tm', 'line')
Inputs may be any that keep to these rules, and one draw needn't show every extreme that they name: The block of 4096 samples holding shot_onset_ticks[s] owns shot s; each block owns at most 32 shots and one owns exactly 32. `span_place_index`: shots owned by the same block have distinct slots.
All inputs are finite; a program needn't handle non-finite values.
Results may differ from a plain program's by a relative error of at most 0.0078.
Values may be sent and summed in bfloat16 or wider, within the bound.
No kernel may reach another device: no remote copies, remote signals or barrier semaphores. Data moves between devices by JAX's collectives and lax.ppermute only.
A program may use at most 64 MiB of HBM per device.

v0:
```python
import math

import jax
import jax.numpy as jnp
from jax import lax
from jax.sharding import PartitionSpec as P


def make_tables(window, shots):
    times = jnp.arange(window, dtype=jnp.int32)
    freqs = jnp.arange(window // 2, dtype=jnp.int32)
    phase = (times[:, None] * freqs[None, :] % window).astype(jnp.float32) * (
        2.0 * math.pi / window
    )
    cosine = jnp.cos(phase)
    sine = jnp.sin(phase)
    forward = jnp.concatenate([cosine, -sine], axis=1).astype(jnp.bfloat16)
    halves = jnp.where(freqs == 0, 0.5, 1.0).astype(jnp.float32)[:, None]
    inverse = jnp.concatenate([halves * cosine.T, -halves * sine.T], axis=0).astype(jnp.bfloat16)
    order = jnp.arange(shots, dtype=jnp.int32)
    turn = (order[:, None] * order[None, :] % shots).astype(jnp.float32) * (2.0 * math.pi / shots)
    return (
        forward,
        inverse,
        jnp.cos(turn).astype(jnp.bfloat16),
        jnp.sin(turn).astype(jnp.bfloat16),
    )


def filter_gathers(station_panels, keep_mask, tables):
    forward, inverse, shot_cos, shot_sin = tables
    shots, count_here, window = station_panels.shape
    freqs = window // 2
    spectrum = jnp.dot(
        station_panels.reshape(shots * count_here, window),
        forward,
        preferred_element_type=jnp.float32,
    )
    spectrum = spectrum.astype(jnp.bfloat16).reshape(shots, count_here * window)
    cos_part = jnp.dot(shot_cos, spectrum, preferred_element_type=jnp.float32).reshape(
        shots, count_here, 2, freqs
    )
    sin_part = jnp.dot(shot_sin, spectrum, preferred_element_type=jnp.float32).reshape(
        shots, count_here, 2, freqs
    )
    sign_pair = jnp.array([1.0, -1.0], dtype=jnp.float32)[:, None]
    masked = (cos_part + sin_part[:, :, ::-1, :] * sign_pair) * keep_mask[:, None, None, :]
    masked = masked.astype(jnp.bfloat16).reshape(shots, count_here * window)
    cos_back = jnp.dot(shot_cos, masked, preferred_element_type=jnp.float32).reshape(
        shots, count_here, 2, freqs
    )
    sin_back = jnp.dot(shot_sin, masked, preferred_element_type=jnp.float32).reshape(
        shots, count_here, 2, freqs
    )
    mixed = (
        (cos_back - sin_back[:, :, ::-1, :] * sign_pair)
        .astype(jnp.bfloat16)
        .reshape(shots * count_here, window)
    )
    filtered = jnp.dot(mixed, inverse, preferred_element_type=jnp.float32) * (
        2.0 / (window * shots)
    )
    return filtered.astype(jnp.bfloat16).reshape(shots, count_here, window)


def cut_windows(traces, starts, window):
    rec_rows, length = traces.shape
    block_count = length // window + 2
    padded = jnp.pad(traces, ((0, 0), (0, block_count * window - length)))
    blocks = jnp.swapaxes(padded.reshape(rec_rows, block_count, window), 0, 1)
    first_block = starts // window
    within = starts % window
    paired = jnp.concatenate(
        [jnp.take(blocks, first_block, axis=0), jnp.take(blocks, first_block + 1, axis=0)], axis=2
    )
    current = 2 * window
    level = (window - 1).bit_length()
    for bit_pos in reversed(range(level)):
        stride = 1 << bit_pos
        narrower = current - stride
        moved = within >> bit_pos & 1 == 1
        paired = jnp.where(
            moved[:, None, None], paired[:, :, stride:current], paired[:, :, :narrower]
        )
        current = narrower
    return paired[:, :, :window]


def on_device(station_traces, shot_onset_ticks, span_place_index, spectral_keep_flags):
    tm_count = lax.axis_size("tm")
    rec_rows, block_len = station_traces.shape
    shots, freqs = spectral_keep_flags.shape
    window = 2 * freqs
    capacity = 2 * shots // tm_count
    per_peer = rec_rows // tm_count
    fire_all, slot_all = (
        lax.all_gather(shot_onset_ticks, "line", axis=0, tiled=True),
        lax.all_gather(span_place_index, "line", axis=0, tiled=True),
    )
    span_holders = fire_all // block_len
    tables = make_tables(window, shots)
    keep_mask = spectral_keep_flags.astype(jnp.float32)
    slot_code = slot_all * tm_count + span_holders
    all_codes = jnp.arange(capacity * tm_count, dtype=jnp.int32)
    matched = slot_code[:, None] == all_codes[None, :]
    sources = jnp.arange(shots, dtype=jnp.int32)
    summed = jnp.sum(jnp.where(matched, sources[:, None], 0), axis=0)
    slot_source = jnp.where(jnp.any(matched, axis=0), summed, shots)
    stacked = station_traces.reshape(tm_count, per_peer, block_len)
    station_panels = cut_windows(
        lax.all_to_all(stacked, "tm", split_axis=0, concat_axis=2, tiled=True)[0], fire_all, window
    )
    filtered = filter_gathers(station_panels, keep_mask, tables)
    count_here = filtered.shape[1]
    slotted = jnp.take(filtered, slot_source, axis=0, mode="fill", fill_value=0)
    slotted = slotted.reshape(capacity, tm_count, count_here, window)
    result = lax.all_to_all(slotted, "tm", split_axis=1, concat_axis=1, tiled=True)
    return result.reshape(capacity, rec_rows, window)


def solution(mesh):
    in_specs = (P("line", "tm"), P("line"), P("line"), P())
    out_specs = P("tm", "line", None)
    return jax.shard_map(
        on_device, mesh=mesh, in_specs=in_specs, out_specs=out_specs, check_vma=False
    )
```

profile of v0, /device:TPU:0, one launch (start us, length us, event | category | flops | bytes accessed | tf_op | source)
XLA Modules:
  0.0 88.2 jit_solution(15858018681813760894)
XLA Ops:
  0.0 5.3 %all-to-all-start = ((bf16[4,8,4096]{2,1,0:T(8,128)(2,1)}), bf16[4,8,4096]{2,1,0:T(8,128)(2,1)S(1)}, u32[]{:S(2)}, u32[]{:S(2)}) async-start(bf16[4,8,4096]{2,1,0:T(8,128)(2,1)} %bitcast.54), calls=%async_computation | async-start | bytes 524288 | tf_op jit(solution)/shard_map/all_to_all | solution.py:111
  5.3 9.2 %negate_convert_fusion = (bf16[1024,512]{1,0:T(8,128)(2,1)S(1)}, bf16[1024,512]{1,0:T(8,128)(2,1)}) fusion(), kind=kLoop, calls=%fused_computation.33 | loop fusion | flops 8912896 | bytes 2097152 | tf_op jit(solution)/shard_map/convert.3
  14.5 0.6 dynamic-slice
  16.3 9.2 %all-reduce.3 = (s32[64]{0:T(128)S(1)}, s32[64]{0:T(128)S(1)}) all-reduce(s32[64]{0:T(128)S(1)} %dynamic-update-slice.1, s32[64]{0:T(128)S(1)} %dynamic-update-slice), channel_id=1, replica_groups=mesh['tm'=4,'line'=8] {'line'}, use_global_device_ids=true, to_apply=%add.2 | all-reduce | flops 128 | bytes 1024
  25.7 0.7 convert_element_type.54
  26.5 9.6 %multiply_convert_fusion.1 = (bf16[512,1024]{1,0:T(8,128)(2,1)}, bf16[512,1024]{1,0:T(8,128)(2,1)}) fusion(f32[512]{0:T(512)S(1)} %fusion.54, f32[512]{0:T(512)S(1)} %fusion.53), kind=kLoop, calls=%fused_computation.27 | loop fusion | flops 9437184 | bytes 2101248 | tf_op jit(solution)/shard_map/convert.1
  36.2 0.6 gather_fusion.1
  36.8 0.6 gather_fusion.2
  37.8 0.6 fusion.23
  41.9 0.8 fusion.74
  43.1 1.3 %fusion.24 = bf16[512,1024]{1,0:T(8,128)(2,1)S(1)} fusion(bf16[1024,512]{1,0:T(8,128)(2,1)S(1)} %get-tuple-element.30, bf16[1024,512]{1,0:T(8,128)(2,1)S(1)} %copy-done, bf16[64,8,1025]{2,1,0:T(8,128)(2,1)S(1)} %get-tuple-element.16, bf16[64,8,1025]{2,1,0:T(8,128)(2,1)S(1)} %get-tuple-element.15, pred[64]{0:T(512)(128)(4,1)S(1)} %get-tuple-element.10), kind=kOutput, calls=%fused_computation.43 | convolution fusion | flops 1078984704 | bytes 5243392 | tf_op jit(solution)/shard_map/dot_general | solution.py:34
  44.9 0.8 dot_general.28
  45.8 1.5 %fusion.37 = f32[64,8,2,512]{3,0,2,1:T(8,128)S(1)} fusion(bf16[8,2,512,64]{2,1,0,3:T(2,128)(2,1)S(1)} %dot_general.28), kind=kOutput, calls=%fused_computation.63 | convolution fusion | flops 67170304 | bytes 3145728 | tf_op jit(solution)/shard_map/dot_general | solution.py:43
  47.3 1.7 %multiply_convert_fusion.3 = bf16[64,8,2,512]{3,0,2,1:T(8,128)(2,1)S(1)} fusion(f32[64,8,2,512]{3,0,2,1:T(8,128)S(1)} %fusion.37, f32[64,512]{1,0:T(8,128)S(1)} %copy-done.3, f32[2]{0:T(128)S(1)} %copy-done.5, bf16[8,2,512,64]{2,1,0,3:T(2,128)(2,1)S(1)} %dot_general.28), kind=kOutput, calls=%fused_computation.32 | convolution fusion | flops 69267456 | bytes 4325384 | tf_op jit(solution)/shard_map/dot_general | solution.py:40
  49.0 1.1 %copy.29 = bf16[64,8,2,512]{3,2,1,0:T(2,128)(2,1)S(1)} copy(bf16[64,8,2,512]{3,0,2,1:T(8,128)(2,1)S(1)} %multiply_convert_fusion.3) | data formatting | bytes 2097152 | tf_op jit(solution)/shard_map/convert_element_type | solution.py:48
  50.0 0.8 reshape.99
  50.9 1.0 %dot_general.32 = bf16[8,2,512,64]{2,1,0,3:T(2,128)(2,1)S(1)} reshape(bf16[8192,64]{0,1:T(8,128)(2,1)S(1)} %bitcast.51) | data formatting | bytes 2097152 | tf_op jit(solution)/shard_map/dot_general | solution.py:49
  51.9 1.5 %fusion.34 = f32[64,8,2,512]{3,0,2,1:T(8,128)S(1)} fusion(bf16[8,2,512,64]{2,1,0,3:T(2,128)(2,1)S(1)} %dot_general.32), kind=kOutput, calls=%fused_computation.60 | convolution fusion | flops 67170304 | bytes 3145728 | tf_op jit(solution)/shard_map/dot_general | solution.py:52
  53.4 1.6 %subtract_convert_fusion = bf16[64,8,2,512]{3,0,2,1:T(8,128)(2,1)S(1)} fusion(f32[64,8,2,512]{3,0,2,1:T(8,128)S(1)} %fusion.34, f32[2]{0:T(128)S(1)} %copy-done.5, bf16[8,2,512,64]{2,1,0,3:T(2,128)(2,1)S(1)} %dot_general.32), kind=kOutput, calls=%fused_computation.31 | convolution fusion | flops 68743168 | bytes 4194312 | tf_op jit(solution)/shard_map/dot_general | solution.py:49
  55.0 1.1 %copy.49 = bf16[64,8,2,512]{3,2,1,0:T(2,128)(2,1)S(1)} copy(bf16[64,8,2,512]{3,0,2,1:T(8,128)(2,1)S(1)} %subtract_convert_fusion) | data formatting | bytes 2097152 | tf_op jit(solution)/shard_map/convert_element_type | solution.py:57
  56.5 1.3 %fusion.27 = bf16[64,8,1024]{2,1,0:T(8,128)(2,1)S(1)} fusion(bf16[512,1024]{1,0:T(8,128)(2,1)S(1)} %bitcast.53, bf16[512,1024]{1,0:T(8,128)(2,1)S(1)} %copy-done.1, bf16[512,1024]{1,0:T(8,128)(2,1)S(1)} %copy-done.2), kind=kOutput, calls=%fused_computation.44 | convolution fusion | flops 1078984704 | bytes 4194304 | tf_op jit(solution)/shard_map/dot_general | solution.py:60
  57.8 0.7 gather_fusion
  58.9 27.8 %all_to_all.20 = bf16[32,4,8,1024]{3,2,0,1:T(8,128)(2,1)S(1)} all-to-all(bf16[32,4,8,1024]{3,2,0,1:T(8,128)(2,1)S(1)} %copy.33), channel_id=1, replica_groups=mesh['tm'=4,'line'=8] {'tm'}, dimensions={1} | all-to-all | bytes 4194304 | tf_op jit(solution)/shard_map/all_to_all | solution.py:117
  86.8 1.5 %copy.48 = bf16[32,4,8,1024]{3,2,1,0:T(8,128)(2,1)} copy(bf16[32,4,8,1024]{3,2,0,1:T(8,128)(2,1)S(1)} %all_to_all.20) | data formatting | bytes 4194304 | tf_op jit(solution)/shard_map/all_to_all | solution.py:117
  (52 shorter events, 6.5 us)
Async XLA Ops:
  0.0 14.5 %copy-start.8 = (u32[32]{0:T(128)S(1)}, u32[32]{0:T(128)}, u32[]{:S(2)}) copy-start(u32[32]{0:T(128)} %constant.126) | copy-start | bytes 388
  0.0 15.8 %copy-start.6 = (s32[8]{0:T(128)S(1)}, s32[8]{0:T(128)}, u32[]{:S(2)}) copy-start(s32[8]{0:T(128)} %param.9) | copy-start | bytes 100
  0.0 16.1 %copy-start.7 = (s32[8]{0:T(128)S(1)}, s32[8]{0:T(128)}, u32[]{:S(2)}) copy-start(s32[8]{0:T(128)} %param.8) | copy-start | bytes 100
  0.0 25.7 %copy-start.4 = (s32[64,512]{1,0:T(8,128)S(1)}, s32[64,512]{1,0:T(8,128)}, u32[]{:S(2)}) copy-start(s32[64,512]{1,0:T(8,128)} %param.10) | copy-start | bytes 393220
  0.0 36.1 %all-to-all-start = ((bf16[4,8,4096]{2,1,0:T(8,128)(2,1)}), bf16[4,8,4096]{2,1,0:T(8,128)(2,1)S(1)}, u32[]{:S(2)}, u32[]{:S(2)}) async-start(bf16[4,8,4096]{2,1,0:T(8,128)(2,1)} %bitcast.54), calls=%async_computation | async-start | bytes 524288 | tf_op jit(solution)/shard_map/all_to_all | solution.py:111
  41.8 1.2 %copy-start = (bf16[1024,512]{1,0:T(8,128)(2,1)S(1)}, bf16[1024,512]{1,0:T(8,128)(2,1)}, u32[]{:S(2)}) copy-start(bf16[1024,512]{1,0:T(8,128)(2,1)} %get-tuple-element.31) | copy-start | bytes 3145732
  45.7 1.5 %copy-start.3 = (f32[64,512]{1,0:T(8,128)S(1)}, f32[64,512]{1,0:T(8,128)}, u32[]{:S(2)}) copy-start(f32[64,512]{1,0:T(8,128)} %convert_element_type.54) | copy-start | bytes 393220
  45.7 1.5 %copy-start.5 = (f32[2]{0:T(128)S(1)}, f32[2]{0:T(128)}, u32[]{:S(2)}) copy-start(f32[2]{0:T(128)} %constant.121.clone) | copy-start | bytes 28
  55.0 1.4 %copy-start.1 = (bf16[512,1024]{1,0:T(8,128)(2,1)S(1)}, bf16[512,1024]{1,0:T(8,128)(2,1)}, u32[]{:S(2)}) copy-start(bf16[512,1024]{1,0:T(8,128)(2,1)} %get-tuple-element.32) | copy-start | bytes 3145732
  55.0 1.5 %copy-start.2 = (bf16[512,1024]{1,0:T(8,128)(2,1)S(1)}, bf16[512,1024]{1,0:T(8,128)(2,1)}, u32[]{:S(2)}) copy-start(bf16[512,1024]{1,0:T(8,128)(2,1)} %get-tuple-element.33) | copy-start | bytes 3145732
where the time goes:
time: 88.6 us; the launch traced here: 88.2 us
  blocking collectives  37 us (42%)
  other arithmetic  24.3 us (27%)
  local copies, waits for them, and re-layouts  11.8 us (13%)
  matrix products  8.86 us (10%)
  starting transfers between devices  5.32 us (6%)
  between operations  0.96 us (1%)
    all_to_all x1, blocking collectives, on_device(): lax.all_to_all(slotted, 'tm', split_axis=1, concat_axis=1, tiled=True)  27.8 us
    another operation x2, other arithmetic  18.8 us
    unnamed x1, blocking collectives  9.17 us
    all_to_all x1, starting transfers between devices, on_device(): lax.all_to_all(stacked, 'tm', split_axis=0, concat_axis=2, tiled=True)[0]  5.32 us
    select_n x9, other arithmetic, cut_windows(): jnp.where(moved[:, None, None], paired[:, :, stride:current], paired[:, :...  4.03 us
    unnamed x24, local copies, waits for them, and re-layouts  1.99 us
  transfers between devices with their start and end apart: 1, of which 0 were waited for; matrix products, arithmetic and copies ran while one was open for 24% of the time, Pallas kernels for 0%

commit v1 on v0

v1 whole, which is shorter than its diff:
```python
import functools
import math

import jax
import jax.numpy as jnp
import ml_dtypes
import numpy as np
from jax import lax
from jax.experimental import pallas as pl
from jax.experimental.pallas import tpu as pltpu
from jax.sharding import PartitionSpec as P

LANES = 128
RECS = 16


def make_tables(window, shots):
    half = window // 2
    quarter = half // 2
    times = np.arange(half)
    freqs = np.concatenate([np.arange(0, half, 2), np.arange(1, half, 2)])

    def waves(rows, columns, period):
        phase = (rows[:, None] * columns[None, :] % period) * (2.0 * math.pi / period)
        return np.cos(phase), np.sin(phase)

    bf16 = ml_dtypes.bfloat16
    cosine, sine = waves(times, freqs, window)
    forward = np.stack(
        [
            np.concatenate([cosine[:, cut], -sine[:, cut]], axis=1)
            for cut in (slice(0, quarter), slice(quarter, half))
        ]
    ).astype(bf16)
    gain = np.where(freqs == 0, 0.5, 1.0)[:, None] * (2.0 / (window * shots))
    inverse = np.stack(
        [
            np.concatenate([gain[cut] * cosine.T[cut], -gain[cut] * sine.T[cut]], axis=0)
            for cut in (slice(0, quarter), slice(quarter, half))
        ]
    ).astype(bf16)
    turn_cos, turn_sin = waves(np.arange(shots), np.arange(shots), shots)
    over_shots = np.block([[turn_cos, turn_sin], [-turn_sin, turn_cos]]).astype(bf16)
    back_rows = np.stack(
        [
            np.concatenate([turn_cos, -turn_sin], axis=1),
            np.concatenate([turn_sin, turn_cos], axis=1),
        ]
    ).astype(bf16)
    shift_cos, shift_sin = waves(np.arange(LANES), freqs, window)
    shifts = np.concatenate([shift_cos, shift_sin], axis=1)
    high = shifts.astype(bf16)
    low = (shifts - high.astype(np.float64)).astype(bf16)
    order = np.zeros((half, half), bf16)
    order[freqs, np.arange(half)] = 1
    return forward, inverse, over_shots, back_rows, np.stack([high, low]), order


def gather_kernel(
    ticks,
    places,
    here,
    traces,
    keep,
    forward,
    inverse,
    over_shots,
    back_rows,
    shifts,
    out,
    tiles,
    folds,
    spectra,
    turns,
    back,
    mixed,
):
    peers, recs, block_len = traces.shape
    shots, half = keep.shape
    window = 2 * half
    quarter = half // 2
    slots = out.shape[0]
    wide = window // LANES
    mid = wide // 2
    per_block = block_len // LANES
    f32, bf16 = jnp.float32, jnp.bfloat16

    for peer in range(peers):
        for tile in range(per_block):
            tiles[peer * per_block + tile] = traces[peer, :, tile * LANES : (tile + 1) * LANES]
    for tile in range(wide):
        tiles[peers * per_block + tile] = jnp.zeros((recs, LANES), bf16)

    lane = lax.broadcasted_iota(jnp.int32, (recs, LANES), 1)

    def cut(shot, carry):
        tick = ticks[shot]
        first = tick // LANES
        within = tick % LANES
        piece = [tiles[first + tile] for tile in range(wide)]
        last = tiles[first + wide]
        piece[0] = jnp.where(lane < within, last.astype(f32), piece[0].astype(f32)).astype(bf16)
        row = pl.multiple_of(shot * recs, recs)
        for tile in range(mid):
            at = slice(tile * LANES, (tile + 1) * LANES)
            folds[0, pl.ds(row, recs), at] = piece[tile] + piece[tile + mid]
            folds[1, pl.ds(row, recs), at] = piece[tile] - piece[tile + mid]
        return carry

    lax.fori_loop(0, shots, cut, 0, unroll=8)

    shot_row = lax.broadcasted_iota(jnp.int32, (shots, LANES), 0)
    shot_lane = lax.broadcasted_iota(jnp.int32, (1, shots), 1)
    within_all = jnp.zeros((shots, LANES), jnp.int32)
    place_all = jnp.full((1, shots), -1, jnp.int32)
    for shot in range(shots):
        tick = ticks[shot]
        within_all = jnp.where(shot_row == shot, tick % LANES, within_all)
        place = jnp.where(tick // block_len == here[0], places[shot], -1)
        place_all = jnp.where(shot_lane == shot, place, place_all)
    shift_lane = lax.broadcasted_iota(jnp.int32, (shots, LANES), 1)
    picks = (within_all == shift_lane).astype(f32).astype(bf16)
    turns[...] = jnp.dot(picks, shifts[0], preferred_element_type=f32) + jnp.dot(
        picks, shifts[1], preferred_element_type=f32
    )
    slot_row = lax.broadcasted_iota(jnp.int32, (slots, shots), 0)
    owned = (slot_row == place_all).astype(f32).astype(bf16)
    for part in range(2):
        back[part * slots : (part + 1) * slots] = jnp.dot(
            owned, back_rows[part], preferred_element_type=f32
        ).astype(bf16)

    rows = shots * recs
    step = min(rows, 256)
    for part in range(2):
        for row in range(0, rows, step):
            found = jnp.dot(
                folds[part, row : row + step], forward[part], preferred_element_type=f32
            )
            for tile in range(mid):
                spectra[part * mid + tile, row : row + step] = found[
                    :, tile * LANES : (tile + 1) * LANES
                ]

    arms = mid // 2
    for rec in range(recs):
        real, imag = [], []
        for tile in range(mid):
            part, arm = tile // arms, tile % arms
            at = slice(tile * LANES, (tile + 1) * LANES)
            cos_turn = turns[:, at]
            sin_turn = turns[:, half + tile * LANES : half + (tile + 1) * LANES]
            cos_part = spectra[part * mid + arm, pl.ds(rec, shots, stride=recs), :]
            sin_part = spectra[part * mid + arms + arm, pl.ds(rec, shots, stride=recs), :]
            real.append((cos_part * cos_turn - sin_part * sin_turn).astype(bf16))
            imag.append((cos_part * sin_turn + sin_part * cos_turn).astype(bf16))
        stacked = jnp.concatenate(
            [jnp.concatenate(real, axis=1), jnp.concatenate(imag, axis=1)], axis=0
        )
        waves = jnp.dot(over_shots[...], stacked, preferred_element_type=f32)
        masked = jnp.concatenate(
            [waves[:shots] * keep[...], waves[shots:] * keep[...]], axis=0
        ).astype(bf16)
        again = jnp.dot(back[...], masked, preferred_element_type=f32)
        for tile in range(mid):
            part, arm = tile // arms, tile % arms
            at = slice(tile * LANES, (tile + 1) * LANES)
            to = pl.ds(rec, slots, stride=recs)
            mixed[part * mid + arm, to, :] = again[:slots, at]
            mixed[part * mid + arms + arm, to, :] = again[slots:, at]

    group = max(1, min(slots, 256 // recs))
    for slot in range(0, slots, group):
        at = slice(slot * recs, (slot + group) * recs)
        even, odd = [
            jnp.dot(
                jnp.concatenate(
                    [mixed[part * mid + tile, at].astype(bf16) for tile in range(mid)], axis=1
                ),
                inverse[part],
                preferred_element_type=f32,
            )
            for part in range(2)
        ]
        out[slot : slot + group, :, :half] = (even + odd).reshape(group, recs, half).astype(bf16)
        out[slot : slot + group, :, half:] = (even - odd).reshape(group, recs, half).astype(bf16)


def filter_gathers(ticks, places, here, traces, keep, tables):
    forward, inverse, over_shots, back_rows, shifts = tables
    peers, rec_rows, block_len = traces.shape
    shots, half = keep.shape
    window = 2 * half
    slots = 2 * shots // peers
    recs = RECS
    total = peers * block_len
    smem = pl.BlockSpec(memory_space=pltpu.SMEM)

    def whole(array):
        return pl.BlockSpec(array.shape, lambda step: (0,) * array.ndim)

    sizes = (
        8 * peers * recs * block_len
        + 4 * 2 * 2 * shots * recs * half
        + 12 * shots * recs * half
        + 8 * slots * recs * window
        + 4 * slots * recs * window
        + 8 * (forward.size + inverse.size + over_shots.size + back_rows.size + shifts.size)
    )
    flops = 2 * rec_rows * (
        shots * window * half
        + slots * window * half
        + 4 * shots * shots * half
        + 4 * slots * shots * half
    )
    return pl.pallas_call(
        gather_kernel,
        grid=(rec_rows // recs,),
        out_shape=jax.ShapeDtypeStruct((slots, rec_rows, window), jnp.bfloat16),
        in_specs=[
            smem,
            smem,
            smem,
            pl.BlockSpec((peers, recs, block_len), lambda step: (0, step, 0)),
            whole(keep),
            whole(forward),
            whole(inverse),
            whole(over_shots),
            whole(back_rows),
            whole(shifts),
        ],
        out_specs=pl.BlockSpec((slots, recs, window), lambda step: (0, step, 0)),
        scratch_shapes=[
            pltpu.VMEM(((total + window) // LANES, recs, LANES), jnp.bfloat16),
            pltpu.VMEM((2, shots * recs, half), jnp.bfloat16),
            pltpu.VMEM((window // LANES, shots * recs, LANES), jnp.float32),
            pltpu.VMEM((shots, window), jnp.float32),
            pltpu.VMEM((2 * slots, 2 * shots), jnp.bfloat16),
            pltpu.VMEM((window // LANES, slots * recs, LANES), jnp.float32),
        ],
        compiler_params=pltpu.CompilerParams(vmem_limit_bytes=min(sizes + (12 << 20), 60 << 20)),
        cost_estimate=pl.CostEstimate(
            flops=flops, bytes_accessed=2 * (traces.size + slots * rec_rows * window), transcendentals=0
        ),
    )(ticks, places, here, traces, keep, forward, inverse, over_shots, back_rows, shifts)


def on_device(station_traces, shot_onset_ticks, span_place_index, spectral_keep_flags):
    shots, half = spectral_keep_flags.shape
    *tables, order = make_tables(2 * half, shots)
    traces = lax.all_gather(station_traces, "tm", axis=0)
    ticks = lax.all_gather(shot_onset_ticks, "line", axis=0, tiled=True)
    places = lax.all_gather(span_place_index, "line", axis=0, tiled=True)
    here = lax.axis_index("tm").astype(jnp.int32).reshape(1)
    keep = jnp.dot(
        spectral_keep_flags.astype(jnp.bfloat16), order, preferred_element_type=jnp.float32
    )
    return filter_gathers(ticks, places, here, traces, keep, tables)


def solution(mesh):
    in_specs = (P("line", "tm"), P("line"), P("line"), P())
    out_specs = P("tm", "line", None)
    return jax.shard_map(
        on_device, mesh=mesh, in_specs=in_specs, out_specs=out_specs, check_vma=False
    )
```

time: 88.6 us -> 67.3 us (0.76)
  blocking collectives: 37 us -> 10.6 us
  other arithmetic: 24.3 us -> 0 us
  waiting for transfers between devices: 0.01 us -> 16.5 us
  Pallas kernels: 0 us -> 15.2 us
  between operations: 0.96 us -> 14.1 us
  matrix products: 8.86 us -> 1.31 us
  starting transfers between devices: 5.32 us -> 0.01 us
  local copies, waits for them, and re-layouts: 11.8 us -> 9.17 us
    all_to_all x1 -> x0, blocking collectives: 27.8 us -> none  [on_device(): lax.all_to_all(slotted, 'tm', split_axis=1, concat_axis=1, tiled=True)]
    another operation x2 -> x0, other arithmetic: 18.8 us -> none
    all_gather x0 -> x1, waiting for transfers between devices: none -> 15.8 us  [on_device(): traces = lax.all_gather(station_traces, 'tm', axis=0)]
    pallas_call x0 -> x1, Pallas kernels: none -> 15.2 us  [filter_gathers(): pl.pallas_call(gather_kernel, grid=(rec_rows // recs,), out_shape=jax.Sha...]
    dot_general x6 -> x1, matrix products: 8.86 us -> 1.31 us  [on_device(): jnp.dot(spectral_keep_flags.astype(jnp.bfloat16), order, preferred_elemen...]
    unnamed x24 -> x17, local copies, waits for them, and re-layouts: 1.99 us -> 9.17 us
    all_to_all x1 -> x0, starting transfers between devices: 5.32 us -> none  [on_device(): lax.all_to_all(stacked, 'tm', split_axis=0, concat_axis=2, tiled=True)[0]]
    select_n x15 -> x0, other arithmetic: 4.6 us -> none  [the longest x9 4.03 us: cut_windows(): jnp.where(moved[:, None, None], paired[:, :, stride:current], paired[:, :...]
  transfers between devices with their start and end apart: 1 -> 1, of which waited for: 0 -> 1; matrix products, arithmetic and copies ran while one was open for 24% -> 6% of each run, Pallas kernels for 0% -> 0%
where the time goes in v1:
time: 67.3 us; the launch traced here: 66.8 us
  waiting for transfers between devices  16.5 us (25%)
  Pallas kernels  15.2 us (23%)
  between operations  14.1 us (21%)
  blocking collectives  10.6 us (16%)
  local copies, waits for them, and re-layouts  9.17 us (14%)
  matrix products  1.31 us (2%)
    all_gather x1, waiting for transfers between devices, on_device(): traces = lax.all_gather(station_traces, 'tm', axis=0)  15.8 us
    pallas_call x1, Pallas kernels, filter_gathers(): pl.pallas_call(gather_kernel, grid=(rec_rows // recs,), out_shape=jax.Sha...  15.2 us
    unnamed x1, blocking collectives  10.6 us
    unnamed x17, local copies, waits for them, and re-layouts  9.17 us
  transfers between devices with their start and end apart: 1, of which 1 were waited for; matrix products, arithmetic and copies ran while one was open for 6% of the time, Pallas kernels for 0%

profile of v1, /device:TPU:0, one launch (start us, length us, event | category | flops | bytes accessed | tf_op | source)
XLA Modules:
  0.0 66.8 jit_solution(3998215887935241246)
XLA Ops:
  6.5 0.0 all-gather.3.cloned.1.call-start
  6.5 0.7 %all-gather.3.cloned.1.call-update = ((bf16[32,4096]{1,0:T(8,128)(2,1)}), bf16[128,4096]{1,0:T(8,128)(2,1)}) async-update(((), (), s32[]{:S(2)}) %all-gather.3.cloned.1.call-start, bf16[32,4096]{1,0:T(8,128)(2,1)} %param.10) | async-update | bytes 1572888
  7.3 1.2 %dynamic-slice = u32[1]{0:T(128)} dynamic-slice(u32[32]{0:T(128)} %constant.25, u32[]{:T(128)S(6)} %add), dynamic_slice_sizes={1} | dynamic-slice | bytes 12
  9.2 0.9 %dynamic-update-slice = s32[64]{0:T(128)S(1)} dynamic-update-slice(s32[64]{0:T(128)S(1)} %broadcast.clone, s32[8]{0:T(128)} %param.11, u32[]{:T(128)} %bitcast) | dynamic-update-slice | bytes 68
  10.0 0.8 %dynamic-update-slice.1 = s32[64]{0:T(128)S(1)} dynamic-update-slice(s32[64]{0:T(128)S(1)} %broadcast.clone.1, s32[8]{0:T(128)} %param.12, u32[]{:T(128)} %bitcast) | dynamic-update-slice | bytes 68
  10.9 10.6 %all-reduce.2 = (s32[64]{0:T(128)S(1)}, s32[64]{0:T(128)S(1)}) all-reduce(s32[64]{0:T(128)S(1)} %dynamic-update-slice, s32[64]{0:T(128)S(1)} %dynamic-update-slice.1), channel_id=1, replica_groups=mesh['tm'=4,'line'=8] {'line'}, use_global_device_ids=true, to_apply=%add | all-reduce | flops 128 | bytes 1024
  21.5 1.3 %convolution_bitcast_fusion.keep = f32[64,512]{1,0:T(8,128)S(1)} fusion(bf16[512,512]{1,0:T(8,128)(2,1)} %constant.17.clone, s32[64,512]{1,0:T(8,128)} %param.13), kind=kOutput, calls=%fused_computation | convolution fusion | flops 33587200 | bytes 786432 | tf_op jit(solution)/shard_map/dot_general | solution.py:255
  22.8 15.8 %all-gather.3.cloned.1.call-done = bf16[128,4096]{1,0:T(8,128)(2,1)} async-done(((bf16[32,4096]{1,0:T(8,128)(2,1)}), bf16[128,4096]{1,0:T(8,128)(2,1)}) %all-gather.3.cloned.1.call-update) | async-done | bytes 1048592 | tf_op jit(solution)/shard_map/all_gather | solution.py:251
  38.6 0.0 copy-start
  38.6 1.2 %copy-done = bf16[128,4096]{1,0:T(8,128)(2,1)S(1)} copy-done((bf16[128,4096]{1,0:T(8,128)(2,1)S(1)}, bf16[128,4096]{1,0:T(8,128)(2,1)}, u32[]{:S(2)}) %copy-start) | copy-done | bytes 1048600
  39.8 0.0 copy-start.1
  39.8 1.2 %copy-done.1 = bf16[2,512,512]{2,1,0:T(8,128)(2,1)S(1)} copy-done((bf16[2,512,512]{2,1,0:T(8,128)(2,1)S(1)}, bf16[2,512,512]{2,1,0:T(8,128)(2,1)}, u32[]{:S(2)}) %copy-start.1) | copy-done | bytes 1048600
  41.0 0.0 copy-start.2
  41.0 1.2 %copy-done.2 = bf16[2,512,512]{2,1,0:T(8,128)(2,1)S(1)} copy-done((bf16[2,512,512]{2,1,0:T(8,128)(2,1)S(1)}, bf16[2,512,512]{2,1,0:T(8,128)(2,1)}, u32[]{:S(2)}) %copy-start.2) | copy-done | bytes 1048600
  42.2 0.0 copy-start.3
  42.2 1.0 %copy-done.3 = bf16[2,128,1024]{2,1,0:T(8,128)(2,1)S(1)} copy-done((bf16[2,128,1024]{2,1,0:T(8,128)(2,1)S(1)}, bf16[2,128,1024]{2,1,0:T(8,128)(2,1)}, u32[]{:S(2)}) %copy-start.3) | copy-done | bytes 524312
  43.3 0.0 copy-start.4
  43.3 0.8 %copy-done.4 = bf16[2,64,128]{2,1,0:T(8,128)(2,1)S(1)} copy-done((bf16[2,64,128]{2,1,0:T(8,128)(2,1)S(1)}, bf16[2,64,128]{2,1,0:T(8,128)(2,1)}, u32[]{:S(2)}) %copy-start.4) | copy-done | bytes 32792
  44.0 0.0 copy-start.5
  44.0 0.8 %copy-done.5 = bf16[128,128]{1,0:T(8,128)(2,1)S(1)} copy-done((bf16[128,128]{1,0:T(8,128)(2,1)S(1)}, bf16[128,128]{1,0:T(8,128)(2,1)}, u32[]{:S(2)}) %copy-start.5) | copy-done | bytes 32792
  44.8 15.2 %shard_map.100 = bf16[32,32,1024]{2,1,0:T(8,128)(2,1)} custom-call(s32[64]{0:T(128)S(1)} %get-tuple-element.5.ticks, s32[64]{0:T(128)S(1)} %get-tuple-element.6.places, s32[1]{0:T(128)} %bitcast.1.here, bf16[4,32,4096]{2,1,0:T(8,128)(2,1)S(1)} %bitcast.6, f32[64,512]{1,0:T(8,128)S(1)} %convolution_bitcast_fusion.keep, bf16[2,512,512]{2,1,0:T(8,128)(2,1)S(1)} %copy-done.2, ...), custom_call_target="tpu_custom_call" | custom-call | flops 4026531840 | bytes 3145728 | tf_op jit(solution)/shard_map/pallas_call | solution.py:216
  (2 shorter events, 0.0 us)
Async XLA Ops:
  6.5 32.0 %all-gather.3.cloned.1.call-start = ((), (), s32[]{:S(2)}) async-start(), calls=%async_computation | async-start | bytes 1310720 | tf_op jit(solution)/shard_map/all_gather | solution.py:251
  38.6 1.2 %copy-start = (bf16[128,4096]{1,0:T(8,128)(2,1)S(1)}, bf16[128,4096]{1,0:T(8,128)(2,1)}, u32[]{:S(2)}) copy-start(bf16[128,4096]{1,0:T(8,128)(2,1)} %all-gather.3.cloned.1.call-done) | copy-start | bytes 3145732
  39.8 1.2 %copy-start.1 = (bf16[2,512,512]{2,1,0:T(8,128)(2,1)S(1)}, bf16[2,512,512]{2,1,0:T(8,128)(2,1)}, u32[]{:S(2)}) copy-start(bf16[2,512,512]{2,1,0:T(8,128)(2,1)} %constant.19.clone.inverse) | copy-start | bytes 3145732
  41.0 1.2 %copy-start.2 = (bf16[2,512,512]{2,1,0:T(8,128)(2,1)S(1)}, bf16[2,512,512]{2,1,0:T(8,128)(2,1)}, u32[]{:S(2)}) copy-start(bf16[2,512,512]{2,1,0:T(8,128)(2,1)} %constant.18.clone.forward) | copy-start | bytes 3145732
  42.2 1.0 %copy-start.3 = (bf16[2,128,1024]{2,1,0:T(8,128)(2,1)S(1)}, bf16[2,128,1024]{2,1,0:T(8,128)(2,1)}, u32[]{:S(2)}) copy-start(bf16[2,128,1024]{2,1,0:T(8,128)(2,1)} %constant.22.clone.shifts) | copy-start | bytes 1572868
  43.3 0.8 %copy-start.4 = (bf16[2,64,128]{2,1,0:T(8,128)(2,1)S(1)}, bf16[2,64,128]{2,1,0:T(8,128)(2,1)}, u32[]{:S(2)}) copy-start(bf16[2,64,128]{2,1,0:T(8,128)(2,1)} %constant.21.clone.back_rows) | copy-start | bytes 98308
  44.0 0.8 %copy-start.5 = (bf16[128,128]{1,0:T(8,128)(2,1)S(1)}, bf16[128,128]{1,0:T(8,128)(2,1)}, u32[]{:S(2)}) copy-start(bf16[128,128]{1,0:T(8,128)(2,1)} %constant.20.clone.over_shots) | copy-start | bytes 98308
Sparse Core Ops, SparseCore 0:
  9.2 29.3 all-gather.2

commit v2 on v1

--- a/solution.py
+++ b/solution.py
@@ -56,26 +56,12 @@
     return forward, inverse, over_shots, back_rows, np.stack([high, low]), order
 
 
-def gather_kernel(
-    ticks,
-    places,
-    here,
-    traces,
-    keep,
-    forward,
-    inverse,
-    over_shots,
-    back_rows,
-    shifts,
-    out,
-    tiles,
-    folds,
-    spectra,
-    turns,
-    back,
-    mixed,
-):
-    peers, recs, block_len = traces.shape
+def gather_kernel(peers, chunk, *refs):
+    ticks, places, here, *refs = refs
+    traces, refs = refs[:peers], refs[peers:]
+    keep, forward, inverse, over_shots, back_rows, shifts, *refs = refs
+    out, tiles, folds, spectra, turns, back, mixed = refs[chunk > 0 :]
+    recs, block_len = traces[-1].shape
     shots, half = keep.shape
     window = 2 * half
     quarter = half // 2
@@ -85,9 +71,10 @@
     per_block = block_len // LANES
     f32, bf16 = jnp.float32, jnp.bfloat16
 
-    for peer in range(peers):
+    for away, block in enumerate(traces):
+        base = partner(here[0], away, peers) * per_block
         for tile in range(per_block):
-            tiles[peer * per_block + tile] = traces[peer, :, tile * LANES : (tile + 1) * LANES]
+            tiles[base + tile] = block[:, tile * LANES : (tile + 1) * LANES]
     for tile in range(wide):
         tiles[peers * per_block + tile] = jnp.zeros((recs, LANES), bf16)
 
@@ -186,50 +173,53 @@
         out[slot : slot + group, :, half:] = (even - odd).reshape(group, recs, half).astype(bf16)
 
 
-def filter_gathers(ticks, places, here, traces, keep, tables):
+def partner(index, away, count):
+    if count & (count - 1) == 0:
+        return index ^ away
+    return (index + away) % count
+
+
+def filter_gathers(ticks, places, here, traces, keep, tables, chunk, chunks, filled):
     forward, inverse, over_shots, back_rows, shifts = tables
-    peers, rec_rows, block_len = traces.shape
+    peers = len(traces)
+    recs, block_len = traces[-1].shape
+    rec_rows = recs * chunks
     shots, half = keep.shape
     window = 2 * half
     slots = 2 * shots // peers
-    recs = RECS
     total = peers * block_len
     smem = pl.BlockSpec(memory_space=pltpu.SMEM)
+    shared = [keep, forward, inverse, over_shots, back_rows, shifts]
 
     def whole(array):
         return pl.BlockSpec(array.shape, lambda step: (0,) * array.ndim)
 
-    sizes = (
-        8 * peers * recs * block_len
-        + 4 * 2 * 2 * shots * recs * half
-        + 12 * shots * recs * half
-        + 8 * slots * recs * window
-        + 4 * slots * recs * window
-        + 8 * (forward.size + inverse.size + over_shots.size + back_rows.size + shifts.size)
-    )
-    flops = 2 * rec_rows * (
+    flops = 2 * recs * (
         shots * window * half
         + slots * window * half
         + 4 * shots * shots * half
         + 4 * slots * shots * half
     )
+    operands = [ticks, places, here, *traces, *shared]
+    in_specs = [
+        smem,
+        smem,
+        smem,
+        pl.BlockSpec((recs, block_len), lambda step: (chunk, 0)),
+        *[whole(block) for block in traces[1:]],
+        *[whole(array) for array in shared],
+    ]
+    aliases = {}
+    if chunk:
+        aliases = {len(operands): 0}
+        operands.append(filled)
+        in_specs.append(pl.BlockSpec(memory_space=pl.ANY))
     return pl.pallas_call(
-        gather_kernel,
-        grid=(rec_rows // recs,),
+        functools.partial(gather_kernel, peers, chunk),
+        grid=(1,),
         out_shape=jax.ShapeDtypeStruct((slots, rec_rows, window), jnp.bfloat16),
-        in_specs=[
-            smem,
-            smem,
-            smem,
-            pl.BlockSpec((peers, recs, block_len), lambda step: (0, step, 0)),
-            whole(keep),
-            whole(forward),
-            whole(inverse),
-            whole(over_shots),
-            whole(back_rows),
-            whole(shifts),
-        ],
-        out_specs=pl.BlockSpec((slots, recs, window), lambda step: (0, step, 0)),
+        in_specs=in_specs,
+        out_specs=pl.BlockSpec((slots, recs, window), lambda step: (0, chunk, 0)),
         scratch_shapes=[
             pltpu.VMEM(((total + window) // LANES, recs, LANES), jnp.bfloat16),
             pltpu.VMEM((2, shots * recs, half), jnp.bfloat16),
@@ -238,24 +228,43 @@
             pltpu.VMEM((2 * slots, 2 * shots), jnp.bfloat16),
             pltpu.VMEM((window // LANES, slots * recs, LANES), jnp.float32),
         ],
-        compiler_params=pltpu.CompilerParams(vmem_limit_bytes=min(sizes + (12 << 20), 60 << 20)),
+        input_output_aliases=aliases,
+        compiler_params=pltpu.CompilerParams(vmem_limit_bytes=60 << 20),
         cost_estimate=pl.CostEstimate(
-            flops=flops, bytes_accessed=2 * (traces.size + slots * rec_rows * window), transcendentals=0
+            flops=flops, bytes_accessed=2 * recs * (total + slots * window), transcendentals=0
         ),
-    )(ticks, places, here, traces, keep, forward, inverse, over_shots, back_rows, shifts)
+    )(*operands)
 
 
 def on_device(station_traces, shot_onset_ticks, span_place_index, spectral_keep_flags):
     shots, half = spectral_keep_flags.shape
     *tables, order = make_tables(2 * half, shots)
-    traces = lax.all_gather(station_traces, "tm", axis=0)
+    peers = lax.axis_size("tm")
+    chunks = station_traces.shape[0] // RECS
+    gathered = []
+    for chunk in range(chunks):
+        part = station_traces[chunk * RECS : (chunk + 1) * RECS]
+        gathered.append(
+            [station_traces]
+            + [
+                lax.ppermute(
+                    part, "tm", [(partner(index, away, peers), index) for index in range(peers)]
+                )
+                for away in range(1, peers)
+            ]
+        )
     ticks = lax.all_gather(shot_onset_ticks, "line", axis=0, tiled=True)
     places = lax.all_gather(span_place_index, "line", axis=0, tiled=True)
     here = lax.axis_index("tm").astype(jnp.int32).reshape(1)
     keep = jnp.dot(
         spectral_keep_flags.astype(jnp.bfloat16), order, preferred_element_type=jnp.float32
     )
-    return filter_gathers(ticks, places, here, traces, keep, tables)
+    filled = None
+    for chunk in range(chunks):
+        filled = filter_gathers(
+            ticks, places, here, gathered[chunk], keep, tables, chunk, chunks, filled
+        )
+    return filled
 
 
 def solution(mesh):

time: 67.3 us -> 46.2 us (0.69)
  waiting for transfers between devices: 16.5 us -> 0.02 us
  between operations: 14.1 us -> 0.72 us
  starting transfers between devices: 0.01 us -> 8.49 us
  Pallas kernels: 15.2 us -> 19.2 us
  local copies, waits for them, and re-layouts: 9.17 us -> 5.93 us
  blocking collectives: 10.6 us -> 9.7 us
    all_gather x1 -> x0, waiting for transfers between devices: 15.8 us -> none  [on_device(): traces = lax.all_gather(station_traces, 'tm', axis=0)]
    ppermute x0 -> x6, starting transfers between devices: none -> 8.49 us  [on_device(): lax.ppermute(part, 'tm', [(partner(index, away, peers), index) for index...]
    unnamed x17, local copies, waits for them, and re-layouts: 9.17 us -> 4.95 us
    pallas_call x1 -> x2, Pallas kernels: 15.2 us -> 19.2 us  [filter_gathers(): pl.pallas_call(functools.partial(gather_kernel, peers, chunk), grid=(1,),...]
    slice x0 -> x1, local copies, waits for them, and re-layouts: none -> 0.98 us  [on_device(): part = station_traces[chunk * RECS:(chunk + 1) * RECS]]
    unnamed x1, blocking collectives: 10.6 us -> 9.7 us
    unnamed x1 -> x0, waiting for transfers between devices: 0.71 us -> none
  transfers between devices with their start and end apart: 1 -> 6, of which waited for: 1 -> 0; matrix products, arithmetic and copies ran while one was open for 6% -> 11% of each run, Pallas kernels for 0% -> 21%
where the time goes in v2:
time: 46.2 us; the launch traced here: 46 us
  Pallas kernels  19.2 us (42%)
  blocking collectives  9.7 us (21%)
  starting transfers between devices  8.49 us (18%)
  local copies, waits for them, and re-layouts  5.93 us (13%)
  matrix products  1.96 us (4%)
  between operations  0.72 us (2%)
    pallas_call x2, Pallas kernels, filter_gathers(): pl.pallas_call(functools.partial(gather_kernel, peers, chunk), grid=(1,),...  19.2 us
    unnamed x1, blocking collectives  9.7 us
    ppermute x6, starting transfers between devices, on_device(): lax.ppermute(part, 'tm', [(partner(index, away, peers), index) for index...  8.49 us
    unnamed x17, local copies, waits for them, and re-layouts  4.95 us
    dot_general x1, matrix products, on_device(): jnp.dot(spectral_keep_flags.astype(jnp.bfloat16), order, preferred_elemen...  1.96 us
    slice x1, local copies, waits for them, and re-layouts, on_device(): part = station_traces[chunk * RECS:(chunk + 1) * RECS]  0.98 us
  transfers between devices with their start and end apart: 6, of which 0 were waited for; matrix products, arithmetic and copies ran while one was open for 11% of the time, Pallas kernels for 21%

profile of v2, /device:TPU:0, one launch (start us, length us, event | category | flops | bytes accessed | tf_op | source)
XLA Modules:
  0.0 46.0 jit_solution(13674500434839579176)
XLA Ops:
  0.0 1.0 %fusion.1 = (bf16[16,4096]{1,0:T(8,128)(2,1)S(1)}, bf16[16,4096]{1,0:T(8,128)(2,1)S(1)}) fusion(bf16[32,4096]{1,0:T(8,128)(2,1)} %refs_3_.3), kind=kLoop, calls=%fused_computation.2 | loop fusion | bytes 524288 | tf_op jit(solution)/shard_map/slice | solution.py:246
  1.0 4.0 %collective-permute-start.5 = (bf16[16,4096]{1,0:T(8,128)(2,1)S(1)}, bf16[16,4096]{1,0:T(8,128)(2,1)S(1)}, u32[]{:S(2)}, u32[]{:S(2)}) collective-permute-start(bf16[16,4096]{1,0:T(8,128)(2,1)S(1)} %get-tuple-element.7), channel_id=1, source_target_pairs={{24,0},{16,8},{8,16},{0,24},{25,1},{17,9},{9,17},{1,25},{26,2},{18... | collective-permute-start | bytes 393224 | tf_op jit(solution)/shard_map/ppermute | solution.py:250
  4.9 0.5 %collective-permute-start.4 = (bf16[16,4096]{1,0:T(8,128)(2,1)S(1)}, bf16[16,4096]{1,0:T(8,128)(2,1)S(1)}, u32[]{:S(2)}, u32[]{:S(2)}) collective-permute-start(bf16[16,4096]{1,0:T(8,128)(2,1)S(1)} %get-tuple-element.7), channel_id=1, source_target_pairs={{16,0},{24,8},{0,16},{8,24},{17,1},{25,9},{1,17},{9,25},{18,2},{26... | collective-permute-start | bytes 393224 | tf_op jit(solution)/shard_map/ppermute | solution.py:250
  5.5 0.1 collective-permute-start.3
  5.6 2.8 %collective-permute-start.2 = (bf16[16,4096]{1,0:T(8,128)(2,1)S(1)}, bf16[16,4096]{1,0:T(8,128)(2,1)S(1)}, u32[]{:S(2)}, u32[]{:S(2)}) collective-permute-start(bf16[16,4096]{1,0:T(8,128)(2,1)S(1)} %get-tuple-element.8), channel_id=1, source_target_pairs={{24,0},{16,8},{8,16},{0,24},{25,1},{17,9},{9,17},{1,25},{26,2},{18... | collective-permute-start | bytes 393224 | tf_op jit(solution)/shard_map/ppermute | solution.py:250
  8.4 0.5 %collective-permute-start.1 = (bf16[16,4096]{1,0:T(8,128)(2,1)S(1)}, bf16[16,4096]{1,0:T(8,128)(2,1)S(1)}, u32[]{:S(2)}, u32[]{:S(2)}) collective-permute-start(bf16[16,4096]{1,0:T(8,128)(2,1)S(1)} %get-tuple-element.8), channel_id=1, source_target_pairs={{16,0},{24,8},{0,16},{8,24},{17,1},{25,9},{1,17},{9,25},{18,2},{26... | collective-permute-start | bytes 393224 | tf_op jit(solution)/shard_map/ppermute | solution.py:250
  8.9 1.2 %dynamic-slice = u32[1]{0:T(128)} dynamic-slice(u32[32]{0:T(128)} %constant.25, u32[]{:T(128)S(6)} %add), dynamic_slice_sizes={1} | dynamic-slice | bytes 12
  10.8 0.9 %dynamic-update-slice = s32[64]{0:T(128)S(1)} dynamic-update-slice(s32[64]{0:T(128)S(1)} %broadcast.clone, s32[8]{0:T(128)} %param.11, u32[]{:T(128)} %bitcast) | dynamic-update-slice | bytes 68
  11.7 0.8 %dynamic-update-slice.1 = s32[64]{0:T(128)S(1)} dynamic-update-slice(s32[64]{0:T(128)S(1)} %broadcast.clone.1, s32[8]{0:T(128)} %param.12, u32[]{:T(128)} %bitcast) | dynamic-update-slice | bytes 68
  12.5 9.7 %all-reduce.2 = (s32[64]{0:T(128)}, s32[64]{0:T(128)}) all-reduce(s32[64]{0:T(128)S(1)} %dynamic-update-slice, s32[64]{0:T(128)S(1)} %dynamic-update-slice.1), channel_id=1, replica_groups=mesh['tm'=4,'line'=8] {'line'}, use_global_device_ids=true, to_apply=%add | all-reduce | flops 128 | bytes 1024
  22.2 2.0 %convolution_bitcast_fusion.refs_7_ = f32[64,512]{1,0:T(8,128)} fusion(bf16[512,512]{1,0:T(8,128)(2,1)} %constant.17.clone, s32[64,512]{1,0:T(8,128)} %param.13), kind=kOutput, calls=%fused_computation | convolution fusion | flops 33587200 | bytes 786432 | tf_op jit(solution)/shard_map/dot_general | solution.py:259
  24.2 0.0 collective-permute-done.5.refs_6_
  24.2 0.5 %collective-permute-start = (bf16[16,4096]{1,0:T(8,128)(2,1)S(1)}, bf16[16,4096]{1,0:T(8,128)(2,1)S(1)}, u32[]{:S(2)}, u32[]{:S(2)}) collective-permute-start(bf16[16,4096]{1,0:T(8,128)(2,1)S(1)} %get-tuple-element.8), channel_id=1, source_target_pairs={{8,0},{0,8},{24,16},{16,24},{9,1},{1,9},{25,17},{17,25},{10,2},{2,... | collective-permute-start | bytes 393224 | tf_op jit(solution)/shard_map/ppermute | solution.py:250
  24.8 0.1 copy-done.3
  24.8 0.6 %copy-done.4 = bf16[16,4096]{1,0:T(8,128)(2,1)} copy-done((bf16[16,4096]{1,0:T(8,128)(2,1)}, bf16[16,4096]{1,0:T(8,128)(2,1)S(1)}, u32[]{:S(2)}) %copy-start.4) | copy-done | bytes 131096
  25.4 0.1 copy-done.5
  25.5 9.6 %shard_map.100.refs_13_ = bf16[32,32,1024]{2,1,0:T(8,128)(2,1)} custom-call(s32[64]{0:T(128)} %get-tuple-element.5.refs_0_, s32[64]{0:T(128)} %get-tuple-element.6.refs_1_, s32[1]{0:T(128)} %bitcast.1.refs_2_, bf16[32,4096]{1,0:T(8,128)(2,1)} %refs_3_.3, bf16[16,4096]{1,0:T(8,128)(2,1)} %copy-done.5, bf16[16,4096]{1,0:T(8,128)(2,1)} %copy-done.4, ...), custom_call_target="tpu_custom_call" | custom-call | flops 2013265920 | bytes 1572864 | tf_op jit(solution)/shard_map/pallas_call | solution.py:217
  35.1 0.0 collective-permute-done.2.refs_6_
  35.1 0.0 collective-permute-done.1.refs_5_
  35.1 0.0 collective-permute-done.refs_4_
  35.1 0.6 %copy-done = bf16[16,4096]{1,0:T(8,128)(2,1)} copy-done((bf16[16,4096]{1,0:T(8,128)(2,1)}, bf16[16,4096]{1,0:T(8,128)(2,1)S(1)}, u32[]{:S(2)}) %copy-start) | copy-done | bytes 131096
  35.7 0.1 copy-done.1
  35.8 0.7 %copy-done.2 = bf16[16,4096]{1,0:T(8,128)(2,1)} copy-done((bf16[16,4096]{1,0:T(8,128)(2,1)}, bf16[16,4096]{1,0:T(8,128)(2,1)S(1)}, u32[]{:S(2)}) %copy-start.2) | copy-done | bytes 131096
  36.4 9.6 %shard_map.101 = bf16[32,32,1024]{2,1,0:T(8,128)(2,1)} custom-call(s32[64]{0:T(128)} %get-tuple-element.5.refs_0_, s32[64]{0:T(128)} %get-tuple-element.6.refs_1_, s32[1]{0:T(128)} %bitcast.1.refs_2_, bf16[32,4096]{1,0:T(8,128)(2,1)} %refs_3_.3, bf16[16,4096]{1,0:T(8,128)(2,1)} %copy-done.2, ...), custom_call_target="tpu_custom_call", output_to_operand_aliasing={{}: (13, {})} | custom-call | flops 2013265920 | bytes 1572864 | tf_op jit(solution)/shard_map/pallas_call | solution.py:217
  (10 shorter events, 0.0 us)
Async XLA Ops:
  1.0 23.2 %collective-permute-start.5 = (bf16[16,4096]{1,0:T(8,128)(2,1)S(1)}, bf16[16,4096]{1,0:T(8,128)(2,1)S(1)}, u32[]{:S(2)}, u32[]{:S(2)}) collective-permute-start(bf16[16,4096]{1,0:T(8,128)(2,1)S(1)} %get-tuple-element.7), channel_id=1, source_target_pairs={{24,0},{16,8},{8,16},{0,24},{25,1},{17,9},{9,17},{1,25},{26,2},{18... | collective-permute-start | bytes 393224 | tf_op jit(solution)/shard_map/ppermute | solution.py:250
  4.9 19.8 %collective-permute-start.4 = (bf16[16,4096]{1,0:T(8,128)(2,1)S(1)}, bf16[16,4096]{1,0:T(8,128)(2,1)S(1)}, u32[]{:S(2)}, u32[]{:S(2)}) collective-permute-start(bf16[16,4096]{1,0:T(8,128)(2,1)S(1)} %get-tuple-element.7), channel_id=1, source_target_pairs={{16,0},{24,8},{0,16},{8,24},{17,1},{25,9},{1,17},{9,25},{18,2},{26... | collective-permute-start | bytes 393224 | tf_op jit(solution)/shard_map/ppermute | solution.py:250
  5.5 19.3 %collective-permute-start.3 = (bf16[16,4096]{1,0:T(8,128)(2,1)S(1)}, bf16[16,4096]{1,0:T(8,128)(2,1)S(1)}, u32[]{:S(2)}, u32[]{:S(2)}) collective-permute-start(bf16[16,4096]{1,0:T(8,128)(2,1)S(1)} %get-tuple-element.7), channel_id=1, source_target_pairs={{8,0},{0,8},{24,16},{16,24},{9,1},{1,9},{25,17},{17,25},{10,2},{2,... | collective-permute-start | bytes 393224 | tf_op jit(solution)/shard_map/ppermute | solution.py:250
  5.6 29.5 %collective-permute-start.2 = (bf16[16,4096]{1,0:T(8,128)(2,1)S(1)}, bf16[16,4096]{1,0:T(8,128)(2,1)S(1)}, u32[]{:S(2)}, u32[]{:S(2)}) collective-permute-start(bf16[16,4096]{1,0:T(8,128)(2,1)S(1)} %get-tuple-element.8), channel_id=1, source_target_pairs={{24,0},{16,8},{8,16},{0,24},{25,1},{17,9},{9,17},{1,25},{26,2},{18... | collective-permute-start | bytes 393224 | tf_op jit(solution)/shard_map/ppermute | solution.py:250
  8.4 26.6 %collective-permute-start.1 = (bf16[16,4096]{1,0:T(8,128)(2,1)S(1)}, bf16[16,4096]{1,0:T(8,128)(2,1)S(1)}, u32[]{:S(2)}, u32[]{:S(2)}) collective-permute-start(bf16[16,4096]{1,0:T(8,128)(2,1)S(1)} %get-tuple-element.8), channel_id=1, source_target_pairs={{16,0},{24,8},{0,16},{8,24},{17,1},{25,9},{1,17},{9,25},{18,2},{26... | collective-permute-start | bytes 393224 | tf_op jit(solution)/shard_map/ppermute | solution.py:250
  24.2 0.6 %copy-start.3 = (bf16[16,4096]{1,0:T(8,128)(2,1)}, bf16[16,4096]{1,0:T(8,128)(2,1)S(1)}, u32[]{:S(2)}) copy-start(bf16[16,4096]{1,0:T(8,128)(2,1)S(1)} %collective-permute-done.5.refs_6_) | copy-start | bytes 393220
  24.2 10.9 %collective-permute-start = (bf16[16,4096]{1,0:T(8,128)(2,1)S(1)}, bf16[16,4096]{1,0:T(8,128)(2,1)S(1)}, u32[]{:S(2)}, u32[]{:S(2)}) collective-permute-start(bf16[16,4096]{1,0:T(8,128)(2,1)S(1)} %get-tuple-element.8), channel_id=1, source_target_pairs={{8,0},{0,8},{24,16},{16,24},{9,1},{1,9},{25,17},{17,25},{10,2},{2,... | collective-permute-start | bytes 393224 | tf_op jit(solution)/shard_map/ppermute | solution.py:250
  24.8 0.6 %copy-start.4 = (bf16[16,4096]{1,0:T(8,128)(2,1)}, bf16[16,4096]{1,0:T(8,128)(2,1)S(1)}, u32[]{:S(2)}) copy-start(bf16[16,4096]{1,0:T(8,128)(2,1)S(1)} %collective-permute-done.4.refs_5_) | copy-start | bytes 393220
  24.8 0.7 %copy-start.5 = (bf16[16,4096]{1,0:T(8,128)(2,1)}, bf16[16,4096]{1,0:T(8,128)(2,1)S(1)}, u32[]{:S(2)}) copy-start(bf16[16,4096]{1,0:T(8,128)(2,1)S(1)} %collective-permute-done.3.refs_4_) | copy-start | bytes 393220
  35.1 0.6 %copy-start = (bf16[16,4096]{1,0:T(8,128)(2,1)}, bf16[16,4096]{1,0:T(8,128)(2,1)S(1)}, u32[]{:S(2)}) copy-start(bf16[16,4096]{1,0:T(8,128)(2,1)S(1)} %collective-permute-done.2.refs_6_) | copy-start | bytes 393220
  35.1 0.7 %copy-start.1 = (bf16[16,4096]{1,0:T(8,128)(2,1)}, bf16[16,4096]{1,0:T(8,128)(2,1)S(1)}, u32[]{:S(2)}) copy-start(bf16[16,4096]{1,0:T(8,128)(2,1)S(1)} %collective-permute-done.1.refs_5_) | copy-start | bytes 393220
  35.8 0.7 %copy-start.2 = (bf16[16,4096]{1,0:T(8,128)(2,1)}, bf16[16,4096]{1,0:T(8,128)(2,1)S(1)}, u32[]{:S(2)}) copy-start(bf16[16,4096]{1,0:T(8,128)(2,1)S(1)} %collective-permute-done.refs_4_) | copy-start | bytes 393220

commit v3 on v2

v3 whole, which is shorter than its diff:
```python
import functools
import math

import jax
import jax.numpy as jnp
import ml_dtypes
import numpy as np
from jax import lax
from jax.experimental import pallas as pl
from jax.experimental.pallas import tpu as pltpu
from jax.sharding import PartitionSpec as P

LANES = 128
RECS = 16


def make_tables(window, shots):
    half = window // 2
    quarter = half // 2
    times = np.arange(half)
    freqs = np.concatenate([np.arange(0, half, 2), np.arange(1, half, 2)])

    def waves(rows, columns, period):
        phase = (rows[:, None] * columns[None, :] % period) * (2.0 * math.pi / period)
        return np.cos(phase), np.sin(phase)

    bf16 = ml_dtypes.bfloat16
    cosine, sine = waves(times, freqs, window)
    forward = np.stack(
        [
            np.concatenate([cosine[:, cut], -sine[:, cut]], axis=1)
            for cut in (slice(0, quarter), slice(quarter, half))
        ]
    ).astype(bf16)
    gain = np.where(freqs == 0, 0.5, 1.0)[:, None] * (2.0 / (window * shots))
    inverse = np.stack(
        [
            np.concatenate([gain[cut] * cosine.T[cut], -gain[cut] * sine.T[cut]], axis=0)
            for cut in (slice(0, quarter), slice(quarter, half))
        ]
    ).astype(bf16)
    turn_cos, turn_sin = waves(np.arange(shots), np.arange(shots), shots)
    over_shots = np.block([[turn_cos, turn_sin], [-turn_sin, turn_cos]]).astype(bf16)
    back_rows = np.stack(
        [
            np.concatenate([turn_cos, -turn_sin], axis=1),
            np.concatenate([turn_sin, turn_cos], axis=1),
        ]
    ).astype(bf16)
    shift_cos, shift_sin = waves(np.arange(LANES), freqs, window)
    shifts = np.concatenate([shift_cos, shift_sin], axis=1)
    high = shifts.astype(bf16)
    low = (shifts - high.astype(np.float64)).astype(bf16)
    order = np.zeros((half, half), bf16)
    order[freqs, np.arange(half)] = 1
    return forward, inverse, over_shots, back_rows, np.stack([high, low]), order


def plan_kernel(peers, *refs):
    codes, refs = refs[:peers], refs[peers:]
    here, flags, order, back_rows, shifts, ticks, keep, turns, back = refs
    shots, half = flags.shape
    slots = back.shape[0] // 2
    share = shots // peers
    block_len = here[2]
    f32, bf16 = jnp.float32, jnp.bfloat16

    keep[...] = jnp.dot(flags[...].astype(f32).astype(bf16), order[...], preferred_element_type=f32)
    shot_row = lax.broadcasted_iota(jnp.int32, (shots, LANES), 0)
    shot_lane = lax.broadcasted_iota(jnp.int32, (1, shots), 1)
    within_all = jnp.zeros((shots, LANES), jnp.int32)
    place_all = jnp.full((1, shots), -1, jnp.int32)
    for away, block in enumerate(codes):
        base = partner(here[1], away, peers) * share
        for item in range(share):
            shot = base + item
            tick = block[item]
            ticks[shot] = tick
            within_all = jnp.where(shot_row == shot, tick % LANES, within_all)
            place = jnp.where(tick // block_len == here[0], block[share + item], -1)
            place_all = jnp.where(shot_lane == shot, place, place_all)
    shift_lane = lax.broadcasted_iota(jnp.int32, (shots, LANES), 1)
    picks = (within_all == shift_lane).astype(f32).astype(bf16)
    turns[...] = jnp.dot(picks, shifts[0], preferred_element_type=f32) + jnp.dot(
        picks, shifts[1], preferred_element_type=f32
    )
    slot_row = lax.broadcasted_iota(jnp.int32, (slots, shots), 0)
    owned = (slot_row == place_all).astype(f32).astype(bf16)
    for part in range(2):
        back[part * slots : (part + 1) * slots] = jnp.dot(
            owned, back_rows[part], preferred_element_type=f32
        ).astype(bf16)


def plan_shots(codes, here, flags, order, back_rows, shifts, slots):
    shots, half = flags.shape
    smem = pl.BlockSpec(memory_space=pltpu.SMEM)
    vmem = pl.BlockSpec(memory_space=pltpu.VMEM)
    return pl.pallas_call(
        functools.partial(plan_kernel, len(codes)),
        out_shape=[
            jax.ShapeDtypeStruct((shots,), jnp.int32),
            jax.ShapeDtypeStruct((shots, half), jnp.float32),
            jax.ShapeDtypeStruct((shots, 2 * half), jnp.float32),
            jax.ShapeDtypeStruct((2 * slots, 2 * shots), jnp.bfloat16),
        ],
        in_specs=[smem] * (len(codes) + 1) + [vmem] * 4,
        out_specs=[smem, vmem, vmem, vmem],
        compiler_params=pltpu.CompilerParams(vmem_limit_bytes=16 << 20),
        cost_estimate=pl.CostEstimate(
            flops=2 * shots * half * (half + 4 * LANES), bytes_accessed=2 << 20, transcendentals=0
        ),
    )(*codes, here, flags, order, back_rows, shifts)


def gather_kernel(peers, chunk, *refs):
    ticks, here, *refs = refs
    traces, refs = refs[:peers], refs[peers:]
    tables, refs = refs[:6], refs[6 + (chunk > 0) :]
    out, records, *refs = refs
    loaded, refs = refs[:6], refs[6:]
    tiles, folds, spectra, mixed, ready, record_sem, table_sem, out_sem = refs
    recs, block_len = records.shape[1:]
    keep, turns, back, over_shots, forward, inverse = loaded
    shots, half = keep.shape
    window = 2 * half
    slots = ready.shape[0]
    wide = window // LANES
    mid = wide // 2
    arms = mid // 2
    per_block = block_len // LANES
    f32, bf16 = jnp.float32, jnp.bfloat16
    rows_here = pl.ds(chunk * recs, recs)

    record_copies = [
        pltpu.make_async_copy(
            block.at[rows_here] if away == 0 else block, records.at[away], record_sem.at[away]
        )
        for away, block in enumerate(traces)
    ]
    table_copies = [
        pltpu.make_async_copy(table, place, table_sem.at[index])
        for index, (table, place) in enumerate(zip(tables, loaded))
    ]
    for copy in record_copies:
        copy.start()
    for index in (4, 1, 0, 2, 3, 5):
        table_copies[index].start()

    for away in range(peers):
        record_copies[away].wait()
        base = partner(here[0], away, peers) * per_block
        for tile in range(per_block):
            tiles[base + tile] = records[away, :, tile * LANES : (tile + 1) * LANES]
    for tile in range(wide):
        tiles[peers * per_block + tile] = jnp.zeros((recs, LANES), bf16)

    lane = lax.broadcasted_iota(jnp.int32, (recs, LANES), 1)

    def cut(shot, carry):
        tick = ticks[shot]
        first = tick // LANES
        within = tick % LANES
        piece = [tiles[first + tile] for tile in range(wide)]
        last = tiles[first + wide]
        piece[0] = jnp.where(lane < within, last.astype(f32), piece[0].astype(f32)).astype(bf16)
        row = pl.multiple_of(shot * recs, recs)
        for tile in range(mid):
            at = slice(tile * LANES, (tile + 1) * LANES)
            folds[0, pl.ds(row, recs), at] = piece[tile] + piece[tile + mid]
            folds[1, pl.ds(row, recs), at] = piece[tile] - piece[tile + mid]
        return carry

    lax.fori_loop(0, shots, cut, 0, unroll=8)

    table_copies[4].wait()
    rows = shots * recs
    step = min(rows, 256)
    for part in range(2):
        for row in range(0, rows, step):
            found = jnp.dot(
                folds[part, row : row + step], forward[part], preferred_element_type=f32
            )
            for tile in range(mid):
                spectra[part * mid + tile, row : row + step] = found[
                    :, tile * LANES : (tile + 1) * LANES
                ]

    for index in range(4):
        table_copies[index].wait()
    batch = 4
    for first in range(0, recs, batch):
        real, imag = [], []
        for rec in range(first, first + batch):
            for tile in range(mid):
                part, arm = tile // arms, tile % arms
                at = slice(tile * LANES, (tile + 1) * LANES)
                cos_turn = turns[:, at]
                sin_turn = turns[:, half + tile * LANES : half + (tile + 1) * LANES]
                cos_part = spectra[part * mid + arm, pl.ds(rec, shots, stride=recs), :]
                sin_part = spectra[part * mid + arms + arm, pl.ds(rec, shots, stride=recs), :]
                real.append((cos_part * cos_turn - sin_part * sin_turn).astype(bf16))
                imag.append((cos_part * sin_turn + sin_part * cos_turn).astype(bf16))
        stacked = jnp.concatenate(
            [jnp.concatenate(real, axis=1), jnp.concatenate(imag, axis=1)], axis=0
        )
        waves = jnp.dot(over_shots[...], stacked, preferred_element_type=f32)
        kept = jnp.concatenate([keep[...]] * batch, axis=1)
        masked = jnp.concatenate([waves[:shots] * kept, waves[shots:] * kept], axis=0).astype(bf16)
        again = jnp.dot(back[...], masked, preferred_element_type=f32)
        for rec in range(batch):
            to = pl.ds(first + rec, slots, stride=recs)
            for tile in range(mid):
                part, arm = tile // arms, tile % arms
                at = slice(rec * half + tile * LANES, rec * half + (tile + 1) * LANES)
                mixed[part * mid + arm, to, :] = again[:slots, at]
                mixed[part * mid + arms + arm, to, :] = again[slots:, at]

    table_copies[5].wait()
    group = max(1, min(slots, 256 // recs))
    out_copies = []
    for slot in range(0, slots, group):
        at = slice(slot * recs, (slot + group) * recs)
        even, odd = [
            jnp.dot(
                jnp.concatenate(
                    [mixed[part * mid + tile, at].astype(bf16) for tile in range(mid)], axis=1
                ),
                inverse[part],
                preferred_element_type=f32,
            )
            for part in range(2)
        ]
        ready[slot : slot + group, :, :half] = (even + odd).reshape(group, recs, half).astype(bf16)
        ready[slot : slot + group, :, half:] = (even - odd).reshape(group, recs, half).astype(bf16)
        copy = pltpu.make_async_copy(
            ready.at[pl.ds(slot, group)],
            out.at[pl.ds(slot, group), rows_here],
            out_sem.at[slot // group],
        )
        copy.start()
        out_copies.append(copy)
    for copy in out_copies:
        copy.wait()


def partner(index, away, count):
    if count & (count - 1) == 0:
        return index ^ away
    return (index + away) % count


def filter_gathers(ticks, here, traces, tables, chunk, chunks, filled):
    keep, turns, back, over_shots, forward, inverse = tables
    peers = len(traces)
    recs, block_len = traces[-1].shape
    rec_rows = recs * chunks
    shots, half = keep.shape
    window = 2 * half
    slots = 2 * shots // peers
    total = peers * block_len
    smem = pl.BlockSpec(memory_space=pltpu.SMEM)
    anywhere = pl.BlockSpec(memory_space=pl.ANY)
    flops = 2 * recs * (
        shots * window * half
        + slots * window * half
        + 4 * shots * shots * half
        + 4 * slots * shots * half
    )
    operands = [ticks, here, *traces, *tables]
    aliases = {}
    if chunk:
        aliases = {len(operands): 0}
        operands.append(filled)
    scratch = [
        pltpu.VMEM((peers, recs, block_len), jnp.bfloat16),
        *[pltpu.VMEM(table.shape, table.dtype) for table in tables],
        pltpu.VMEM(((total + window) // LANES, recs, LANES), jnp.bfloat16),
        pltpu.VMEM((2, shots * recs, half), jnp.bfloat16),
        pltpu.VMEM((window // LANES, shots * recs, LANES), jnp.float32),
        pltpu.VMEM((window // LANES, slots * recs, LANES), jnp.float32),
        pltpu.VMEM((slots, recs, window), jnp.bfloat16),
    ]
    size = sum(math.prod(ref.shape) * jnp.dtype(ref.dtype).itemsize for ref in scratch)
    return pl.pallas_call(
        functools.partial(gather_kernel, peers, chunk),
        out_shape=jax.ShapeDtypeStruct((slots, rec_rows, window), jnp.bfloat16),
        in_specs=[smem, smem] + [anywhere] * (len(operands) - 2),
        out_specs=anywhere,
        scratch_shapes=[
            *scratch,
            pltpu.SemaphoreType.DMA((peers,)),
            pltpu.SemaphoreType.DMA((len(tables),)),
            pltpu.SemaphoreType.DMA((slots,)),
        ],
        input_output_aliases=aliases,
        compiler_params=pltpu.CompilerParams(vmem_limit_bytes=min(size + (8 << 20), 60 << 20)),
        cost_estimate=pl.CostEstimate(
            flops=flops, bytes_accessed=2 * recs * (total + slots * window), transcendentals=0
        ),
    )(*operands)


def on_device(station_traces, shot_onset_ticks, span_place_index, spectral_keep_flags):
    shots, half = spectral_keep_flags.shape
    forward, inverse, over_shots, back_rows, shifts, order = make_tables(2 * half, shots)
    peers = lax.axis_size("tm")
    lines = lax.axis_size("line")
    chunks = station_traces.shape[0] // RECS
    slots = 2 * shots // peers

    def fetch(block, axis, count):
        return [
            lax.ppermute(
                block, axis, [(partner(index, away, count), index) for index in range(count)]
            )
            for away in range(1, count)
        ]

    gathered = [
        [station_traces, *fetch(station_traces[chunk * RECS : (chunk + 1) * RECS], "tm", peers)]
        for chunk in range(chunks)
    ]
    codes = jnp.concatenate([shot_onset_ticks, span_place_index])
    codes = [codes, *fetch(codes, "line", lines)]
    block_len = station_traces.shape[1]
    here = jnp.stack([lax.axis_index("tm"), lax.axis_index("line"), block_len]).astype(jnp.int32)
    ticks, keep, turns, back = plan_shots(
        codes, here, spectral_keep_flags, order, back_rows, shifts, slots
    )
    tables = [keep, turns, back, over_shots, forward, inverse]
    filled = None
    for chunk in range(chunks):
        filled = filter_gathers(ticks, here, gathered[chunk], tables, chunk, chunks, filled)
    return filled


def solution(mesh):
    in_specs = (P("line", "tm"), P("line"), P("line"), P())
    out_specs = P("tm", "line", None)
    return jax.shard_map(
        on_device, mesh=mesh, in_specs=in_specs, out_specs=out_specs, check_vma=False
    )
```

time: 46.2 us -> 55.2 us (1.19)
  waiting for transfers between devices: 0.02 us -> 10 us
  blocking collectives: 9.7 us -> 0 us
  starting transfers between devices: 8.49 us -> 14 us
  local copies, waits for them, and re-layouts: 5.93 us -> 8.88 us
  matrix products: 1.96 us -> 0 us
  Pallas kernels: 19.2 us -> 20.9 us
  other arithmetic: 0 us -> 0.82 us
  between operations: 0.72 us -> 0.08 us
    ppermute x6 -> x13, waiting for transfers between devices: 0.02 us -> 10 us  [fetch(): lax.ppermute(block, axis, [(partner(index, away, count), index) for index...]
    unnamed x1 -> x0, blocking collectives: 9.7 us -> none
    ppermute x6 -> x13, starting transfers between devices: 8.49 us -> 14 us  [fetch(): lax.ppermute(block, axis, [(partner(index, away, count), index) for index...]
    unnamed x17 -> x16, local copies, waits for them, and re-layouts: 4.95 us -> 7.9 us
    dot_general x1 -> x0, matrix products: 1.96 us -> none  [on_device(): jnp.dot(spectral_keep_flags.astype(jnp.bfloat16), order, preferred_elemen...]
    pallas_call x2 -> x3, Pallas kernels: 19.2 us -> 20.9 us  [the longest x2 18.8 us: filter_gathers(): pl.pallas_call(functools.partial(gather_kernel, peers, chunk), out_shape=...]
    concatenate x0 -> x1, other arithmetic: none -> 0.75 us  [on_device(): codes = jnp.concatenate([shot_onset_ticks, span_place_index])]
  transfers between devices with their start and end apart: 6 -> 13, of which waited for: 0 -> 5; matrix products, arithmetic and copies ran while one was open for 11% -> 2% of each run, Pallas kernels for 21% -> 21%
where the time goes in v3:
time: 55.2 us; the launch traced here: 54.7 us
  Pallas kernels  20.9 us (38%)
  starting transfers between devices  14 us (25%)
  waiting for transfers between devices  10 us (18%)
  local copies, waits for them, and re-layouts  8.88 us (16%)
  other arithmetic  0.82 us (1%)
    pallas_call x2, Pallas kernels, filter_gathers(): pl.pallas_call(functools.partial(gather_kernel, peers, chunk), out_shape=...  18.8 us
    ppermute x13, starting transfers between devices, fetch(): lax.ppermute(block, axis, [(partner(index, away, count), index) for index...  14 us
    ppermute x13, waiting for transfers between devices, fetch(): lax.ppermute(block, axis, [(partner(index, away, count), index) for index...  10 us
    unnamed x16, local copies, waits for them, and re-layouts  7.9 us
    pallas_call x1, Pallas kernels, plan_shots(): pl.pallas_call(functools.partial(plan_kernel, len(codes)), out_shape=[jax...  2.01 us
  transfers between devices with their start and end apart: 13, of which 5 were waited for; matrix products, arithmetic and copies ran while one was open for 2% of the time, Pallas kernels for 21%

profile of v3, /device:TPU:0, one launch (start us, length us, event | category | flops | bytes accessed | tf_op | source)
XLA Modules:
  0.0 54.7 jit_solution(14709562304021395807)
XLA Ops:
  0.0 1.0 %fusion = (bf16[16,4096]{1,0:T(8,128)(2,1)S(1)}, bf16[16,4096]{1,0:T(8,128)(2,1)S(1)}) fusion(bf16[32,4096]{1,0:T(8,128)(2,1)} %refs_2_.3), kind=kLoop, calls=%fused_computation.2 | loop fusion | bytes 524288 | tf_op jit(solution)/shard_map/slice | solution.py:321
  1.0 4.0 %collective-permute-start.12 = (bf16[16,4096]{1,0:T(8,128)(2,1)S(1)}, bf16[16,4096]{1,0:T(8,128)(2,1)S(1)}, u32[]{:S(2)}, u32[]{:S(2)}) collective-permute-start(bf16[16,4096]{1,0:T(8,128)(2,1)S(1)} %get-tuple-element.13), channel_id=1, source_target_pairs={{24,0},{16,8},{8,16},{0,24},{25,1},{17,9},{9,17},{1,25},{26,2},{18... | collective-permute-start | bytes 393224 | tf_op jit(solution)/shard_map/ppermute | solution.py:314
  5.6 0.7 %pad_add_fusion.refs_0_ = s32[16]{0:T(128)S(1)} fusion(s32[8]{0:T(128)} %param.12, s32[8]{0:T(128)} %param.11), kind=kLoop, calls=%fused_computation | loop fusion | flops 16 | bytes 128 | tf_op jit(solution)/shard_map/concatenate | solution.py:324
  6.3 2.6 %collective-permute-start.6 = (s32[16]{0:T(128)S(1)}, s32[16]{0:T(128)S(1)}, u32[]{:S(2)}, u32[]{:S(2)}) collective-permute-start(s32[16]{0:T(128)S(1)} %pad_add_fusion.refs_0_), channel_id=1, source_target_pairs={{7,0},{6,1},{5,2},{4,3},{3,4},{2,5},{1,6},{0,7},{15,8},{14,9},{13,... | collective-permute-start | bytes 200 | tf_op jit(solution)/shard_map/ppermute | solution.py:314
  8.9 1.5 %collective-permute-start.5 = (s32[16]{0:T(128)S(1)}, s32[16]{0:T(128)S(1)}, u32[]{:S(2)}, u32[]{:S(2)}) collective-permute-start(s32[16]{0:T(128)S(1)} %pad_add_fusion.refs_0_), channel_id=1, source_target_pairs={{6,0},{7,1},{4,2},{5,3},{2,4},{3,5},{0,6},{1,7},{14,8},{15,9},{12,... | collective-permute-start | bytes 200 | tf_op jit(solution)/shard_map/ppermute | solution.py:314
  10.5 0.6 %collective-permute-done.6.refs_7_ = s32[16]{0:T(128)S(1)} collective-permute-done((s32[16]{0:T(128)S(1)}, s32[16]{0:T(128)S(1)}, u32[]{:S(2)}, u32[]{:S(2)}) %collective-permute-start.6) | collective-permute-done | bytes 96 | tf_op jit(solution)/shard_map/ppermute | solution.py:314
  11.2 3.1 %collective-permute-done.5.refs_6_ = s32[16]{0:T(128)S(1)} collective-permute-done((s32[16]{0:T(128)S(1)}, s32[16]{0:T(128)S(1)}, u32[]{:S(2)}, u32[]{:S(2)}) %collective-permute-start.5) | collective-permute-done | bytes 96 | tf_op jit(solution)/shard_map/ppermute | solution.py:314
  14.3 0.7 %collective-permute-done.4.refs_5_ = s32[16]{0:T(128)S(1)} collective-permute-done((s32[16]{0:T(128)S(1)}, s32[16]{0:T(128)S(1)}, u32[]{:S(2)}, u32[]{:S(2)}) %collective-permute-start.4) | collective-permute-done | bytes 96 | tf_op jit(solution)/shard_map/ppermute | solution.py:314
  15.0 1.6 %collective-permute-start.2 = (s32[16]{0:T(128)S(1)}, s32[16]{0:T(128)S(1)}, u32[]{:S(2)}, u32[]{:S(2)}) collective-permute-start(s32[16]{0:T(128)S(1)} %pad_add_fusion.refs_0_), channel_id=1, source_target_pairs={{3,0},{2,1},{1,2},{0,3},{7,4},{6,5},{5,6},{4,7},{11,8},{10,9},{9,1... | collective-permute-start | bytes 200 | tf_op jit(solution)/shard_map/ppermute | solution.py:314
  16.6 2.1 %collective-permute-done.3.refs_4_ = s32[16]{0:T(128)S(1)} collective-permute-done((s32[16]{0:T(128)S(1)}, s32[16]{0:T(128)S(1)}, u32[]{:S(2)}, u32[]{:S(2)}) %collective-permute-start.3) | collective-permute-done | bytes 96 | tf_op jit(solution)/shard_map/ppermute | solution.py:314
  18.8 3.5 %collective-permute-done.1.refs_2_ = s32[16]{0:T(128)S(1)} collective-permute-done((s32[16]{0:T(128)S(1)}, s32[16]{0:T(128)S(1)}, u32[]{:S(2)}, u32[]{:S(2)}) %collective-permute-start.1) | collective-permute-done | bytes 96 | tf_op jit(solution)/shard_map/ppermute | solution.py:314
  22.3 2.4 %collective-permute-start.9 = (bf16[16,4096]{1,0:T(8,128)(2,1)S(1)}, bf16[16,4096]{1,0:T(8,128)(2,1)S(1)}, u32[]{:S(2)}, u32[]{:S(2)}) collective-permute-start(bf16[16,4096]{1,0:T(8,128)(2,1)S(1)} %get-tuple-element.14), channel_id=1, source_target_pairs={{24,0},{16,8},{8,16},{0,24},{25,1},{17,9},{9,17},{1,25},{26,2},{18... | collective-permute-start | bytes 393224 | tf_op jit(solution)/shard_map/ppermute | solution.py:314
  25.2 1.0 %copy-done = bf16[2,128,1024]{2,1,0:T(8,128)(2,1)S(1)} copy-done((bf16[2,128,1024]{2,1,0:T(8,128)(2,1)S(1)}, bf16[2,128,1024]{2,1,0:T(8,128)(2,1)}, u32[]{:S(2)}) %copy-start) | copy-done | bytes 524312
  26.3 1.0 %copy-done.1 = bf16[512,512]{1,0:T(8,128)(2,1)S(1)} copy-done((bf16[512,512]{1,0:T(8,128)(2,1)S(1)}, bf16[512,512]{1,0:T(8,128)(2,1)}, u32[]{:S(2)}) %copy-start.1) | copy-done | bytes 524312
  27.3 0.9 %copy-done.3 = s32[64,512]{1,0:T(8,128)S(1)} copy-done((s32[64,512]{1,0:T(8,128)S(1)}, s32[64,512]{1,0:T(8,128)}, u32[]{:S(2)}) %copy-start.3) | copy-done | bytes 131096
  28.2 0.8 %copy-done.4 = bf16[2,64,128]{2,1,0:T(8,128)(2,1)S(1)} copy-done((bf16[2,64,128]{2,1,0:T(8,128)(2,1)S(1)}, bf16[2,64,128]{2,1,0:T(8,128)(2,1)}, u32[]{:S(2)}) %copy-start.4) | copy-done | bytes 32792
  29.0 2.0 %shard_map.100 = (s32[64]{0:T(128)S(1)}, f32[64,512]{1,0:T(8,128)S(1)}, f32[64,1024]{1,0:T(8,128)S(1)}, bf16[64,128]{1,0:T(8,128)(2,1)S(1)}) custom-call(s32[16]{0:T(128)S(1)} %pad_add_fusion.refs_0_, s32[16]{0:T(128)S(1)} %collective-permute-done.refs_1_, s32[16]{0:T(128)S(1)} %collective-permute-done.1.refs_2_, s32[16]{0:T(128)S(1)} %collective-permute-done.2.refs_3_, ...), custom_call_target="tpu_custom_call" | custom-call | flops 67108864 | bytes 2097152 | tf_op jit(solution)/shard_map/pallas_call | solution.py:99
  31.0 0.6 %collective-permute-start.7 = (bf16[16,4096]{1,0:T(8,128)(2,1)S(1)}, bf16[16,4096]{1,0:T(8,128)(2,1)S(1)}, u32[]{:S(2)}, u32[]{:S(2)}) collective-permute-start(bf16[16,4096]{1,0:T(8,128)(2,1)S(1)} %get-tuple-element.14), channel_id=1, source_target_pairs={{8,0},{0,8},{24,16},{16,24},{9,1},{1,9},{25,17},{17,25},{10,2},{2,... | collective-permute-start | bytes 393224 | tf_op jit(solution)/shard_map/ppermute | solution.py:314
  31.6 0.9 %copy-done.2 = bf16[32,4096]{1,0:T(8,128)(2,1)S(1)} copy-done((bf16[32,4096]{1,0:T(8,128)(2,1)S(1)}, bf16[32,4096]{1,0:T(8,128)(2,1)}, u32[]{:S(2)}) %copy-start.2) | copy-done | bytes 262168
  32.6 1.2 %copy-done.5 = bf16[2,512,512]{2,1,0:T(8,128)(2,1)S(1)} copy-done((bf16[2,512,512]{2,1,0:T(8,128)(2,1)S(1)}, bf16[2,512,512]{2,1,0:T(8,128)(2,1)}, u32[]{:S(2)}) %copy-start.5) | copy-done | bytes 1048600
  33.8 1.2 %copy-done.6 = bf16[2,512,512]{2,1,0:T(8,128)(2,1)S(1)} copy-done((bf16[2,512,512]{2,1,0:T(8,128)(2,1)S(1)}, bf16[2,512,512]{2,1,0:T(8,128)(2,1)}, u32[]{:S(2)}) %copy-start.6) | copy-done | bytes 1048600
  35.0 0.8 %copy-done.7 = bf16[128,128]{1,0:T(8,128)(2,1)S(1)} copy-done((bf16[128,128]{1,0:T(8,128)(2,1)S(1)}, bf16[128,128]{1,0:T(8,128)(2,1)}, u32[]{:S(2)}) %copy-start.7) | copy-done | bytes 32792
  35.8 9.4 %shard_map.101.refs_12_ = bf16[32,32,1024]{2,1,0:T(8,128)(2,1)} custom-call(s32[64]{0:T(128)S(1)} %get-tuple-element.9.refs_0_, s32[3]{0:T(128)S(1)} %pad_add_fusion.1.refs_8_.refs_1_, bf16[32,4096]{1,0:T(8,128)(2,1)S(1)} %copy-done.2, bf16[16,4096]{1,0:T(8,128)(2,1)S(1)} %collective-permute-done.10.refs_3_, ...), custom_call_target="tpu_custom_call" | custom-call | flops 2013265920 | bytes 1572864 | tf_op jit(solution)/shard_map/pallas_call | solution.py:285
  45.2 9.4 %shard_map.102 = bf16[32,32,1024]{2,1,0:T(8,128)(2,1)} custom-call(s32[64]{0:T(128)S(1)} %get-tuple-element.9.refs_0_, s32[3]{0:T(128)S(1)} %pad_add_fusion.1.refs_8_.refs_1_, bf16[32,4096]{1,0:T(8,128)(2,1)S(1)} %copy-done.2, bf16[16,4096]{1,0:T(8,128)(2,1)S(1)} %collective-permute-done.7.refs_3_, ...), custom_call_target="tpu_custom_call", output_to_operand_aliasing={{}: (12, {})} | custom-call | flops 2013265920 | bytes 1572864 | tf_op jit(solution)/shard_map/pallas_call | solution.py:285
  (24 shorter events, 1.4 us)
Async XLA Ops:
  1.0 30.0 %collective-permute-start.12 = (bf16[16,4096]{1,0:T(8,128)(2,1)S(1)}, bf16[16,4096]{1,0:T(8,128)(2,1)S(1)}, u32[]{:S(2)}, u32[]{:S(2)}) collective-permute-start(bf16[16,4096]{1,0:T(8,128)(2,1)S(1)} %get-tuple-element.13), channel_id=1, source_target_pairs={{24,0},{16,8},{8,16},{0,24},{25,1},{17,9},{9,17},{1,25},{26,2},{18... | collective-permute-start | bytes 393224 | tf_op jit(solution)/shard_map/ppermute | solution.py:314
  4.9 26.7 %collective-permute-start.11 = (bf16[16,4096]{1,0:T(8,128)(2,1)S(1)}, bf16[16,4096]{1,0:T(8,128)(2,1)S(1)}, u32[]{:S(2)}, u32[]{:S(2)}) collective-permute-start(bf16[16,4096]{1,0:T(8,128)(2,1)S(1)} %get-tuple-element.13), channel_id=1, source_target_pairs={{16,0},{24,8},{0,16},{8,24},{17,1},{25,9},{1,17},{9,25},{18,2},{26... | collective-permute-start | bytes 393224 | tf_op jit(solution)/shard_map/ppermute | solution.py:314
  5.5 26.2 %collective-permute-start.10 = (bf16[16,4096]{1,0:T(8,128)(2,1)S(1)}, bf16[16,4096]{1,0:T(8,128)(2,1)S(1)}, u32[]{:S(2)}, u32[]{:S(2)}) collective-permute-start(bf16[16,4096]{1,0:T(8,128)(2,1)S(1)} %get-tuple-element.13), channel_id=1, source_target_pairs={{8,0},{0,8},{24,16},{16,24},{9,1},{1,9},{25,17},{17,25},{10,2},{2,... | collective-permute-start | bytes 393224 | tf_op jit(solution)/shard_map/ppermute | solution.py:314
  6.3 4.8 %collective-permute-start.6 = (s32[16]{0:T(128)S(1)}, s32[16]{0:T(128)S(1)}, u32[]{:S(2)}, u32[]{:S(2)}) collective-permute-start(s32[16]{0:T(128)S(1)} %pad_add_fusion.refs_0_), channel_id=1, source_target_pairs={{7,0},{6,1},{5,2},{4,3},{3,4},{2,5},{1,6},{0,7},{15,8},{14,9},{13,... | collective-permute-start | bytes 200 | tf_op jit(solution)/shard_map/ppermute | solution.py:314
  8.9 5.3 %collective-permute-start.5 = (s32[16]{0:T(128)S(1)}, s32[16]{0:T(128)S(1)}, u32[]{:S(2)}, u32[]{:S(2)}) collective-permute-start(s32[16]{0:T(128)S(1)} %pad_add_fusion.refs_0_), channel_id=1, source_target_pairs={{6,0},{7,1},{4,2},{5,3},{2,4},{3,5},{0,6},{1,7},{14,8},{15,9},{12,... | collective-permute-start | bytes 200 | tf_op jit(solution)/shard_map/ppermute | solution.py:314
  11.1 3.9 %collective-permute-start.4 = (s32[16]{0:T(128)S(1)}, s32[16]{0:T(128)S(1)}, u32[]{:S(2)}, u32[]{:S(2)}) collective-permute-start(s32[16]{0:T(128)S(1)} %pad_add_fusion.refs_0_), channel_id=1, source_target_pairs={{5,0},{4,1},{7,2},{6,3},{1,4},{0,5},{3,6},{2,7},{13,8},{12,9},{15,... | collective-permute-start | bytes 200 | tf_op jit(solution)/shard_map/ppermute | solution.py:314
  14.3 4.5 %collective-permute-start.3 = (s32[16]{0:T(128)S(1)}, s32[16]{0:T(128)S(1)}, u32[]{:S(2)}, u32[]{:S(2)}) collective-permute-start(s32[16]{0:T(128)S(1)} %pad_add_fusion.refs_0_), channel_id=1, source_target_pairs={{4,0},{5,1},{6,2},{7,3},{0,4},{1,5},{2,6},{3,7},{12,8},{13,9},{14,... | collective-permute-start | bytes 200 | tf_op jit(solution)/shard_map/ppermute | solution.py:314
  15.0 3.8 %collective-permute-start.2 = (s32[16]{0:T(128)S(1)}, s32[16]{0:T(128)S(1)}, u32[]{:S(2)}, u32[]{:S(2)}) collective-permute-start(s32[16]{0:T(128)S(1)} %pad_add_fusion.refs_0_), channel_id=1, source_target_pairs={{3,0},{2,1},{1,2},{0,3},{7,4},{6,5},{5,6},{4,7},{11,8},{10,9},{9,1... | collective-permute-start | bytes 200 | tf_op jit(solution)/shard_map/ppermute | solution.py:314
  18.7 3.5 %collective-permute-start.1 = (s32[16]{0:T(128)S(1)}, s32[16]{0:T(128)S(1)}, u32[]{:S(2)}, u32[]{:S(2)}) collective-permute-start(s32[16]{0:T(128)S(1)} %pad_add_fusion.refs_0_), channel_id=1, source_target_pairs={{2,0},{3,1},{0,2},{1,3},{6,4},{7,5},{4,6},{5,7},{10,8},{11,9},{8,1... | collective-permute-start | bytes 200 | tf_op jit(solution)/shard_map/ppermute | solution.py:314
  18.7 6.0 %collective-permute-start = (s32[16]{0:T(128)S(1)}, s32[16]{0:T(128)S(1)}, u32[]{:S(2)}, u32[]{:S(2)}) collective-permute-start(s32[16]{0:T(128)S(1)} %pad_add_fusion.refs_0_), channel_id=1, source_target_pairs={{1,0},{0,1},{3,2},{2,3},{5,4},{4,5},{7,6},{6,7},{9,8},{8,9},{11,10... | collective-permute-start | bytes 200 | tf_op jit(solution)/shard_map/ppermute | solution.py:314
  22.3 22.9 %collective-permute-start.9 = (bf16[16,4096]{1,0:T(8,128)(2,1)S(1)}, bf16[16,4096]{1,0:T(8,128)(2,1)S(1)}, u32[]{:S(2)}, u32[]{:S(2)}) collective-permute-start(bf16[16,4096]{1,0:T(8,128)(2,1)S(1)} %get-tuple-element.14), channel_id=1, source_target_pairs={{24,0},{16,8},{8,16},{0,24},{25,1},{17,9},{9,17},{1,25},{26,2},{18... | collective-permute-start | bytes 393224 | tf_op jit(solution)/shard_map/ppermute | solution.py:314
  24.7 20.5 %collective-permute-start.8 = (bf16[16,4096]{1,0:T(8,128)(2,1)S(1)}, bf16[16,4096]{1,0:T(8,128)(2,1)S(1)}, u32[]{:S(2)}, u32[]{:S(2)}) collective-permute-start(bf16[16,4096]{1,0:T(8,128)(2,1)S(1)} %get-tuple-element.14), channel_id=1, source_target_pairs={{16,0},{24,8},{0,16},{8,24},{17,1},{25,9},{1,17},{9,25},{18,2},{26... | collective-permute-start | bytes 393224 | tf_op jit(solution)/shard_map/ppermute | solution.py:314
  25.2 1.0 %copy-start = (bf16[2,128,1024]{2,1,0:T(8,128)(2,1)S(1)}, bf16[2,128,1024]{2,1,0:T(8,128)(2,1)}, u32[]{:S(2)}) copy-start(bf16[2,128,1024]{2,1,0:T(8,128)(2,1)} %constant.24.clone.refs_12_) | copy-start | bytes 1572868
  26.3 1.0 %copy-start.1 = (bf16[512,512]{1,0:T(8,128)(2,1)S(1)}, bf16[512,512]{1,0:T(8,128)(2,1)}, u32[]{:S(2)}) copy-start(bf16[512,512]{1,0:T(8,128)(2,1)} %constant.22.clone.refs_10_) | copy-start | bytes 1572868
  27.3 0.9 %copy-start.3 = (s32[64,512]{1,0:T(8,128)S(1)}, s32[64,512]{1,0:T(8,128)}, u32[]{:S(2)}) copy-start(s32[64,512]{1,0:T(8,128)} %refs_9_.3) | copy-start | bytes 393220
  28.2 0.8 %copy-start.4 = (bf16[2,64,128]{2,1,0:T(8,128)(2,1)S(1)}, bf16[2,64,128]{2,1,0:T(8,128)(2,1)}, u32[]{:S(2)}) copy-start(bf16[2,64,128]{2,1,0:T(8,128)(2,1)} %constant.23.clone.refs_11_) | copy-start | bytes 98308
  31.0 14.2 %collective-permute-start.7 = (bf16[16,4096]{1,0:T(8,128)(2,1)S(1)}, bf16[16,4096]{1,0:T(8,128)(2,1)S(1)}, u32[]{:S(2)}, u32[]{:S(2)}) collective-permute-start(bf16[16,4096]{1,0:T(8,128)(2,1)S(1)} %get-tuple-element.14), channel_id=1, source_target_pairs={{8,0},{0,8},{24,16},{16,24},{9,1},{1,9},{25,17},{17,25},{10,2},{2,... | collective-permute-start | bytes 393224 | tf_op jit(solution)/shard_map/ppermute | solution.py:314
  31.6 1.0 %copy-start.2 = (bf16[32,4096]{1,0:T(8,128)(2,1)S(1)}, bf16[32,4096]{1,0:T(8,128)(2,1)}, u32[]{:S(2)}) copy-start(bf16[32,4096]{1,0:T(8,128)(2,1)} %refs_2_.3) | copy-start | bytes 786436
  32.6 1.2 %copy-start.5 = (bf16[2,512,512]{2,1,0:T(8,128)(2,1)S(1)}, bf16[2,512,512]{2,1,0:T(8,128)(2,1)}, u32[]{:S(2)}) copy-start(bf16[2,512,512]{2,1,0:T(8,128)(2,1)} %constant.27.clone.refs_11_) | copy-start | bytes 3145732
  33.8 1.2 %copy-start.6 = (bf16[2,512,512]{2,1,0:T(8,128)(2,1)S(1)}, bf16[2,512,512]{2,1,0:T(8,128)(2,1)}, u32[]{:S(2)}) copy-start(bf16[2,512,512]{2,1,0:T(8,128)(2,1)} %constant.26.clone.refs_10_) | copy-start | bytes 3145732
  35.0 0.8 %copy-start.7 = (bf16[128,128]{1,0:T(8,128)(2,1)S(1)}, bf16[128,128]{1,0:T(8,128)(2,1)}, u32[]{:S(2)}) copy-start(bf16[128,128]{1,0:T(8,128)(2,1)} %constant.25.clone.refs_9_) | copy-start | bytes 98308

commit v4 on v3

--- a/solution.py
+++ b/solution.py
@@ -56,13 +56,11 @@
     return forward, inverse, over_shots, back_rows, np.stack([high, low]), order
 
 
-def plan_kernel(peers, *refs):
-    codes, refs = refs[:peers], refs[peers:]
-    here, flags, order, back_rows, shifts, ticks, keep, turns, back = refs
+def plan_kernel(codes, here, flags, order, back_rows, shifts, ticks, keep, turns, back):
     shots, half = flags.shape
     slots = back.shape[0] // 2
-    share = shots // peers
-    block_len = here[2]
+    lines, share = codes.shape[0], codes.shape[1] // 2
+    start = here[0] * here[1]
     f32, bf16 = jnp.float32, jnp.bfloat16
 
     keep[...] = jnp.dot(flags[...].astype(f32).astype(bf16), order[...], preferred_element_type=f32)
@@ -70,15 +68,14 @@
     shot_lane = lax.broadcasted_iota(jnp.int32, (1, shots), 1)
     within_all = jnp.zeros((shots, LANES), jnp.int32)
     place_all = jnp.full((1, shots), -1, jnp.int32)
-    for away, block in enumerate(codes):
-        base = partner(here[1], away, peers) * share
-        for item in range(share):
-            shot = base + item
-            tick = block[item]
-            ticks[shot] = tick
-            within_all = jnp.where(shot_row == shot, tick % LANES, within_all)
-            place = jnp.where(tick // block_len == here[0], block[share + item], -1)
-            place_all = jnp.where(shot_lane == shot, place, place_all)
+    for shot in range(shots):
+        line, item = divmod(shot, share)
+        tick = codes[line, item]
+        ticks[shot] = tick
+        within_all = jnp.where(shot_row == shot, tick & (LANES - 1), within_all)
+        mine = (tick >= start) & (tick < start + here[1])
+        place = jnp.where(mine, codes[line, share + item], -1)
+        place_all = jnp.where(shot_lane == shot, place, place_all)
     shift_lane = lax.broadcasted_iota(jnp.int32, (shots, LANES), 1)
     picks = (within_all == shift_lane).astype(f32).astype(bf16)
     turns[...] = jnp.dot(picks, shifts[0], preferred_element_type=f32) + jnp.dot(
@@ -97,20 +94,20 @@
     smem = pl.BlockSpec(memory_space=pltpu.SMEM)
     vmem = pl.BlockSpec(memory_space=pltpu.VMEM)
     return pl.pallas_call(
-        functools.partial(plan_kernel, len(codes)),
+        plan_kernel,
         out_shape=[
             jax.ShapeDtypeStruct((shots,), jnp.int32),
             jax.ShapeDtypeStruct((shots, half), jnp.float32),
             jax.ShapeDtypeStruct((shots, 2 * half), jnp.float32),
             jax.ShapeDtypeStruct((2 * slots, 2 * shots), jnp.bfloat16),
         ],
-        in_specs=[smem] * (len(codes) + 1) + [vmem] * 4,
+        in_specs=[smem, smem] + [vmem] * 4,
         out_specs=[smem, vmem, vmem, vmem],
-        compiler_params=pltpu.CompilerParams(vmem_limit_bytes=16 << 20),
+        compiler_params=pltpu.CompilerParams(vmem_limit_bytes=60 << 20),
         cost_estimate=pl.CostEstimate(
             flops=2 * shots * half * (half + 4 * LANES), bytes_accessed=2 << 20, transcendentals=0
         ),
-    )(*codes, here, flags, order, back_rows, shifts)
+    )(codes, here, flags, order, back_rows, shifts)
 
 
 def gather_kernel(peers, chunk, *refs):
@@ -157,27 +154,26 @@
 
     lane = lax.broadcasted_iota(jnp.int32, (recs, LANES), 1)
 
-    def cut(shot, carry):
+    def cut(shot):
         tick = ticks[shot]
-        first = tick // LANES
-        within = tick % LANES
+        first = lax.shift_right_logical(tick, LANES.bit_length() - 1)
+        within = tick & (LANES - 1)
         piece = [tiles[first + tile] for tile in range(wide)]
         last = tiles[first + wide]
         piece[0] = jnp.where(lane < within, last.astype(f32), piece[0].astype(f32)).astype(bf16)
-        row = pl.multiple_of(shot * recs, recs)
+        rows = slice(shot * recs, (shot + 1) * recs)
         for tile in range(mid):
             at = slice(tile * LANES, (tile + 1) * LANES)
-            folds[0, pl.ds(row, recs), at] = piece[tile] + piece[tile + mid]
-            folds[1, pl.ds(row, recs), at] = piece[tile] - piece[tile + mid]
-        return carry
-
-    lax.fori_loop(0, shots, cut, 0, unroll=8)
+            folds[0, rows, at] = piece[tile] + piece[tile + mid]
+            folds[1, rows, at] = piece[tile] - piece[tile + mid]
 
     table_copies[4].wait()
     rows = shots * recs
-    step = min(rows, 256)
-    for part in range(2):
-        for row in range(0, rows, step):
+    step = min(rows, 512)
+    for row in range(0, rows, step):
+        for shot in range(row // recs, (row + step) // recs):
+            cut(shot)
+        for part in range(2):
             found = jnp.dot(
                 folds[part, row : row + step], forward[part], preferred_element_type=f32
             )
@@ -281,7 +277,6 @@
         pltpu.VMEM((window // LANES, slots * recs, LANES), jnp.float32),
         pltpu.VMEM((slots, recs, window), jnp.bfloat16),
     ]
-    size = sum(math.prod(ref.shape) * jnp.dtype(ref.dtype).itemsize for ref in scratch)
     return pl.pallas_call(
         functools.partial(gather_kernel, peers, chunk),
         out_shape=jax.ShapeDtypeStruct((slots, rec_rows, window), jnp.bfloat16),
@@ -294,7 +289,7 @@
             pltpu.SemaphoreType.DMA((slots,)),
         ],
         input_output_aliases=aliases,
-        compiler_params=pltpu.CompilerParams(vmem_limit_bytes=min(size + (8 << 20), 60 << 20)),
+        compiler_params=pltpu.CompilerParams(vmem_limit_bytes=60 << 20),
         cost_estimate=pl.CostEstimate(
             flops=flops, bytes_accessed=2 * recs * (total + slots * window), transcendentals=0
         ),
@@ -322,9 +317,9 @@
         for chunk in range(chunks)
     ]
     codes = jnp.concatenate([shot_onset_ticks, span_place_index])
-    codes = [codes, *fetch(codes, "line", lines)]
-    block_len = station_traces.shape[1]
-    here = jnp.stack([lax.axis_index("tm"), lax.axis_index("line"), block_len]).astype(jnp.int32)
+    codes = jnp.broadcast_to(codes[None], (lines, codes.shape[0]))
+    codes = lax.all_to_all(codes, "line", split_axis=0, concat_axis=0, tiled=True)
+    here = jnp.stack([lax.axis_index("tm"), station_traces.shape[1]]).astype(jnp.int32)
     ticks, keep, turns, back = plan_shots(
         codes, here, spectral_keep_flags, order, back_rows, shifts, slots
     )

time: 55.2 us -> 45.1 us (0.82)
  waiting for transfers between devices: 10 us -> 4.89 us
  local copies, waits for them, and re-layouts: 8.88 us -> 4.21 us
  starting transfers between devices: 14 us -> 13.4 us
    ppermute x13 -> x6, waiting for transfers between devices: 10 us -> 0.02 us  [fetch(): lax.ppermute(block, axis, [(partner(index, away, count), index) for index...]
    ppermute x13 -> x6, starting transfers between devices: 14 us -> 8.55 us  [fetch(): lax.ppermute(block, axis, [(partner(index, away, count), index) for index...]
    unnamed x16 -> x14, local copies, waits for them, and re-layouts: 7.9 us -> 2.63 us
    all_to_all x0 -> x1, starting transfers between devices: none -> 4.88 us  [on_device(): lax.all_to_all(codes, 'line', split_axis=0, concat_axis=0, tiled=True)]
    all_to_all x0 -> x1, waiting for transfers between devices: none -> 4.87 us  [on_device(): lax.all_to_all(codes, 'line', split_axis=0, concat_axis=0, tiled=True)]
    broadcast_in_dim x0 -> x1, local copies, waits for them, and re-layouts: none -> 0.6 us  [on_device(): codes = jnp.broadcast_to(codes[None], (lines, codes.shape[0]))]
  transfers between devices with their start and end apart: 13 -> 7, of which waited for: 5 -> 1; matrix products, arithmetic and copies ran while one was open for 2% -> 4% of each run, Pallas kernels for 21% -> 26%
where the time goes in v4:
time: 45.1 us; the launch traced here: 44.8 us
  Pallas kernels  20.9 us (46%)
  starting transfers between devices  13.4 us (30%)
  waiting for transfers between devices  4.89 us (11%)
  local copies, waits for them, and re-layouts  4.21 us (9%)
  other arithmetic  1.36 us (3%)
    pallas_call x2, Pallas kernels, filter_gathers(): pl.pallas_call(functools.partial(gather_kernel, peers, chunk), out_shape=...  18.5 us
    ppermute x6, starting transfers between devices, fetch(): lax.ppermute(block, axis, [(partner(index, away, count), index) for index...  8.55 us
    all_to_all x1, starting transfers between devices, on_device(): lax.all_to_all(codes, 'line', split_axis=0, concat_axis=0, tiled=True)  4.88 us
    all_to_all x1, waiting for transfers between devices, on_device(): lax.all_to_all(codes, 'line', split_axis=0, concat_axis=0, tiled=True)  4.87 us
    unnamed x14, local copies, waits for them, and re-layouts  2.63 us
    pallas_call x1, Pallas kernels, plan_shots(): pl.pallas_call(plan_kernel, out_shape=[jax.ShapeDtypeStruct((shots,), jnp...  2.31 us
    slice x1, local copies, waits for them, and re-layouts, on_device(): station_traces[chunk * RECS:(chunk + 1) * RECS]  0.98 us
  transfers between devices with their start and end apart: 7, of which 1 were waited for; matrix products, arithmetic and copies ran while one was open for 4% of the time, Pallas kernels for 26%

profile of v4, /device:TPU:0, one launch (start us, length us, event | category | flops | bytes accessed | tf_op | source)
XLA Modules:
  0.0 44.8 jit_solution(4862491361403721234)
XLA Ops:
  0.0 1.0 %fusion = (bf16[16,4096]{1,0:T(8,128)(2,1)S(1)}, bf16[16,4096]{1,0:T(8,128)(2,1)S(1)}) fusion(bf16[32,4096]{1,0:T(8,128)(2,1)} %refs_2_.3), kind=kLoop, calls=%fused_computation.2 | loop fusion | bytes 524288 | tf_op jit(solution)/shard_map/slice | solution.py:316
  1.0 4.0 %collective-permute-start.5 = (bf16[16,4096]{1,0:T(8,128)(2,1)S(1)}, bf16[16,4096]{1,0:T(8,128)(2,1)S(1)}, u32[]{:S(2)}, u32[]{:S(2)}) collective-permute-start(bf16[16,4096]{1,0:T(8,128)(2,1)S(1)} %get-tuple-element.13), channel_id=1, source_target_pairs={{24,0},{16,8},{8,16},{0,24},{25,1},{17,9},{9,17},{1,25},{26,2},{18... | collective-permute-start | bytes 393224 | tf_op jit(solution)/shard_map/ppermute | solution.py:309
  4.9 0.5 %collective-permute-start.4 = (bf16[16,4096]{1,0:T(8,128)(2,1)S(1)}, bf16[16,4096]{1,0:T(8,128)(2,1)S(1)}, u32[]{:S(2)}, u32[]{:S(2)}) collective-permute-start(bf16[16,4096]{1,0:T(8,128)(2,1)S(1)} %get-tuple-element.13), channel_id=1, source_target_pairs={{16,0},{24,8},{0,16},{8,24},{17,1},{25,9},{1,17},{9,25},{18,2},{26... | collective-permute-start | bytes 393224 | tf_op jit(solution)/shard_map/ppermute | solution.py:309
  5.5 0.1 collective-permute-start.3
  5.6 2.8 %collective-permute-start.2 = (bf16[16,4096]{1,0:T(8,128)(2,1)S(1)}, bf16[16,4096]{1,0:T(8,128)(2,1)S(1)}, u32[]{:S(2)}, u32[]{:S(2)}) collective-permute-start(bf16[16,4096]{1,0:T(8,128)(2,1)S(1)} %get-tuple-element.14), channel_id=1, source_target_pairs={{24,0},{16,8},{8,16},{0,24},{25,1},{17,9},{9,17},{1,25},{26,2},{18... | collective-permute-start | bytes 393224 | tf_op jit(solution)/shard_map/ppermute | solution.py:309
  8.4 0.5 %collective-permute-start.1 = (bf16[16,4096]{1,0:T(8,128)(2,1)S(1)}, bf16[16,4096]{1,0:T(8,128)(2,1)S(1)}, u32[]{:S(2)}, u32[]{:S(2)}) collective-permute-start(bf16[16,4096]{1,0:T(8,128)(2,1)S(1)} %get-tuple-element.14), channel_id=1, source_target_pairs={{16,0},{24,8},{0,16},{8,24},{17,1},{25,9},{1,17},{9,25},{18,2},{26... | collective-permute-start | bytes 393224 | tf_op jit(solution)/shard_map/ppermute | solution.py:309
  8.9 0.7 %pad_add_fusion = s32[16]{0:T(128)S(1)} fusion(s32[8]{0:T(128)} %param.12, s32[8]{0:T(128)} %param.11), kind=kLoop, calls=%fused_computation | loop fusion | flops 16 | bytes 128 | tf_op jit(solution)/shard_map/concatenate | solution.py:319
  9.7 0.6 %broadcast_in_dim.2 = s32[8,1,16]{2,1,0:T(1,128)} broadcast(s32[16]{0:T(128)S(1)} %pad_add_fusion), dimensions={2} | broadcast | bytes 576 | tf_op jit(solution)/shard_map/broadcast_in_dim | solution.py:320
  10.3 4.9 %all-to-all-start = ((s32[8,1,16]{2,1,0:T(1,128)}), s32[8,1,16]{2,1,0:T(1,128)S(1)}, u32[]{:S(2)}, u32[]{:S(2)}) async-start(s32[8,1,16]{2,1,0:T(1,128)} %broadcast_in_dim.2), calls=%async_computation | async-start | bytes 8192 | tf_op jit(solution)/shard_map/all_to_all | solution.py:321
  15.2 0.6 %pad_add_fusion.1.here.refs_1_ = s32[2]{0:T(128)} fusion(s32[1]{0:T(128)} %constant.18.clone.1, s32[1]{0:T(128)} %bitcast.1), kind=kLoop, calls=%fused_computation.1 | loop fusion | flops 2 | bytes 16 | tf_op jit(solution)/shard_map/stack | solution.py:322
  15.8 4.9 %all-to-all-done = s32[8,1,16]{2,1,0:T(1,128)S(1)} async-done(((s32[8,1,16]{2,1,0:T(1,128)}), s32[8,1,16]{2,1,0:T(1,128)S(1)}, u32[]{:S(2)}, u32[]{:S(2)}) %all-to-all-start) | async-done | bytes 544 | tf_op jit(solution)/shard_map/all_to_all | solution.py:321
  20.7 0.6 %copy-done = s32[8,1,16]{2,1,0:T(1,128)} copy-done((s32[8,1,16]{2,1,0:T(1,128)}, s32[8,1,16]{2,1,0:T(1,128)S(1)}, u32[]{:S(2)}) %copy-start) | copy-done | bytes 536
  21.2 2.3 %shard_map.100 = (s32[64]{0:T(128)}, f32[64,512]{1,0:T(8,128)}, f32[64,1024]{1,0:T(8,128)}, bf16[64,128]{1,0:T(8,128)(2,1)}) custom-call(s32[8,16]{1,0:T(8,128)} %bitcast.2, s32[2]{0:T(128)} %pad_add_fusion.1.here.refs_1_, s32[64,512]{1,0:T(8,128)} %flags.1, bf16[512,512]{1,0:T(8,128)(2,1)} %constant.19.clone.order, ...), custom_call_target="tpu_custom_call" | custom-call | flops 67108864 | bytes 2097152 | tf_op jit(solution)/shard_map/pallas_call | solution.py:96
  23.6 0.6 %collective-permute-start = (bf16[16,4096]{1,0:T(8,128)(2,1)S(1)}, bf16[16,4096]{1,0:T(8,128)(2,1)S(1)}, u32[]{:S(2)}, u32[]{:S(2)}) collective-permute-start(bf16[16,4096]{1,0:T(8,128)(2,1)S(1)} %get-tuple-element.14), channel_id=1, source_target_pairs={{8,0},{0,8},{24,16},{16,24},{9,1},{1,9},{25,17},{17,25},{10,2},{2,... | collective-permute-start | bytes 393224 | tf_op jit(solution)/shard_map/ppermute | solution.py:309
  24.2 0.0 collective-permute-done.4.refs_4_
  24.2 0.0 collective-permute-done.3.refs_3_
  24.2 0.0 copy-done.3
  24.2 0.6 %copy-done.4 = bf16[16,4096]{1,0:T(8,128)(2,1)} copy-done((bf16[16,4096]{1,0:T(8,128)(2,1)}, bf16[16,4096]{1,0:T(8,128)(2,1)S(1)}, u32[]{:S(2)}) %copy-start.4) | copy-done | bytes 131096
  24.9 0.1 copy-done.5
  24.9 9.3 %shard_map.101.refs_12_ = bf16[32,32,1024]{2,1,0:T(8,128)(2,1)} custom-call(s32[64]{0:T(128)} %get-tuple-element.9.refs_0_, s32[2]{0:T(128)} %pad_add_fusion.1.here.refs_1_, bf16[32,4096]{1,0:T(8,128)(2,1)} %refs_2_.3, bf16[16,4096]{1,0:T(8,128)(2,1)} %copy-done.5, bf16[16,4096]{1,0:T(8,128)(2,1)} %copy-done.4, bf16[16,4096]{1,0:T(8,128)(2,1)} %copy-done.3, ...), custom_call_target="tpu_custom_call" | custom-call | flops 2013265920 | bytes 1572864 | tf_op jit(solution)/shard_map/pallas_call | solution.py:280
  34.2 0.6 %copy-done.1 = bf16[16,4096]{1,0:T(8,128)(2,1)} copy-done((bf16[16,4096]{1,0:T(8,128)(2,1)}, bf16[16,4096]{1,0:T(8,128)(2,1)S(1)}, u32[]{:S(2)}) %copy-start.1) | copy-done | bytes 131096
  34.9 0.1 copy-done.2
  34.9 0.7 %copy-done.6 = bf16[16,4096]{1,0:T(8,128)(2,1)} copy-done((bf16[16,4096]{1,0:T(8,128)(2,1)}, bf16[16,4096]{1,0:T(8,128)(2,1)S(1)}, u32[]{:S(2)}) %copy-start.6) | copy-done | bytes 131096
  35.6 9.3 %shard_map.102 = bf16[32,32,1024]{2,1,0:T(8,128)(2,1)} custom-call(s32[64]{0:T(128)} %get-tuple-element.9.refs_0_, s32[2]{0:T(128)} %pad_add_fusion.1.here.refs_1_, bf16[32,4096]{1,0:T(8,128)(2,1)} %refs_2_.3, bf16[16,4096]{1,0:T(8,128)(2,1)} %copy-done.6, bf16[16,4096]{1,0:T(8,128)(2,1)} %copy-done.2, ...), custom_call_target="tpu_custom_call", output_to_operand_aliasing={{}: (12, {})} | custom-call | flops 2013265920 | bytes 1572864 | tf_op jit(solution)/shard_map/pallas_call | solution.py:280
  (11 shorter events, 0.0 us)
Async XLA Ops:
  1.0 22.6 %collective-permute-start.5 = (bf16[16,4096]{1,0:T(8,128)(2,1)S(1)}, bf16[16,4096]{1,0:T(8,128)(2,1)S(1)}, u32[]{:S(2)}, u32[]{:S(2)}) collective-permute-start(bf16[16,4096]{1,0:T(8,128)(2,1)S(1)} %get-tuple-element.13), channel_id=1, source_target_pairs={{24,0},{16,8},{8,16},{0,24},{25,1},{17,9},{9,17},{1,25},{26,2},{18... | collective-permute-start | bytes 393224 | tf_op jit(solution)/shard_map/ppermute | solution.py:309
  4.9 19.2 %collective-permute-start.4 = (bf16[16,4096]{1,0:T(8,128)(2,1)S(1)}, bf16[16,4096]{1,0:T(8,128)(2,1)S(1)}, u32[]{:S(2)}, u32[]{:S(2)}) collective-permute-start(bf16[16,4096]{1,0:T(8,128)(2,1)S(1)} %get-tuple-element.13), channel_id=1, source_target_pairs={{16,0},{24,8},{0,16},{8,24},{17,1},{25,9},{1,17},{9,25},{18,2},{26... | collective-permute-start | bytes 393224 | tf_op jit(solution)/shard_map/ppermute | solution.py:309
  5.5 18.7 %collective-permute-start.3 = (bf16[16,4096]{1,0:T(8,128)(2,1)S(1)}, bf16[16,4096]{1,0:T(8,128)(2,1)S(1)}, u32[]{:S(2)}, u32[]{:S(2)}) collective-permute-start(bf16[16,4096]{1,0:T(8,128)(2,1)S(1)} %get-tuple-element.13), channel_id=1, source_target_pairs={{8,0},{0,8},{24,16},{16,24},{9,1},{1,9},{25,17},{17,25},{10,2},{2,... | collective-permute-start | bytes 393224 | tf_op jit(solution)/shard_map/ppermute | solution.py:309
  5.6 28.6 %collective-permute-start.2 = (bf16[16,4096]{1,0:T(8,128)(2,1)S(1)}, bf16[16,4096]{1,0:T(8,128)(2,1)S(1)}, u32[]{:S(2)}, u32[]{:S(2)}) collective-permute-start(bf16[16,4096]{1,0:T(8,128)(2,1)S(1)} %get-tuple-element.14), channel_id=1, source_target_pairs={{24,0},{16,8},{8,16},{0,24},{25,1},{17,9},{9,17},{1,25},{26,2},{18... | collective-permute-start | bytes 393224 | tf_op jit(solution)/shard_map/ppermute | solution.py:309
  8.4 25.8 %collective-permute-start.1 = (bf16[16,4096]{1,0:T(8,128)(2,1)S(1)}, bf16[16,4096]{1,0:T(8,128)(2,1)S(1)}, u32[]{:S(2)}, u32[]{:S(2)}) collective-permute-start(bf16[16,4096]{1,0:T(8,128)(2,1)S(1)} %get-tuple-element.14), channel_id=1, source_target_pairs={{16,0},{24,8},{0,16},{8,24},{17,1},{25,9},{1,17},{9,25},{18,2},{26... | collective-permute-start | bytes 393224 | tf_op jit(solution)/shard_map/ppermute | solution.py:309
  10.3 10.4 %all-to-all-start = ((s32[8,1,16]{2,1,0:T(1,128)}), s32[8,1,16]{2,1,0:T(1,128)S(1)}, u32[]{:S(2)}, u32[]{:S(2)}) async-start(s32[8,1,16]{2,1,0:T(1,128)} %broadcast_in_dim.2), calls=%async_computation | async-start | bytes 8192 | tf_op jit(solution)/shard_map/all_to_all | solution.py:321
  20.7 0.6 %copy-start = (s32[8,1,16]{2,1,0:T(1,128)}, s32[8,1,16]{2,1,0:T(1,128)S(1)}, u32[]{:S(2)}) copy-start(s32[8,1,16]{2,1,0:T(1,128)S(1)} %all-to-all-done) | copy-start | bytes 1540
  23.6 0.7 %copy-start.3 = (bf16[16,4096]{1,0:T(8,128)(2,1)}, bf16[16,4096]{1,0:T(8,128)(2,1)S(1)}, u32[]{:S(2)}) copy-start(bf16[16,4096]{1,0:T(8,128)(2,1)S(1)} %collective-permute-done.5.refs_5_) | copy-start | bytes 393220
  23.6 10.6 %collective-permute-start = (bf16[16,4096]{1,0:T(8,128)(2,1)S(1)}, bf16[16,4096]{1,0:T(8,128)(2,1)S(1)}, u32[]{:S(2)}, u32[]{:S(2)}) collective-permute-start(bf16[16,4096]{1,0:T(8,128)(2,1)S(1)} %get-tuple-element.14), channel_id=1, source_target_pairs={{8,0},{0,8},{24,16},{16,24},{9,1},{1,9},{25,17},{17,25},{10,2},{2,... | collective-permute-start | bytes 393224 | tf_op jit(solution)/shard_map/ppermute | solution.py:309
  24.2 0.7 %copy-start.4 = (bf16[16,4096]{1,0:T(8,128)(2,1)}, bf16[16,4096]{1,0:T(8,128)(2,1)S(1)}, u32[]{:S(2)}) copy-start(bf16[16,4096]{1,0:T(8,128)(2,1)S(1)} %collective-permute-done.4.refs_4_) | copy-start | bytes 393220
  24.2 0.7 %copy-start.5 = (bf16[16,4096]{1,0:T(8,128)(2,1)}, bf16[16,4096]{1,0:T(8,128)(2,1)S(1)}, u32[]{:S(2)}) copy-start(bf16[16,4096]{1,0:T(8,128)(2,1)S(1)} %collective-permute-done.3.refs_3_) | copy-start | bytes 393220
  34.2 0.7 %copy-start.1 = (bf16[16,4096]{1,0:T(8,128)(2,1)}, bf16[16,4096]{1,0:T(8,128)(2,1)S(1)}, u32[]{:S(2)}) copy-start(bf16[16,4096]{1,0:T(8,128)(2,1)S(1)} %collective-permute-done.2.refs_5_) | copy-start | bytes 393220
  34.2 0.7 %copy-start.2 = (bf16[16,4096]{1,0:T(8,128)(2,1)}, bf16[16,4096]{1,0:T(8,128)(2,1)S(1)}, u32[]{:S(2)}) copy-start(bf16[16,4096]{1,0:T(8,128)(2,1)S(1)} %collective-permute-done.1.refs_4_) | copy-start | bytes 393220
  34.9 0.7 %copy-start.6 = (bf16[16,4096]{1,0:T(8,128)(2,1)}, bf16[16,4096]{1,0:T(8,128)(2,1)S(1)}, u32[]{:S(2)}) copy-start(bf16[16,4096]{1,0:T(8,128)(2,1)S(1)} %collective-permute-done.refs_3_) | copy-start | bytes 393220

commit v5 on v1

v5 whole, which is shorter than its diff:
```python
import functools
import math

import jax
import jax.numpy as jnp
import ml_dtypes
import numpy as np
from jax import lax
from jax.experimental import pallas as pl
from jax.experimental.pallas import tpu as pltpu
from jax.sharding import PartitionSpec as P

LANES = 128
RECS = 16


def make_tables(window, shots):
    half = window // 2
    quarter = half // 2
    times = np.arange(half)
    freqs = np.concatenate([np.arange(0, half, 2), np.arange(1, half, 2)])

    def waves(rows, columns, period):
        phase = (rows[:, None] * columns[None, :] % period) * (2.0 * math.pi / period)
        return np.cos(phase), np.sin(phase)

    bf16 = ml_dtypes.bfloat16
    cosine, sine = waves(times, freqs, window)
    forward = np.stack(
        [
            np.concatenate([cosine[:, cut], -sine[:, cut]], axis=1)
            for cut in (slice(0, quarter), slice(quarter, half))
        ]
    ).astype(bf16)
    gain = np.where(freqs == 0, 0.5, 1.0)[:, None] * (2.0 / (window * shots))
    inverse = np.stack(
        [
            np.concatenate([gain[cut] * cosine.T[cut], -gain[cut] * sine.T[cut]], axis=0)
            for cut in (slice(0, quarter), slice(quarter, half))
        ]
    ).astype(bf16)
    turn_cos, turn_sin = waves(np.arange(shots), np.arange(shots), shots)
    over_shots = np.block([[turn_cos, turn_sin], [-turn_sin, turn_cos]]).astype(bf16)
    back_rows = np.stack(
        [
            np.concatenate([turn_cos, -turn_sin], axis=1),
            np.concatenate([turn_sin, turn_cos], axis=1),
        ]
    ).astype(bf16)
    order = np.zeros((half, half), bf16)
    order[freqs, np.arange(half)] = 1
    return forward, inverse, over_shots, back_rows, order


def partner(index, away, count):
    if count & (count - 1) == 0:
        return index ^ away
    return (index + away) % count


def gather_kernel(peers, *refs):
    codes, here, *refs = refs
    traces, refs = refs[:peers], refs[peers:]
    keep, over_shots, back_rows = refs[:3]
    table_refs, out = refs[3:5], refs[5]
    forward, inverse, tiles, folds, spectra, mixed, swapped, ready, table_sem, out_sem = refs[6:]
    rec_rows, block_len = traces[0].shape
    shots, half = keep.shape
    window = 2 * half
    quarter = half // 2
    slots = ready.shape[1]
    share = codes.shape[1] // 2
    recs = RECS
    wide = window // LANES
    mid = wide // 2
    per_block = block_len // LANES
    f32, bf16 = jnp.float32, jnp.bfloat16

    table_copies = [
        pltpu.make_async_copy(table, place, table_sem.at[index])
        for index, (table, place) in enumerate(zip(table_refs, (forward, inverse)))
    ]
    for copy in table_copies:
        copy.start()

    for away, block in enumerate(traces):
        base = partner(here[0], away, peers) * per_block
        for tile in range(per_block):
            tiles[base + tile] = block[:, tile * LANES : (tile + 1) * LANES]
    for tile in range(wide):
        tiles[peers * per_block + tile] = jnp.zeros((rec_rows, LANES), bf16)

    start = here[0] * here[1]
    shot_lane = lax.broadcasted_iota(jnp.int32, (1, shots), 1)
    place_all = jnp.full((1, shots), -1, jnp.int32)
    for shot in range(shots):
        line, item = divmod(shot, share)
        tick = codes[line, item]
        mine = (tick >= start) & (tick < start + here[1])
        place = jnp.where(mine, codes[line, share + item], -1)
        place_all = jnp.where(shot_lane == shot, place, place_all)
    slot_row = lax.broadcasted_iota(jnp.int32, (slots, shots), 0)
    owned = (slot_row == place_all).astype(f32).astype(bf16)
    back = jnp.concatenate(
        [jnp.dot(owned, back_rows[part], preferred_element_type=f32) for part in range(2)], axis=0
    ).astype(bf16)

    lane = lax.broadcasted_iota(jnp.int16, (recs, LANES), 1)

    def cut(shot, rows):
        tick = codes[shot // share, shot % share]
        first = lax.shift_right_logical(tick, LANES.bit_length() - 1)
        within = tick & (LANES - 1)
        piece = [tiles[first + tile, rows] for tile in range(wide + 1)]
        early = lane < within.astype(jnp.int16)
        piece = [jnp.where(early, piece[tile + 1], piece[tile]) for tile in range(wide)]
        turn = (LANES - within) & (LANES - 1)
        sums = [pltpu.roll(piece[tile] + piece[tile + mid], turn, 1) for tile in range(mid)]
        gaps = [pltpu.roll(piece[tile] - piece[tile + mid], turn, 1) for tile in range(mid)]
        return sums, gaps

    out_copies = []
    for chunk in range(rec_rows // recs):
        rows = slice(chunk * recs, (chunk + 1) * recs)
        for first in range(0, shots, 16):
            cuts = [cut(shot, rows) for shot in range(first, first + 16)]
            for part in range(2):
                for tile in range(mid):
                    panel = jnp.stack([cuts[item][part][tile] for item in range(16)])
                    folds[part, :, first : first + 16, tile * LANES : (tile + 1) * LANES] = (
                        jnp.swapaxes(panel, 0, 1)
                    )
        if chunk == 0:
            table_copies[0].wait()
        group = 8
        for rec in range(0, recs, group):
            for part in range(2):
                found = jnp.dot(
                    folds[part, rec : rec + group].reshape(group * shots, half),
                    forward[part],
                    preferred_element_type=f32,
                )
                spectra[part, rec * shots : (rec + group) * shots] = found.astype(bf16)
        for rec in range(recs):
            at = slice(rec * shots, (rec + 1) * shots)
            even, odd = spectra[0, at], spectra[1, at]
            stacked = jnp.concatenate(
                [
                    jnp.concatenate([even[:, :quarter], odd[:, :quarter]], axis=1),
                    jnp.concatenate([even[:, quarter:], odd[:, quarter:]], axis=1),
                ],
                axis=0,
            )
            waves = jnp.dot(over_shots[...], stacked, preferred_element_type=f32)
            masked = jnp.concatenate(
                [waves[:shots] * keep[...], waves[shots:] * keep[...]], axis=0
            ).astype(bf16)
            again = jnp.dot(back, masked, preferred_element_type=f32).astype(bf16)
            at = slice(rec * slots, (rec + 1) * slots)
            for part in range(2):
                columns = slice(part * quarter, (part + 1) * quarter)
                mixed[part, at, :quarter] = again[:slots, columns]
                mixed[part, at, quarter:] = again[slots:, columns]
        if chunk == 0:
            table_copies[1].wait()
        for rec in range(0, recs, group):
            at = slice(rec * slots, (rec + group) * slots)
            even, odd = [
                jnp.dot(mixed[part, at], inverse[part], preferred_element_type=f32)
                for part in range(2)
            ]
            swapped[rec : rec + group, :, :half] = (
                (even + odd).astype(bf16).reshape(group, slots, half)
            )
            swapped[rec : rec + group, :, half:] = (
                (even - odd).astype(bf16).reshape(group, slots, half)
            )
        for slot in range(0, slots, 16):
            for tile in range(wide):
                at = slice(tile * LANES, (tile + 1) * LANES)
                ready[chunk, slot : slot + 16, :, at] = jnp.swapaxes(
                    swapped[:, slot : slot + 16, at], 0, 1
                )
        copy = pltpu.make_async_copy(
            ready.at[chunk], out.at[:, pl.ds(chunk * recs, recs)], out_sem.at[chunk]
        )
        copy.start()
        out_copies.append(copy)
    for copy in out_copies:
        copy.wait()


def filter_gathers(codes, here, traces, keep, tables):
    forward, inverse, over_shots, back_rows = tables
    peers = len(traces)
    rec_rows, block_len = traces[0].shape
    shots, half = keep.shape
    window = 2 * half
    slots = 2 * shots // peers
    total = peers * block_len
    chunks = rec_rows // RECS
    smem = pl.BlockSpec(memory_space=pltpu.SMEM)
    vmem = pl.BlockSpec(memory_space=pltpu.VMEM)
    anywhere = pl.BlockSpec(memory_space=pl.ANY)
    flops = 2 * rec_rows * (
        shots * window * half
        + slots * window * half
        + 4 * shots * shots * half
        + 4 * slots * shots * half
    )
    bf16 = jnp.bfloat16
    return pl.pallas_call(
        functools.partial(gather_kernel, peers),
        out_shape=jax.ShapeDtypeStruct((slots, rec_rows, window), bf16),
        in_specs=[smem, smem] + [vmem] * (peers + 3) + [anywhere] * 2,
        out_specs=anywhere,
        scratch_shapes=[
            pltpu.VMEM(forward.shape, bf16),
            pltpu.VMEM(inverse.shape, bf16),
            pltpu.VMEM(((total + window) // LANES, rec_rows, LANES), bf16),
            pltpu.VMEM((2, RECS, shots, half), bf16),
            pltpu.VMEM((2, RECS * shots, half), bf16),
            pltpu.VMEM((2, RECS * slots, half), bf16),
            pltpu.VMEM((RECS, slots, window), bf16),
            pltpu.VMEM((chunks, slots, RECS, window), bf16),
            pltpu.SemaphoreType.DMA((2,)),
            pltpu.SemaphoreType.DMA((chunks,)),
        ],
        compiler_params=pltpu.CompilerParams(vmem_limit_bytes=60 << 20),
        cost_estimate=pl.CostEstimate(
            flops=flops,
            bytes_accessed=2 * rec_rows * (total + slots * window),
            transcendentals=0,
        ),
    )(codes, here, *traces, keep, over_shots, back_rows, forward, inverse)


def on_device(station_traces, shot_onset_ticks, span_place_index, spectral_keep_flags):
    shots, half = spectral_keep_flags.shape
    *tables, order = make_tables(2 * half, shots)
    peers = lax.axis_size("tm")
    lines = lax.axis_size("line")
    traces = [station_traces] + [
        lax.ppermute(
            station_traces,
            "tm",
            [(partner(index, away, peers), index) for index in range(peers)],
        )
        for away in range(1, peers)
    ]
    codes = jnp.concatenate([shot_onset_ticks, span_place_index])
    codes = jnp.broadcast_to(codes[None], (lines, codes.shape[0]))
    codes = lax.all_to_all(codes, "line", split_axis=0, concat_axis=0, tiled=True)
    here = jnp.stack([lax.axis_index("tm"), station_traces.shape[1]]).astype(jnp.int32)
    keep = jnp.dot(
        spectral_keep_flags.astype(jnp.bfloat16), order, preferred_element_type=jnp.float32
    )
    return filter_gathers(codes, here, traces, keep, tables)


def solution(mesh):
    in_specs = (P("line", "tm"), P("line"), P("line"), P())
    out_specs = P("tm", "line", None)
    return jax.shard_map(
        on_device, mesh=mesh, in_specs=in_specs, out_specs=out_specs, check_vma=False
    )
```

time: 67.3 us -> 33.1 us (0.49)
  between operations: 14.1 us -> 0.04 us
  waiting for transfers between devices: 16.5 us -> 2.9 us
  blocking collectives: 10.6 us -> 0 us
  starting transfers between devices: 0.01 us -> 9.81 us
  local copies, waits for them, and re-layouts: 9.17 us -> 1.46 us
  other arithmetic: 0 us -> 1.36 us
    all_gather x1 -> x0, waiting for transfers between devices: 15.8 us -> none  [on_device(): traces = lax.all_gather(station_traces, 'tm', axis=0)]
    unnamed x1 -> x0, blocking collectives: 10.6 us -> none
    unnamed x17 -> x8, local copies, waits for them, and re-layouts: 9.17 us -> 0.86 us
    all_to_all x0 -> x1, starting transfers between devices: none -> 5.35 us  [on_device(): lax.all_to_all(codes, 'line', split_axis=0, concat_axis=0, tiled=True)]
    ppermute x0 -> x3, starting transfers between devices: none -> 4.46 us  [on_device(): lax.ppermute(station_traces, 'tm', [(partner(index, away, peers), index)...]
    all_to_all x0 -> x1, waiting for transfers between devices: none -> 2.89 us  [on_device(): lax.all_to_all(codes, 'line', split_axis=0, concat_axis=0, tiled=True)]
    concatenate x0 -> x1, other arithmetic: none -> 0.75 us  [on_device(): codes = jnp.concatenate([shot_onset_ticks, span_place_index])]
    unnamed x1 -> x0, waiting for transfers between devices: 0.71 us -> none
  transfers between devices with their start and end apart: 1 -> 4, of which waited for: 1 -> 1; matrix products, arithmetic and copies ran while one was open for 6% -> 12% of each run, Pallas kernels for 0% -> 0%
where the time goes in v5:
time: 33.1 us; the launch traced here: 32.8 us
  Pallas kernels  15.3 us (46%)
  starting transfers between devices  9.81 us (30%)
  waiting for transfers between devices  2.9 us (9%)
  matrix products  1.98 us (6%)
  local copies, waits for them, and re-layouts  1.46 us (4%)
  other arithmetic  1.36 us (4%)
    pallas_call x1, Pallas kernels, filter_gathers(): pl.pallas_call(functools.partial(gather_kernel, peers), out_shape=jax.Sha...  15.3 us
    all_to_all x1, starting transfers between devices, on_device(): lax.all_to_all(codes, 'line', split_axis=0, concat_axis=0, tiled=True)  5.35 us
    ppermute x3, starting transfers between devices, on_device(): lax.ppermute(station_traces, 'tm', [(partner(index, away, peers), index)...  4.46 us
    all_to_all x1, waiting for transfers between devices, on_device(): lax.all_to_all(codes, 'line', split_axis=0, concat_axis=0, tiled=True)  2.89 us
    dot_general x1, matrix products, on_device(): jnp.dot(spectral_keep_flags.astype(jnp.bfloat16), order, preferred_elemen...  1.98 us
    unnamed x8, local copies, waits for them, and re-layouts  0.86 us
    concatenate x1, other arithmetic, on_device(): codes = jnp.concatenate([shot_onset_ticks, span_place_index])  0.75 us
  transfers between devices with their start and end apart: 4, of which 1 were waited for; matrix products, arithmetic and copies ran while one was open for 12% of the time, Pallas kernels for 0%

profile of v5, /device:TPU:0, one launch (start us, length us, event | category | flops | bytes accessed | tf_op | source)
XLA Modules:
  0.0 32.8 jit_solution(7833818694371410470)
XLA Ops:
  0.0 3.0 %collective-permute-start.1 = (bf16[32,4096]{1,0:T(8,128)(2,1)}, bf16[32,4096]{1,0:T(8,128)(2,1)S(1)}, u32[]{:S(2)}, u32[]{:S(2)}) collective-permute-start(bf16[32,4096]{1,0:T(8,128)(2,1)} %refs_2_.1), channel_id=1, source_target_pairs={{16,0},{24,8},{0,16},{8,24},{17,1},{25,9},{1,17},{9,25},{18,2},{26... | collective-permute-start | bytes 786440 | tf_op jit(solution)/shard_map/ppermute | solution.py:244
  3.0 1.5 %collective-permute-start = (bf16[32,4096]{1,0:T(8,128)(2,1)}, bf16[32,4096]{1,0:T(8,128)(2,1)S(1)}, u32[]{:S(2)}, u32[]{:S(2)}) collective-permute-start(bf16[32,4096]{1,0:T(8,128)(2,1)} %refs_2_.1), channel_id=1, source_target_pairs={{8,0},{0,8},{24,16},{16,24},{9,1},{1,9},{25,17},{17,25},{10,2},{2,... | collective-permute-start | bytes 786440 | tf_op jit(solution)/shard_map/ppermute | solution.py:244
  4.5 0.0 collective-permute-start.2
  4.5 0.7 %pad_add_fusion = s32[16]{0:T(128)S(1)} fusion(s32[8]{0:T(128)} %param.11, s32[8]{0:T(128)} %param.10), kind=kLoop, calls=%fused_computation.2 | loop fusion | flops 16 | bytes 128 | tf_op jit(solution)/shard_map/concatenate | solution.py:251
  5.2 0.6 %broadcast_in_dim.2 = s32[8,1,16]{2,1,0:T(1,128)} broadcast(s32[16]{0:T(128)S(1)} %pad_add_fusion), dimensions={2} | broadcast | bytes 576 | tf_op jit(solution)/shard_map/broadcast_in_dim | solution.py:252
  5.8 5.4 %all-to-all-start = ((s32[8,1,16]{2,1,0:T(1,128)}), s32[8,1,16]{2,1,0:T(1,128)S(1)}, u32[]{:S(2)}, u32[]{:S(2)}) async-start(s32[8,1,16]{2,1,0:T(1,128)} %broadcast_in_dim.2), calls=%async_computation | async-start | bytes 8192 | tf_op jit(solution)/shard_map/all_to_all | solution.py:253
  11.2 2.0 %convolution_bitcast_fusion.refs_6_ = f32[64,512]{1,0:T(8,128)} fusion(bf16[512,512]{1,0:T(8,128)(2,1)} %constant.17.clone, s32[64,512]{1,0:T(8,128)} %param.12), kind=kOutput, calls=%fused_computation | convolution fusion | flops 33587200 | bytes 786432 | tf_op jit(solution)/shard_map/dot_general | solution.py:255
  13.1 0.6 %pad_add_fusion.1.refs_1_ = s32[2]{0:T(128)} fusion(s32[1]{0:T(128)} %constant.16.clone.1, s32[1]{0:T(128)} %bitcast.1), kind=kLoop, calls=%fused_computation.3 | loop fusion | flops 2 | bytes 16 | tf_op jit(solution)/shard_map/stack | solution.py:254
  13.7 2.9 %all-to-all-done = s32[8,1,16]{2,1,0:T(1,128)S(1)} async-done(((s32[8,1,16]{2,1,0:T(1,128)}), s32[8,1,16]{2,1,0:T(1,128)S(1)}, u32[]{:S(2)}, u32[]{:S(2)}) %all-to-all-start) | async-done | bytes 544 | tf_op jit(solution)/shard_map/all_to_all | solution.py:253
  16.6 0.0 copy-start
  16.6 0.0 collective-permute-done.1.refs_4_
  16.6 0.0 copy-start.1
  16.7 0.0 collective-permute-done.refs_3_
  16.7 0.0 copy-start.2
  16.7 0.0 collective-permute-done.2.refs_5_
  16.7 0.0 copy-start.3
  16.7 0.5 %copy-done = s32[8,1,16]{2,1,0:T(1,128)} copy-done((s32[8,1,16]{2,1,0:T(1,128)}, s32[8,1,16]{2,1,0:T(1,128)S(1)}, u32[]{:S(2)}) %copy-start) | copy-done | bytes 536
  17.2 0.1 copy-done.1
  17.4 0.1 copy-done.2
  17.5 0.1 copy-done.3
  17.5 15.3 %shard_map.91 = bf16[32,32,1024]{2,1,0:T(8,128)(2,1)} custom-call(s32[8,16]{1,0:T(8,128)} %bitcast.5, s32[2]{0:T(128)} %pad_add_fusion.1.refs_1_, bf16[32,4096]{1,0:T(8,128)(2,1)} %refs_2_.1, bf16[32,4096]{1,0:T(8,128)(2,1)} %copy-done.2, bf16[32,4096]{1,0:T(8,128)(2,1)} %copy-done.1, bf16[32,4096]{1,0:T(8,128)(2,1)} %copy-done.3, ...), custom_call_target="tpu_custom_call" | custom-call | flops 4026531840 | bytes 3145728 | tf_op jit(solution)/shard_map/pallas_call | solution.py:212
Async XLA Ops:
  0.0 16.6 %collective-permute-start.1 = (bf16[32,4096]{1,0:T(8,128)(2,1)}, bf16[32,4096]{1,0:T(8,128)(2,1)S(1)}, u32[]{:S(2)}, u32[]{:S(2)}) collective-permute-start(bf16[32,4096]{1,0:T(8,128)(2,1)} %refs_2_.1), channel_id=1, source_target_pairs={{16,0},{24,8},{0,16},{8,24},{17,1},{25,9},{1,17},{9,25},{18,2},{26... | collective-permute-start | bytes 786440 | tf_op jit(solution)/shard_map/ppermute | solution.py:244
  3.0 13.7 %collective-permute-start = (bf16[32,4096]{1,0:T(8,128)(2,1)}, bf16[32,4096]{1,0:T(8,128)(2,1)S(1)}, u32[]{:S(2)}, u32[]{:S(2)}) collective-permute-start(bf16[32,4096]{1,0:T(8,128)(2,1)} %refs_2_.1), channel_id=1, source_target_pairs={{8,0},{0,8},{24,16},{16,24},{9,1},{1,9},{25,17},{17,25},{10,2},{2,... | collective-permute-start | bytes 786440 | tf_op jit(solution)/shard_map/ppermute | solution.py:244
  4.5 12.2 %collective-permute-start.2 = (bf16[32,4096]{1,0:T(8,128)(2,1)}, bf16[32,4096]{1,0:T(8,128)(2,1)S(1)}, u32[]{:S(2)}, u32[]{:S(2)}) collective-permute-start(bf16[32,4096]{1,0:T(8,128)(2,1)} %refs_2_.1), channel_id=1, source_target_pairs={{24,0},{16,8},{8,16},{0,24},{25,1},{17,9},{9,17},{1,25},{26,2},{18... | collective-permute-start | bytes 786440 | tf_op jit(solution)/shard_map/ppermute | solution.py:244
  5.8 10.8 %all-to-all-start = ((s32[8,1,16]{2,1,0:T(1,128)}), s32[8,1,16]{2,1,0:T(1,128)S(1)}, u32[]{:S(2)}, u32[]{:S(2)}) async-start(s32[8,1,16]{2,1,0:T(1,128)} %broadcast_in_dim.2), calls=%async_computation | async-start | bytes 8192 | tf_op jit(solution)/shard_map/all_to_all | solution.py:253
  16.6 0.6 %copy-start = (s32[8,1,16]{2,1,0:T(1,128)}, s32[8,1,16]{2,1,0:T(1,128)S(1)}, u32[]{:S(2)}) copy-start(s32[8,1,16]{2,1,0:T(1,128)S(1)} %all-to-all-done) | copy-start | bytes 1540
  16.6 0.7 %copy-start.1 = (bf16[32,4096]{1,0:T(8,128)(2,1)}, bf16[32,4096]{1,0:T(8,128)(2,1)S(1)}, u32[]{:S(2)}) copy-start(bf16[32,4096]{1,0:T(8,128)(2,1)S(1)} %collective-permute-done.1.refs_4_) | copy-start | bytes 786436
  16.7 0.8 %copy-start.2 = (bf16[32,4096]{1,0:T(8,128)(2,1)}, bf16[32,4096]{1,0:T(8,128)(2,1)S(1)}, u32[]{:S(2)}) copy-start(bf16[32,4096]{1,0:T(8,128)(2,1)S(1)} %collective-permute-done.refs_3_) | copy-start | bytes 786436
  16.7 0.9 %copy-start.3 = (bf16[32,4096]{1,0:T(8,128)(2,1)}, bf16[32,4096]{1,0:T(8,128)(2,1)S(1)}, u32[]{:S(2)}) copy-start(bf16[32,4096]{1,0:T(8,128)(2,1)S(1)} %collective-permute-done.2.refs_5_) | copy-start | bytes 786436

commit v6 on v5

--- a/solution.py
+++ b/solution.py
@@ -40,6 +40,9 @@
         ]
     ).astype(bf16)
     turn_cos, turn_sin = waves(np.arange(shots), np.arange(shots), shots)
+    forward, inverse = [
+        table.reshape(2, half, half // LANES, LANES).swapaxes(1, 2) for table in (forward, inverse)
+    ]
     over_shots = np.block([[turn_cos, turn_sin], [-turn_sin, turn_cos]]).astype(bf16)
     back_rows = np.stack(
         [
@@ -67,12 +70,12 @@
     rec_rows, block_len = traces[0].shape
     shots, half = keep.shape
     window = 2 * half
-    quarter = half // 2
-    slots = ready.shape[1]
+    slots = ready.shape[2]
     share = codes.shape[1] // 2
     recs = RECS
     wide = window // LANES
     mid = wide // 2
+    arms = mid // 2
     per_block = block_len // LANES
     f32, bf16 = jnp.float32, jnp.bfloat16
 
@@ -119,6 +122,13 @@
         gaps = [pltpu.roll(piece[tile] - piece[tile + mid], turn, 1) for tile in range(mid)]
         return sums, gaps
 
+    def product(left, right, part):
+        return jnp.dot(
+            left,
+            jnp.concatenate([right[part, tile] for tile in range(mid)], axis=1),
+            preferred_element_type=f32,
+        )
+
     out_copies = []
     for chunk in range(rec_rows // recs):
         rows = slice(chunk * recs, (chunk + 1) * recs)
@@ -127,30 +137,30 @@
             for part in range(2):
                 for tile in range(mid):
                     panel = jnp.stack([cuts[item][part][tile] for item in range(16)])
-                    folds[part, :, first : first + 16, tile * LANES : (tile + 1) * LANES] = (
-                        jnp.swapaxes(panel, 0, 1)
-                    )
+                    folds[part, tile, :, first : first + 16] = jnp.swapaxes(panel, 0, 1)
         if chunk == 0:
             table_copies[0].wait()
         group = 8
         for rec in range(0, recs, group):
             for part in range(2):
-                found = jnp.dot(
-                    folds[part, rec : rec + group].reshape(group * shots, half),
-                    forward[part],
-                    preferred_element_type=f32,
-                )
-                spectra[part, rec * shots : (rec + group) * shots] = found.astype(bf16)
+                panel = [
+                    folds[part, tile, rec : rec + group].reshape(group * shots, LANES)
+                    for tile in range(mid)
+                ]
+                found = product(jnp.concatenate(panel, axis=1), forward, part).astype(bf16)
+                for tile in range(mid):
+                    spectra[part, tile, rec * shots : (rec + group) * shots] = found[
+                        :, tile * LANES : (tile + 1) * LANES
+                    ]
         for rec in range(recs):
             at = slice(rec * shots, (rec + 1) * shots)
-            even, odd = spectra[0, at], spectra[1, at]
-            stacked = jnp.concatenate(
-                [
-                    jnp.concatenate([even[:, :quarter], odd[:, :quarter]], axis=1),
-                    jnp.concatenate([even[:, quarter:], odd[:, quarter:]], axis=1),
-                ],
-                axis=0,
-            )
+            real, imag = [
+                jnp.concatenate(
+                    [spectra[part, tile, at] for part in range(2) for tile in tiles_of], axis=1
+                )
+                for tiles_of in (range(arms), range(arms, mid))
+            ]
+            stacked = jnp.concatenate([real, imag], axis=0)
             waves = jnp.dot(over_shots[...], stacked, preferred_element_type=f32)
             masked = jnp.concatenate(
                 [waves[:shots] * keep[...], waves[shots:] * keep[...]], axis=0
@@ -158,34 +168,42 @@
             again = jnp.dot(back, masked, preferred_element_type=f32).astype(bf16)
             at = slice(rec * slots, (rec + 1) * slots)
             for part in range(2):
-                columns = slice(part * quarter, (part + 1) * quarter)
-                mixed[part, at, :quarter] = again[:slots, columns]
-                mixed[part, at, quarter:] = again[slots:, columns]
+                for arm in range(arms):
+                    tile = part * arms + arm
+                    columns = slice(tile * LANES, (tile + 1) * LANES)
+                    mixed[part, arm, at] = again[:slots, columns]
+                    mixed[part, arms + arm, at] = again[slots:, columns]
         if chunk == 0:
             table_copies[1].wait()
         for rec in range(0, recs, group):
             at = slice(rec * slots, (rec + group) * slots)
             even, odd = [
-                jnp.dot(mixed[part, at], inverse[part], preferred_element_type=f32)
+                product(
+                    jnp.concatenate([mixed[part, tile, at] for tile in range(mid)], axis=1),
+                    inverse,
+                    part,
+                )
                 for part in range(2)
             ]
-            swapped[rec : rec + group, :, :half] = (
-                (even + odd).astype(bf16).reshape(group, slots, half)
+            early, late = (even + odd).astype(bf16), (even - odd).astype(bf16)
+            for tile in range(mid):
+                columns = slice(tile * LANES, (tile + 1) * LANES)
+                for half_at, found in ((tile, early), (tile + mid, late)):
+                    swapped[half_at, rec : rec + group] = found[:, columns].reshape(
+                        group, slots, LANES
+                    )
+        for tile in range(wide):
+            for slot in range(0, slots, 16):
+                ready[chunk, tile, slot : slot + 16] = jnp.swapaxes(
+                    swapped[tile, :, slot : slot + 16], 0, 1
+                )
+            copy = pltpu.make_async_copy(
+                ready.at[chunk, tile],
+                out.at[:, pl.ds(chunk * recs, recs), pl.ds(tile * LANES, LANES)],
+                out_sem.at[chunk, tile],
             )
-            swapped[rec : rec + group, :, half:] = (
-                (even - odd).astype(bf16).reshape(group, slots, half)
-            )
-        for slot in range(0, slots, 16):
-            for tile in range(wide):
-                at = slice(tile * LANES, (tile + 1) * LANES)
-                ready[chunk, slot : slot + 16, :, at] = jnp.swapaxes(
-                    swapped[:, slot : slot + 16, at], 0, 1
-                )
-        copy = pltpu.make_async_copy(
-            ready.at[chunk], out.at[:, pl.ds(chunk * recs, recs)], out_sem.at[chunk]
-        )
-        copy.start()
-        out_copies.append(copy)
+            copy.start()
+            out_copies.append(copy)
     for copy in out_copies:
         copy.wait()
 
@@ -218,13 +236,13 @@
             pltpu.VMEM(forward.shape, bf16),
             pltpu.VMEM(inverse.shape, bf16),
             pltpu.VMEM(((total + window) // LANES, rec_rows, LANES), bf16),
-            pltpu.VMEM((2, RECS, shots, half), bf16),
-            pltpu.VMEM((2, RECS * shots, half), bf16),
-            pltpu.VMEM((2, RECS * slots, half), bf16),
-            pltpu.VMEM((RECS, slots, window), bf16),
-            pltpu.VMEM((chunks, slots, RECS, window), bf16),
+            pltpu.VMEM((2, half // LANES, RECS, shots, LANES), bf16),
+            pltpu.VMEM((2, half // LANES, RECS * shots, LANES), bf16),
+            pltpu.VMEM((2, half // LANES, RECS * slots, LANES), bf16),
+            pltpu.VMEM((window // LANES, RECS, slots, LANES), bf16),
+            pltpu.VMEM((chunks, window // LANES, slots, RECS, LANES), bf16),
             pltpu.SemaphoreType.DMA((2,)),
-            pltpu.SemaphoreType.DMA((chunks,)),
+            pltpu.SemaphoreType.DMA((chunks, window // LANES)),
         ],
         compiler_params=pltpu.CompilerParams(vmem_limit_bytes=60 << 20),
         cost_estimate=pl.CostEstimate(

time: 33.1 us -> 33.2 us (level)
  no operation moved by 1% of the time
where the time goes in v6:
time: 33.2 us; the launch traced here: 32.9 us
  Pallas kernels  15.4 us (46%)
  starting transfers between devices  9.81 us (30%)
  waiting for transfers between devices  2.9 us (9%)
  matrix products  1.98 us (6%)
  local copies, waits for them, and re-layouts  1.46 us (4%)
  other arithmetic  1.36 us (4%)
    pallas_call x1, Pallas kernels, filter_gathers(): pl.pallas_call(functools.partial(gather_kernel, peers), out_shape=jax.Sha...  15.4 us
    all_to_all x1, starting transfers between devices, on_device(): lax.all_to_all(codes, 'line', split_axis=0, concat_axis=0, tiled=True)  5.35 us
    ppermute x3, starting transfers between devices, on_device(): lax.ppermute(station_traces, 'tm', [(partner(index, away, peers), index)...  4.46 us
    all_to_all x1, waiting for transfers between devices, on_device(): lax.all_to_all(codes, 'line', split_axis=0, concat_axis=0, tiled=True)  2.89 us
    dot_general x1, matrix products, on_device(): jnp.dot(spectral_keep_flags.astype(jnp.bfloat16), order, preferred_elemen...  1.98 us
    unnamed x8, local copies, waits for them, and re-layouts  0.86 us
    concatenate x1, other arithmetic, on_device(): codes = jnp.concatenate([shot_onset_ticks, span_place_index])  0.75 us
  transfers between devices with their start and end apart: 4, of which 1 were waited for; matrix products, arithmetic and copies ran while one was open for 12% of the time, Pallas kernels for 0%

profile of v6, /device:TPU:0, one launch (start us, length us, event | category | flops | bytes accessed | tf_op | source)
XLA Modules:
  0.0 32.9 jit_solution(4726119918238317962)
XLA Ops:
  0.0 3.0 %collective-permute-start.1 = (bf16[32,4096]{1,0:T(8,128)(2,1)}, bf16[32,4096]{1,0:T(8,128)(2,1)S(1)}, u32[]{:S(2)}, u32[]{:S(2)}) collective-permute-start(bf16[32,4096]{1,0:T(8,128)(2,1)} %refs_2_.1), channel_id=1, source_target_pairs={{16,0},{24,8},{0,16},{8,24},{17,1},{25,9},{1,17},{9,25},{18,2},{26... | collective-permute-start | bytes 786440 | tf_op jit(solution)/shard_map/ppermute | solution.py:262
  3.0 1.5 %collective-permute-start = (bf16[32,4096]{1,0:T(8,128)(2,1)}, bf16[32,4096]{1,0:T(8,128)(2,1)S(1)}, u32[]{:S(2)}, u32[]{:S(2)}) collective-permute-start(bf16[32,4096]{1,0:T(8,128)(2,1)} %refs_2_.1), channel_id=1, source_target_pairs={{8,0},{0,8},{24,16},{16,24},{9,1},{1,9},{25,17},{17,25},{10,2},{2,... | collective-permute-start | bytes 786440 | tf_op jit(solution)/shard_map/ppermute | solution.py:262
  4.5 0.0 collective-permute-start.2
  4.5 0.7 %pad_add_fusion = s32[16]{0:T(128)S(1)} fusion(s32[8]{0:T(128)} %param.11, s32[8]{0:T(128)} %param.10), kind=kLoop, calls=%fused_computation.2 | loop fusion | flops 16 | bytes 128 | tf_op jit(solution)/shard_map/concatenate | solution.py:269
  5.2 0.6 %broadcast_in_dim.2 = s32[8,1,16]{2,1,0:T(1,128)} broadcast(s32[16]{0:T(128)S(1)} %pad_add_fusion), dimensions={2} | broadcast | bytes 576 | tf_op jit(solution)/shard_map/broadcast_in_dim | solution.py:270
  5.8 5.4 %all-to-all-start = ((s32[8,1,16]{2,1,0:T(1,128)}), s32[8,1,16]{2,1,0:T(1,128)S(1)}, u32[]{:S(2)}, u32[]{:S(2)}) async-start(s32[8,1,16]{2,1,0:T(1,128)} %broadcast_in_dim.2), calls=%async_computation | async-start | bytes 8192 | tf_op jit(solution)/shard_map/all_to_all | solution.py:271
  11.2 2.0 %convolution_bitcast_fusion.refs_6_ = f32[64,512]{1,0:T(8,128)} fusion(bf16[512,512]{1,0:T(8,128)(2,1)} %constant.17.clone, s32[64,512]{1,0:T(8,128)} %param.12), kind=kOutput, calls=%fused_computation | convolution fusion | flops 33587200 | bytes 786432 | tf_op jit(solution)/shard_map/dot_general | solution.py:273
  13.1 0.6 %pad_add_fusion.1.refs_1_ = s32[2]{0:T(128)} fusion(s32[1]{0:T(128)} %constant.16.clone.1, s32[1]{0:T(128)} %bitcast.1), kind=kLoop, calls=%fused_computation.3 | loop fusion | flops 2 | bytes 16 | tf_op jit(solution)/shard_map/stack | solution.py:272
  13.7 2.9 %all-to-all-done = s32[8,1,16]{2,1,0:T(1,128)S(1)} async-done(((s32[8,1,16]{2,1,0:T(1,128)}), s32[8,1,16]{2,1,0:T(1,128)S(1)}, u32[]{:S(2)}, u32[]{:S(2)}) %all-to-all-start) | async-done | bytes 544 | tf_op jit(solution)/shard_map/all_to_all | solution.py:271
  16.6 0.0 copy-start
  16.6 0.0 collective-permute-done.1.refs_4_
  16.6 0.0 copy-start.1
  16.7 0.0 collective-permute-done.refs_3_
  16.7 0.0 copy-start.2
  16.7 0.0 collective-permute-done.2.refs_5_
  16.7 0.0 copy-start.3
  16.7 0.5 %copy-done = s32[8,1,16]{2,1,0:T(1,128)} copy-done((s32[8,1,16]{2,1,0:T(1,128)}, s32[8,1,16]{2,1,0:T(1,128)S(1)}, u32[]{:S(2)}) %copy-start) | copy-done | bytes 536
  17.2 0.1 copy-done.1
  17.4 0.1 copy-done.2
  17.5 0.1 copy-done.3
  17.5 15.4 %shard_map.91 = bf16[32,32,1024]{2,1,0:T(8,128)(2,1)} custom-call(s32[8,16]{1,0:T(8,128)} %bitcast.5, s32[2]{0:T(128)} %pad_add_fusion.1.refs_1_, bf16[32,4096]{1,0:T(8,128)(2,1)} %refs_2_.1, bf16[32,4096]{1,0:T(8,128)(2,1)} %copy-done.2, bf16[32,4096]{1,0:T(8,128)(2,1)} %copy-done.1, bf16[32,4096]{1,0:T(8,128)(2,1)} %copy-done.3, ...), custom_call_target="tpu_custom_call" | custom-call | flops 4026531840 | bytes 3145728 | tf_op jit(solution)/shard_map/pallas_call | solution.py:230
Async XLA Ops:
  0.0 16.6 %collective-permute-start.1 = (bf16[32,4096]{1,0:T(8,128)(2,1)}, bf16[32,4096]{1,0:T(8,128)(2,1)S(1)}, u32[]{:S(2)}, u32[]{:S(2)}) collective-permute-start(bf16[32,4096]{1,0:T(8,128)(2,1)} %refs_2_.1), channel_id=1, source_target_pairs={{16,0},{24,8},{0,16},{8,24},{17,1},{25,9},{1,17},{9,25},{18,2},{26... | collective-permute-start | bytes 786440 | tf_op jit(solution)/shard_map/ppermute | solution.py:262
  3.0 13.7 %collective-permute-start = (bf16[32,4096]{1,0:T(8,128)(2,1)}, bf16[32,4096]{1,0:T(8,128)(2,1)S(1)}, u32[]{:S(2)}, u32[]{:S(2)}) collective-permute-start(bf16[32,4096]{1,0:T(8,128)(2,1)} %refs_2_.1), channel_id=1, source_target_pairs={{8,0},{0,8},{24,16},{16,24},{9,1},{1,9},{25,17},{17,25},{10,2},{2,... | collective-permute-start | bytes 786440 | tf_op jit(solution)/shard_map/ppermute | solution.py:262
  4.5 12.2 %collective-permute-start.2 = (bf16[32,4096]{1,0:T(8,128)(2,1)}, bf16[32,4096]{1,0:T(8,128)(2,1)S(1)}, u32[]{:S(2)}, u32[]{:S(2)}) collective-permute-start(bf16[32,4096]{1,0:T(8,128)(2,1)} %refs_2_.1), channel_id=1, source_target_pairs={{24,0},{16,8},{8,16},{0,24},{25,1},{17,9},{9,17},{1,25},{26,2},{18... | collective-permute-start | bytes 786440 | tf_op jit(solution)/shard_map/ppermute | solution.py:262
  5.8 10.8 %all-to-all-start = ((s32[8,1,16]{2,1,0:T(1,128)}), s32[8,1,16]{2,1,0:T(1,128)S(1)}, u32[]{:S(2)}, u32[]{:S(2)}) async-start(s32[8,1,16]{2,1,0:T(1,128)} %broadcast_in_dim.2), calls=%async_computation | async-start | bytes 8192 | tf_op jit(solution)/shard_map/all_to_all | solution.py:271
  16.6 0.6 %copy-start = (s32[8,1,16]{2,1,0:T(1,128)}, s32[8,1,16]{2,1,0:T(1,128)S(1)}, u32[]{:S(2)}) copy-start(s32[8,1,16]{2,1,0:T(1,128)S(1)} %all-to-all-done) | copy-start | bytes 1540
  16.6 0.7 %copy-start.1 = (bf16[32,4096]{1,0:T(8,128)(2,1)}, bf16[32,4096]{1,0:T(8,128)(2,1)S(1)}, u32[]{:S(2)}) copy-start(bf16[32,4096]{1,0:T(8,128)(2,1)S(1)} %collective-permute-done.1.refs_4_) | copy-start | bytes 786436
  16.7 0.8 %copy-start.2 = (bf16[32,4096]{1,0:T(8,128)(2,1)}, bf16[32,4096]{1,0:T(8,128)(2,1)S(1)}, u32[]{:S(2)}) copy-start(bf16[32,4096]{1,0:T(8,128)(2,1)S(1)} %collective-permute-done.refs_3_) | copy-start | bytes 786436
  16.7 0.9 %copy-start.3 = (bf16[32,4096]{1,0:T(8,128)(2,1)}, bf16[32,4096]{1,0:T(8,128)(2,1)S(1)}, u32[]{:S(2)}) copy-start(bf16[32,4096]{1,0:T(8,128)(2,1)S(1)} %collective-permute-done.2.refs_5_) | copy-start | bytes 786436

commit v7 on v6

--- a/solution.py
+++ b/solution.py
@@ -66,7 +66,7 @@
     traces, refs = refs[:peers], refs[peers:]
     keep, over_shots, back_rows = refs[:3]
     table_refs, out = refs[3:5], refs[5]
-    forward, inverse, tiles, folds, spectra, mixed, swapped, ready, table_sem, out_sem = refs[6:]
+    forward, inverse, tiles, folds, spectra, waved, mixed, swapped, ready, table_sem, out_sem = refs[6:]
     rec_rows, block_len = traces[0].shape
     shots, half = keep.shape
     window = 2 * half
@@ -165,6 +165,12 @@
             masked = jnp.concatenate(
                 [waves[:shots] * keep[...], waves[shots:] * keep[...]], axis=0
             ).astype(bf16)
+            at = slice(2 * rec * shots, 2 * (rec + 1) * shots)
+            for tile in range(mid):
+                waved[tile, at] = masked[:, tile * LANES : (tile + 1) * LANES]
+        for rec in range(recs):
+            at = slice(2 * rec * shots, 2 * (rec + 1) * shots)
+            masked = jnp.concatenate([waved[tile, at] for tile in range(mid)], axis=1)
             again = jnp.dot(back, masked, preferred_element_type=f32).astype(bf16)
             at = slice(rec * slots, (rec + 1) * slots)
             for part in range(2):
@@ -238,6 +244,7 @@
             pltpu.VMEM(((total + window) // LANES, rec_rows, LANES), bf16),
             pltpu.VMEM((2, half // LANES, RECS, shots, LANES), bf16),
             pltpu.VMEM((2, half // LANES, RECS * shots, LANES), bf16),
+            pltpu.VMEM((half // LANES, 2 * RECS * shots, LANES), bf16),
             pltpu.VMEM((2, half // LANES, RECS * slots, LANES), bf16),
             pltpu.VMEM((window // LANES, RECS, slots, LANES), bf16),
             pltpu.VMEM((chunks, window // LANES, slots, RECS, LANES), bf16),

time: 33.2 us -> 29 us (0.87)
  Pallas kernels: 15.4 us -> 11.2 us
    pallas_call x1, Pallas kernels: 15.4 us -> 11.2 us  [filter_gathers(): pl.pallas_call(functools.partial(gather_kernel, peers), out_shape=jax.Sha...]
  transfers between devices with their start and end apart: 4 -> 4, of which waited for: 1 -> 1; matrix products, arithmetic and copies ran while one was open for 12% -> 14% of each run, Pallas kernels for 0% -> 0%
where the time goes in v7:
time: 29 us; the launch traced here: 28.8 us
  Pallas kernels  11.2 us (39%)
  starting transfers between devices  9.81 us (34%)
  waiting for transfers between devices  2.9 us (10%)
  matrix products  1.98 us (7%)
  local copies, waits for them, and re-layouts  1.46 us (5%)
  other arithmetic  1.36 us (5%)
    pallas_call x1, Pallas kernels, filter_gathers(): pl.pallas_call(functools.partial(gather_kernel, peers), out_shape=jax.Sha...  11.2 us
    all_to_all x1, starting transfers between devices, on_device(): lax.all_to_all(codes, 'line', split_axis=0, concat_axis=0, tiled=True)  5.35 us
    ppermute x3, starting transfers between devices, on_device(): lax.ppermute(station_traces, 'tm', [(partner(index, away, peers), index)...  4.46 us
    all_to_all x1, waiting for transfers between devices, on_device(): lax.all_to_all(codes, 'line', split_axis=0, concat_axis=0, tiled=True)  2.89 us
    dot_general x1, matrix products, on_device(): jnp.dot(spectral_keep_flags.astype(jnp.bfloat16), order, preferred_elemen...  1.98 us
    unnamed x8, local copies, waits for them, and re-layouts  0.86 us
    concatenate x1, other arithmetic, on_device(): codes = jnp.concatenate([shot_onset_ticks, span_place_index])  0.75 us
    another operation x1, other arithmetic, on_device(): jnp.stack([lax.axis_index('tm'), station_traces.shape[1]]).astype(jnp.int32)  0.61 us
  transfers between devices with their start and end apart: 4, of which 1 were waited for; matrix products, arithmetic and copies ran while one was open for 14% of the time, Pallas kernels for 0%

profile of v7, /device:TPU:0, one launch (start us, length us, event | category | flops | bytes accessed | tf_op | source)
XLA Modules:
  0.0 28.8 jit_solution(16488288073551691106)
XLA Ops:
  0.0 3.0 %collective-permute-start.1 = (bf16[32,4096]{1,0:T(8,128)(2,1)}, bf16[32,4096]{1,0:T(8,128)(2,1)S(1)}, u32[]{:S(2)}, u32[]{:S(2)}) collective-permute-start(bf16[32,4096]{1,0:T(8,128)(2,1)} %refs_2_.1), channel_id=1, source_target_pairs={{16,0},{24,8},{0,16},{8,24},{17,1},{25,9},{1,17},{9,25},{18,2},{26... | collective-permute-start | bytes 786440 | tf_op jit(solution)/shard_map/ppermute | solution.py:269
  3.0 1.5 %collective-permute-start = (bf16[32,4096]{1,0:T(8,128)(2,1)}, bf16[32,4096]{1,0:T(8,128)(2,1)S(1)}, u32[]{:S(2)}, u32[]{:S(2)}) collective-permute-start(bf16[32,4096]{1,0:T(8,128)(2,1)} %refs_2_.1), channel_id=1, source_target_pairs={{8,0},{0,8},{24,16},{16,24},{9,1},{1,9},{25,17},{17,25},{10,2},{2,... | collective-permute-start | bytes 786440 | tf_op jit(solution)/shard_map/ppermute | solution.py:269
  4.5 0.0 collective-permute-start.2
  4.5 0.7 %pad_add_fusion = s32[16]{0:T(128)S(1)} fusion(s32[8]{0:T(128)} %param.11, s32[8]{0:T(128)} %param.10), kind=kLoop, calls=%fused_computation.2 | loop fusion | flops 16 | bytes 128 | tf_op jit(solution)/shard_map/concatenate | solution.py:276
  5.2 0.6 %broadcast_in_dim.2 = s32[8,1,16]{2,1,0:T(1,128)} broadcast(s32[16]{0:T(128)S(1)} %pad_add_fusion), dimensions={2} | broadcast | bytes 576 | tf_op jit(solution)/shard_map/broadcast_in_dim | solution.py:277
  5.8 5.4 %all-to-all-start = ((s32[8,1,16]{2,1,0:T(1,128)}), s32[8,1,16]{2,1,0:T(1,128)S(1)}, u32[]{:S(2)}, u32[]{:S(2)}) async-start(s32[8,1,16]{2,1,0:T(1,128)} %broadcast_in_dim.2), calls=%async_computation | async-start | bytes 8192 | tf_op jit(solution)/shard_map/all_to_all | solution.py:278
  11.2 2.0 %convolution_bitcast_fusion.refs_6_ = f32[64,512]{1,0:T(8,128)} fusion(bf16[512,512]{1,0:T(8,128)(2,1)} %constant.17.clone, s32[64,512]{1,0:T(8,128)} %param.12), kind=kOutput, calls=%fused_computation | convolution fusion | flops 33587200 | bytes 786432 | tf_op jit(solution)/shard_map/dot_general | solution.py:280
  13.1 0.6 %pad_add_fusion.1.refs_1_ = s32[2]{0:T(128)} fusion(s32[1]{0:T(128)} %constant.16.clone.1, s32[1]{0:T(128)} %bitcast.1), kind=kLoop, calls=%fused_computation.3 | loop fusion | flops 2 | bytes 16 | tf_op jit(solution)/shard_map/stack | solution.py:279
  13.7 2.9 %all-to-all-done = s32[8,1,16]{2,1,0:T(1,128)S(1)} async-done(((s32[8,1,16]{2,1,0:T(1,128)}), s32[8,1,16]{2,1,0:T(1,128)S(1)}, u32[]{:S(2)}, u32[]{:S(2)}) %all-to-all-start) | async-done | bytes 544 | tf_op jit(solution)/shard_map/all_to_all | solution.py:278
  16.6 0.0 copy-start
  16.6 0.0 collective-permute-done.1.refs_4_
  16.6 0.0 copy-start.1
  16.7 0.0 collective-permute-done.refs_3_
  16.7 0.0 copy-start.2
  16.7 0.0 collective-permute-done.2.refs_5_
  16.7 0.0 copy-start.3
  16.7 0.5 %copy-done = s32[8,1,16]{2,1,0:T(1,128)} copy-done((s32[8,1,16]{2,1,0:T(1,128)}, s32[8,1,16]{2,1,0:T(1,128)S(1)}, u32[]{:S(2)}) %copy-start) | copy-done | bytes 536
  17.2 0.1 copy-done.1
  17.4 0.1 copy-done.2
  17.5 0.1 copy-done.3
  17.5 11.2 %shard_map.91 = bf16[32,32,1024]{2,1,0:T(8,128)(2,1)} custom-call(s32[8,16]{1,0:T(8,128)} %bitcast.5, s32[2]{0:T(128)} %pad_add_fusion.1.refs_1_, bf16[32,4096]{1,0:T(8,128)(2,1)} %refs_2_.1, bf16[32,4096]{1,0:T(8,128)(2,1)} %copy-done.2, bf16[32,4096]{1,0:T(8,128)(2,1)} %copy-done.1, bf16[32,4096]{1,0:T(8,128)(2,1)} %copy-done.3, ...), custom_call_target="tpu_custom_call" | custom-call | flops 4026531840 | bytes 3145728 | tf_op jit(solution)/shard_map/pallas_call | solution.py:236
Async XLA Ops:
  0.0 16.6 %collective-permute-start.1 = (bf16[32,4096]{1,0:T(8,128)(2,1)}, bf16[32,4096]{1,0:T(8,128)(2,1)S(1)}, u32[]{:S(2)}, u32[]{:S(2)}) collective-permute-start(bf16[32,4096]{1,0:T(8,128)(2,1)} %refs_2_.1), channel_id=1, source_target_pairs={{16,0},{24,8},{0,16},{8,24},{17,1},{25,9},{1,17},{9,25},{18,2},{26... | collective-permute-start | bytes 786440 | tf_op jit(solution)/shard_map/ppermute | solution.py:269
  3.0 13.7 %collective-permute-start = (bf16[32,4096]{1,0:T(8,128)(2,1)}, bf16[32,4096]{1,0:T(8,128)(2,1)S(1)}, u32[]{:S(2)}, u32[]{:S(2)}) collective-permute-start(bf16[32,4096]{1,0:T(8,128)(2,1)} %refs_2_.1), channel_id=1, source_target_pairs={{8,0},{0,8},{24,16},{16,24},{9,1},{1,9},{25,17},{17,25},{10,2},{2,... | collective-permute-start | bytes 786440 | tf_op jit(solution)/shard_map/ppermute | solution.py:269
  4.5 12.2 %collective-permute-start.2 = (bf16[32,4096]{1,0:T(8,128)(2,1)}, bf16[32,4096]{1,0:T(8,128)(2,1)S(1)}, u32[]{:S(2)}, u32[]{:S(2)}) collective-permute-start(bf16[32,4096]{1,0:T(8,128)(2,1)} %refs_2_.1), channel_id=1, source_target_pairs={{24,0},{16,8},{8,16},{0,24},{25,1},{17,9},{9,17},{1,25},{26,2},{18... | collective-permute-start | bytes 786440 | tf_op jit(solution)/shard_map/ppermute | solution.py:269
  5.8 10.8 %all-to-all-start = ((s32[8,1,16]{2,1,0:T(1,128)}), s32[8,1,16]{2,1,0:T(1,128)S(1)}, u32[]{:S(2)}, u32[]{:S(2)}) async-start(s32[8,1,16]{2,1,0:T(1,128)} %broadcast_in_dim.2), calls=%async_computation | async-start | bytes 8192 | tf_op jit(solution)/shard_map/all_to_all | solution.py:278
  16.6 0.6 %copy-start = (s32[8,1,16]{2,1,0:T(1,128)}, s32[8,1,16]{2,1,0:T(1,128)S(1)}, u32[]{:S(2)}) copy-start(s32[8,1,16]{2,1,0:T(1,128)S(1)} %all-to-all-done) | copy-start | bytes 1540
  16.6 0.7 %copy-start.1 = (bf16[32,4096]{1,0:T(8,128)(2,1)}, bf16[32,4096]{1,0:T(8,128)(2,1)S(1)}, u32[]{:S(2)}) copy-start(bf16[32,4096]{1,0:T(8,128)(2,1)S(1)} %collective-permute-done.1.refs_4_) | copy-start | bytes 786436
  16.7 0.8 %copy-start.2 = (bf16[32,4096]{1,0:T(8,128)(2,1)}, bf16[32,4096]{1,0:T(8,128)(2,1)S(1)}, u32[]{:S(2)}) copy-start(bf16[32,4096]{1,0:T(8,128)(2,1)S(1)} %collective-permute-done.refs_3_) | copy-start | bytes 786436
  16.7 0.9 %copy-start.3 = (bf16[32,4096]{1,0:T(8,128)(2,1)}, bf16[32,4096]{1,0:T(8,128)(2,1)S(1)}, u32[]{:S(2)}) copy-start(bf16[32,4096]{1,0:T(8,128)(2,1)S(1)} %collective-permute-done.2.refs_5_) | copy-start | bytes 786436

commit v8 on v5

v8 whole, which is shorter than its diff:
```python
import functools
import math

import jax
import jax.numpy as jnp
import ml_dtypes
import numpy as np
from jax import lax
from jax.experimental import pallas as pl
from jax.experimental.pallas import tpu as pltpu
from jax.sharding import PartitionSpec as P

LANES = 128
RECS = 16


def make_tables(window, shots):
    half = window // 2
    quarter = half // 2
    times = np.arange(half)
    freqs = np.concatenate([np.arange(0, half, 2), np.arange(1, half, 2)])

    def waves(rows, columns, period):
        phase = (rows[:, None] * columns[None, :] % period) * (2.0 * math.pi / period)
        return np.cos(phase), np.sin(phase)

    bf16 = ml_dtypes.bfloat16
    cosine, sine = waves(times, freqs, window)
    forward = np.stack(
        [
            np.concatenate([cosine[:, cut], -sine[:, cut]], axis=1)
            for cut in (slice(0, quarter), slice(quarter, half))
        ]
    ).astype(bf16)
    gain = np.where(freqs == 0, 0.5, 1.0)[:, None] * (2.0 / (window * shots))
    inverse = np.stack(
        [
            np.concatenate([gain[cut] * cosine.T[cut], -gain[cut] * sine.T[cut]], axis=0)
            for cut in (slice(0, quarter), slice(quarter, half))
        ]
    ).astype(bf16)
    turn_cos, turn_sin = waves(np.arange(shots), np.arange(shots), shots)
    forward, inverse = [
        table.reshape(2, half, half // LANES, LANES).swapaxes(1, 2) for table in (forward, inverse)
    ]
    over_shots = np.block([[turn_cos, turn_sin], [-turn_sin, turn_cos]]).astype(bf16)
    back_rows = np.stack(
        [
            np.concatenate([turn_cos, -turn_sin], axis=1),
            np.concatenate([turn_sin, turn_cos], axis=1),
        ]
    ).astype(bf16)
    order = np.zeros((half, half), bf16)
    order[freqs, np.arange(half)] = 1
    return forward, inverse, over_shots, back_rows, order


def partner(index, away, count):
    if count & (count - 1) == 0:
        return index ^ away
    return (index + away) % count


def plan_kernel(codes, here, flags, order, back_rows, keep, back):
    shots = flags.shape[0]
    slots = back.shape[0] // 2
    share = codes.shape[1] // 2
    f32, bf16 = jnp.float32, jnp.bfloat16
    keep[...] = jnp.dot(flags[...].astype(f32).astype(bf16), order[...], preferred_element_type=f32)
    start = here[0] * here[1]
    shot_lane = lax.broadcasted_iota(jnp.int32, (1, shots), 1)
    place_all = jnp.full((1, shots), -1, jnp.int32)
    for shot in range(shots):
        line, item = divmod(shot, share)
        tick = codes[line, item]
        mine = (tick >= start) & (tick < start + here[1])
        place = jnp.where(mine, codes[line, share + item], -1)
        place_all = jnp.where(shot_lane == shot, place, place_all)
    slot_row = lax.broadcasted_iota(jnp.int32, (slots, shots), 0)
    owned = (slot_row == place_all).astype(f32).astype(bf16)
    for part in range(2):
        back[part * slots : (part + 1) * slots] = jnp.dot(
            owned, back_rows[part], preferred_element_type=f32
        ).astype(bf16)


def plan_shots(codes, here, flags, order, back_rows, slots):
    shots, half = flags.shape
    smem = pl.BlockSpec(memory_space=pltpu.SMEM)
    vmem = pl.BlockSpec(memory_space=pltpu.VMEM)
    return pl.pallas_call(
        plan_kernel,
        out_shape=[
            jax.ShapeDtypeStruct((shots, half), jnp.float32),
            jax.ShapeDtypeStruct((2 * slots, 2 * shots), jnp.bfloat16),
        ],
        in_specs=[smem, smem, vmem, vmem, vmem],
        out_specs=[vmem, vmem],
        compiler_params=pltpu.CompilerParams(vmem_limit_bytes=60 << 20),
        cost_estimate=pl.CostEstimate(flops=0, bytes_accessed=8 << 20, transcendentals=0),
    )(codes, here, flags, order, back_rows)


def gather_kernel(peers, chunk, *refs):
    codes, here, *refs = refs
    traces, refs = refs[:peers], refs[peers:]
    keep, over_shots, back = refs[:3]
    table_refs, refs = refs[3:5], refs[5 + (chunk > 0) :]
    out, forward, inverse, tiles, folds, spectra, waved, mixed, swapped, ready = refs[:10]
    table_sem, out_sem = refs[10:]
    recs, block_len = traces[0].shape
    shots, half = keep.shape
    window = 2 * half
    slots = ready.shape[1]
    share = codes.shape[1] // 2
    wide = window // LANES
    mid = wide // 2
    arms = mid // 2
    per_block = block_len // LANES
    f32, bf16 = jnp.float32, jnp.bfloat16

    table_copies = [
        pltpu.make_async_copy(table, place, table_sem.at[index])
        for index, (table, place) in enumerate(zip(table_refs, (forward, inverse)))
    ]
    for copy in table_copies:
        copy.start()

    for away, block in enumerate(traces):
        base = partner(here[0], away, peers) * per_block
        for tile in range(per_block):
            tiles[base + tile] = block[:, tile * LANES : (tile + 1) * LANES]
    for tile in range(wide):
        tiles[peers * per_block + tile] = jnp.zeros((recs, LANES), bf16)

    lane = lax.broadcasted_iota(jnp.int16, (recs, LANES), 1)

    def cut(shot):
        tick = codes[shot // share, shot % share]
        first = lax.shift_right_logical(tick, LANES.bit_length() - 1)
        within = tick & (LANES - 1)
        piece = [tiles[first + tile] for tile in range(wide + 1)]
        early = lane < within.astype(jnp.int16)
        piece = [jnp.where(early, piece[tile + 1], piece[tile]) for tile in range(wide)]
        turn = (LANES - within) & (LANES - 1)
        sums = [pltpu.roll(piece[tile] + piece[tile + mid], turn, 1) for tile in range(mid)]
        gaps = [pltpu.roll(piece[tile] - piece[tile + mid], turn, 1) for tile in range(mid)]
        return sums, gaps

    def product(left, right, part):
        return jnp.dot(
            left,
            jnp.concatenate([right[part, tile] for tile in range(mid)], axis=1),
            preferred_element_type=f32,
        )

    out_copies = []
    for first in range(0, shots, 16):
        cuts = [cut(shot) for shot in range(first, first + 16)]
        for part in range(2):
            for tile in range(mid):
                panel = jnp.stack([cuts[item][part][tile] for item in range(16)])
                folds[part, tile, :, first : first + 16] = jnp.swapaxes(panel, 0, 1)
    table_copies[0].wait()
    group = 8
    for rec in range(0, recs, group):
        for part in range(2):
            panel = [
                folds[part, tile, rec : rec + group].reshape(group * shots, LANES)
                for tile in range(mid)
            ]
            found = product(jnp.concatenate(panel, axis=1), forward, part).astype(bf16)
            for tile in range(mid):
                spectra[part, tile, rec * shots : (rec + group) * shots] = found[
                    :, tile * LANES : (tile + 1) * LANES
                ]
    for rec in range(recs):
        at = slice(rec * shots, (rec + 1) * shots)
        real, imag = [
            jnp.concatenate(
                [spectra[part, tile, at] for part in range(2) for tile in tiles_of], axis=1
            )
            for tiles_of in (range(arms), range(arms, mid))
        ]
        stacked = jnp.concatenate([real, imag], axis=0)
        waves = jnp.dot(over_shots[...], stacked, preferred_element_type=f32)
        masked = jnp.concatenate(
            [waves[:shots] * keep[...], waves[shots:] * keep[...]], axis=0
        ).astype(bf16)
        at = slice(2 * rec * shots, 2 * (rec + 1) * shots)
        for tile in range(mid):
            waved[tile, at] = masked[:, tile * LANES : (tile + 1) * LANES]
    for rec in range(recs):
        at = slice(2 * rec * shots, 2 * (rec + 1) * shots)
        masked = jnp.concatenate([waved[tile, at] for tile in range(mid)], axis=1)
        again = jnp.dot(back[...], masked, preferred_element_type=f32).astype(bf16)
        at = slice(rec * slots, (rec + 1) * slots)
        for part in range(2):
            for arm in range(arms):
                tile = part * arms + arm
                columns = slice(tile * LANES, (tile + 1) * LANES)
                mixed[part, arm, at] = again[:slots, columns]
                mixed[part, arms + arm, at] = again[slots:, columns]
    table_copies[1].wait()
    for rec in range(0, recs, group):
        at = slice(rec * slots, (rec + group) * slots)
        even, odd = [
            product(
                jnp.concatenate([mixed[part, tile, at] for tile in range(mid)], axis=1),
                inverse,
                part,
            )
            for part in range(2)
        ]
        early, late = (even + odd).astype(bf16), (even - odd).astype(bf16)
        for tile in range(mid):
            columns = slice(tile * LANES, (tile + 1) * LANES)
            for half_at, found in ((tile, early), (tile + mid, late)):
                swapped[half_at, rec : rec + group] = found[:, columns].reshape(
                    group, slots, LANES
                )
    for tile in range(wide):
        for slot in range(0, slots, 16):
            ready[tile, slot : slot + 16] = jnp.swapaxes(
                swapped[tile, :, slot : slot + 16], 0, 1
            )
        copy = pltpu.make_async_copy(
            ready.at[tile],
            out.at[:, pl.ds(chunk * recs, recs), pl.ds(tile * LANES, LANES)],
            out_sem.at[tile],
        )
        copy.start()
        out_copies.append(copy)
    for copy in out_copies:
        copy.wait()


def filter_gathers(codes, here, traces, tables, chunk, chunks, filled):
    keep, over_shots, back, forward, inverse = tables
    peers = len(traces)
    recs, block_len = traces[0].shape
    rec_rows = recs * chunks
    shots, half = keep.shape
    window = 2 * half
    slots = 2 * shots // peers
    total = peers * block_len
    smem = pl.BlockSpec(memory_space=pltpu.SMEM)
    vmem = pl.BlockSpec(memory_space=pltpu.VMEM)
    anywhere = pl.BlockSpec(memory_space=pl.ANY)
    bf16 = jnp.bfloat16
    operands = [codes, here, *traces, keep, over_shots, back, forward, inverse]
    aliases = {}
    if chunk:
        aliases = {len(operands): 0}
        operands.append(filled)
    return pl.pallas_call(
        functools.partial(gather_kernel, peers, chunk),
        out_shape=jax.ShapeDtypeStruct((slots, rec_rows, window), bf16),
        in_specs=[smem, smem] + [vmem] * (peers + 3) + [anywhere] * (2 + (chunk > 0)),
        out_specs=anywhere,
        scratch_shapes=[
            pltpu.VMEM(forward.shape, bf16),
            pltpu.VMEM(inverse.shape, bf16),
            pltpu.VMEM(((total + window) // LANES, recs, LANES), bf16),
            pltpu.VMEM((2, half // LANES, recs, shots, LANES), bf16),
            pltpu.VMEM((2, half // LANES, recs * shots, LANES), bf16),
            pltpu.VMEM((half // LANES, 2 * recs * shots, LANES), bf16),
            pltpu.VMEM((2, half // LANES, recs * slots, LANES), bf16),
            pltpu.VMEM((window // LANES, recs, slots, LANES), bf16),
            pltpu.VMEM((window // LANES, slots, recs, LANES), bf16),
            pltpu.SemaphoreType.DMA((2,)),
            pltpu.SemaphoreType.DMA((window // LANES,)),
        ],
        input_output_aliases=aliases,
        compiler_params=pltpu.CompilerParams(vmem_limit_bytes=60 << 20),
        cost_estimate=pl.CostEstimate(flops=0, bytes_accessed=20 << 20, transcendentals=0),
    )(*operands)


def on_device(station_traces, shot_onset_ticks, span_place_index, spectral_keep_flags):
    shots, half = spectral_keep_flags.shape
    forward, inverse, over_shots, back_rows, order = make_tables(2 * half, shots)
    peers = lax.axis_size("tm")
    lines = lax.axis_size("line")
    chunks = station_traces.shape[0] // RECS
    gathered = []
    for chunk in range(chunks):
        part = station_traces[chunk * RECS : (chunk + 1) * RECS]
        gathered.append(
            [part]
            + [
                lax.ppermute(
                    part, "tm", [(partner(index, away, peers), index) for index in range(peers)]
                )
                for away in range(1, peers)
            ]
        )
    codes = jnp.concatenate([shot_onset_ticks, span_place_index])
    codes = jnp.broadcast_to(codes[None], (lines, codes.shape[0]))
    codes = lax.all_to_all(codes, "line", split_axis=0, concat_axis=0, tiled=True)
    here = jnp.stack([lax.axis_index("tm"), station_traces.shape[1]]).astype(jnp.int32)
    keep, back = plan_shots(
        codes, here, spectral_keep_flags, order, back_rows, 2 * shots // peers
    )
    tables = [keep, over_shots, back, forward, inverse]
    filled = None
    for chunk in range(chunks):
        filled = filter_gathers(codes, here, gathered[chunk], tables, chunk, chunks, filled)
    return filled


def solution(mesh):
    in_specs = (P("line", "tm"), P("line"), P("line"), P())
    out_specs = P("tm", "line", None)
    return jax.shard_map(
        on_device, mesh=mesh, in_specs=in_specs, out_specs=out_specs, check_vma=False
    )
```

time: 33.1 us -> 42.4 us (1.28)
  starting transfers between devices: 9.81 us -> 15.2 us
  local copies, waits for them, and re-layouts: 1.46 us -> 4.15 us
  matrix products: 1.98 us -> 0 us
  waiting for transfers between devices: 2.9 us -> 4.85 us
  Pallas kernels: 15.3 us -> 16.4 us
    ppermute x3 -> x6, starting transfers between devices: 4.46 us -> 10.3 us  [on_device(): lax.ppermute(part, 'tm', [(partner(index, away, peers), index) for index...]
    dot_general x1 -> x0, matrix products: 1.98 us -> none  [on_device(): jnp.dot(spectral_keep_flags.astype(jnp.bfloat16), order, preferred_elemen...]
    all_to_all x1, waiting for transfers between devices: 2.89 us -> 4.83 us  [on_device(): lax.all_to_all(codes, 'line', split_axis=0, concat_axis=0, tiled=True)]
    unnamed x8 -> x18, local copies, waits for them, and re-layouts: 0.86 us -> 2.57 us
    pallas_call x1 -> x3, Pallas kernels: 15.3 us -> 16.4 us  [the longest x2 14.5 us: filter_gathers(): pl.pallas_call(functools.partial(gather_kernel, peers, chunk), out_shape=...]
    slice x0 -> x1, local copies, waits for them, and re-layouts: none -> 0.98 us  [on_device(): part = station_traces[chunk * RECS:(chunk + 1) * RECS]]
    all_to_all x1, starting transfers between devices: 5.35 us -> 4.88 us  [on_device(): lax.all_to_all(codes, 'line', split_axis=0, concat_axis=0, tiled=True)]
  transfers between devices with their start and end apart: 4 -> 7, of which waited for: 1 -> 1; matrix products, arithmetic and copies ran while one was open for 12% -> 5% of each run, Pallas kernels for 0% -> 22%
where the time goes in v8:
time: 42.4 us; the launch traced here: 42.1 us
  Pallas kernels  16.4 us (39%)
  starting transfers between devices  15.2 us (36%)
  waiting for transfers between devices  4.85 us (11%)
  local copies, waits for them, and re-layouts  4.15 us (10%)
  other arithmetic  1.4 us (3%)
    pallas_call x2, Pallas kernels, filter_gathers(): pl.pallas_call(functools.partial(gather_kernel, peers, chunk), out_shape=...  14.5 us
    ppermute x6, starting transfers between devices, on_device(): lax.ppermute(part, 'tm', [(partner(index, away, peers), index) for index...  10.3 us
    all_to_all x1, starting transfers between devices, on_device(): lax.all_to_all(codes, 'line', split_axis=0, concat_axis=0, tiled=True)  4.88 us
    all_to_all x1, waiting for transfers between devices, on_device(): lax.all_to_all(codes, 'line', split_axis=0, concat_axis=0, tiled=True)  4.83 us
    unnamed x18, local copies, waits for them, and re-layouts  2.57 us
    pallas_call x1, Pallas kernels, plan_shots(): pl.pallas_call(plan_kernel, out_shape=[jax.ShapeDtypeStruct((shots, half)...  1.94 us
    slice x1, local copies, waits for them, and re-layouts, on_device(): part = station_traces[chunk * RECS:(chunk + 1) * RECS]  0.98 us
  transfers between devices with their start and end apart: 7, of which 1 were waited for; matrix products, arithmetic and copies ran while one was open for 5% of the time, Pallas kernels for 22%

profile of v8, /device:TPU:0, one launch (start us, length us, event | category | flops | bytes accessed | tf_op | source)
XLA Modules:
  0.0 42.1 jit_solution(10467327496944000554)
XLA Ops:
  0.0 1.0 %fusion = (bf16[16,4096]{1,0:T(8,128)(2,1)S(1)}, bf16[16,4096]{1,0:T(8,128)(2,1)S(1)}) fusion(bf16[32,4096]{1,0:T(8,128)(2,1)} %param.9), kind=kLoop, calls=%fused_computation.2 | loop fusion | bytes 524288 | tf_op jit(solution)/shard_map/slice | solution.py:288
  1.0 4.0 %collective-permute-start.5 = (bf16[16,4096]{1,0:T(8,128)(2,1)S(1)}, bf16[16,4096]{1,0:T(8,128)(2,1)S(1)}, u32[]{:S(2)}, u32[]{:S(2)}) collective-permute-start(bf16[16,4096]{1,0:T(8,128)(2,1)S(1)} %get-tuple-element.9.refs_2_), channel_id=1, source_target_pairs={{24,0},{16,8},{8,16},{0,24},{25,1},{17,9},{9,17},{1,25},{26,2},{18... | collective-permute-start | bytes 393224 | tf_op jit(solution)/shard_map/ppermute | solution.py:292
  5.0 0.5 %collective-permute-start.4 = (bf16[16,4096]{1,0:T(8,128)(2,1)S(1)}, bf16[16,4096]{1,0:T(8,128)(2,1)S(1)}, u32[]{:S(2)}, u32[]{:S(2)}) collective-permute-start(bf16[16,4096]{1,0:T(8,128)(2,1)S(1)} %get-tuple-element.9.refs_2_), channel_id=1, source_target_pairs={{16,0},{24,8},{0,16},{8,24},{17,1},{25,9},{1,17},{9,25},{18,2},{26... | collective-permute-start | bytes 393224 | tf_op jit(solution)/shard_map/ppermute | solution.py:292
  5.5 0.1 collective-permute-start.3
  5.6 2.8 %collective-permute-start.2 = (bf16[16,4096]{1,0:T(8,128)(2,1)S(1)}, bf16[16,4096]{1,0:T(8,128)(2,1)S(1)}, u32[]{:S(2)}, u32[]{:S(2)}) collective-permute-start(bf16[16,4096]{1,0:T(8,128)(2,1)S(1)} %get-tuple-element.10.refs_2_), channel_id=1, source_target_pairs={{24,0},{16,8},{8,16},{0,24},{25,1},{17,9},{9,17},{1,25},{26,2},{18... | collective-permute-start | bytes 393224 | tf_op jit(solution)/shard_map/ppermute | solution.py:292
  8.5 0.5 %collective-permute-start.1 = (bf16[16,4096]{1,0:T(8,128)(2,1)S(1)}, bf16[16,4096]{1,0:T(8,128)(2,1)S(1)}, u32[]{:S(2)}, u32[]{:S(2)}) collective-permute-start(bf16[16,4096]{1,0:T(8,128)(2,1)S(1)} %get-tuple-element.10.refs_2_), channel_id=1, source_target_pairs={{16,0},{24,8},{0,16},{8,24},{17,1},{25,9},{1,17},{9,25},{18,2},{26... | collective-permute-start | bytes 393224 | tf_op jit(solution)/shard_map/ppermute | solution.py:292
  9.0 0.0 collective-permute-done.5.refs_5_
  9.0 2.3 %collective-permute-start = (bf16[16,4096]{1,0:T(8,128)(2,1)S(1)}, bf16[16,4096]{1,0:T(8,128)(2,1)S(1)}, u32[]{:S(2)}, u32[]{:S(2)}) collective-permute-start(bf16[16,4096]{1,0:T(8,128)(2,1)S(1)} %get-tuple-element.10.refs_2_), channel_id=1, source_target_pairs={{8,0},{0,8},{24,16},{16,24},{9,1},{1,9},{25,17},{17,25},{10,2},{2,... | collective-permute-start | bytes 393224 | tf_op jit(solution)/shard_map/ppermute | solution.py:292
  11.3 0.7 %pad_add_fusion = s32[16]{0:T(128)S(1)} fusion(s32[8]{0:T(128)} %param.11, s32[8]{0:T(128)} %param.10), kind=kLoop, calls=%fused_computation | loop fusion | flops 16 | bytes 128 | tf_op jit(solution)/shard_map/concatenate | solution.py:298
  12.0 0.6 %broadcast_in_dim.2 = s32[8,1,16]{2,1,0:T(1,128)} broadcast(s32[16]{0:T(128)S(1)} %pad_add_fusion), dimensions={2} | broadcast | bytes 576 | tf_op jit(solution)/shard_map/broadcast_in_dim | solution.py:299
  12.6 4.9 %all-to-all-start = ((s32[8,1,16]{2,1,0:T(1,128)}), s32[8,1,16]{2,1,0:T(1,128)S(1)}, u32[]{:S(2)}, u32[]{:S(2)}) async-start(s32[8,1,16]{2,1,0:T(1,128)} %broadcast_in_dim.2), calls=%async_computation | async-start | bytes 8192 | tf_op jit(solution)/shard_map/all_to_all | solution.py:300
  17.5 0.7 %pad_add_fusion.1.here.refs_1_ = s32[2]{0:T(128)} fusion(s32[1]{0:T(128)} %constant.16.clone.1, s32[1]{0:T(128)} %bitcast.1), kind=kLoop, calls=%fused_computation.1 | loop fusion | flops 2 | bytes 16 | tf_op jit(solution)/shard_map/stack | solution.py:301
  18.2 4.8 %all-to-all-done = s32[8,1,16]{2,1,0:T(1,128)S(1)} async-done(((s32[8,1,16]{2,1,0:T(1,128)}), s32[8,1,16]{2,1,0:T(1,128)S(1)}, u32[]{:S(2)}, u32[]{:S(2)}) %all-to-all-start) | async-done | bytes 544 | tf_op jit(solution)/shard_map/all_to_all | solution.py:300
  23.0 0.6 %copy-done.8 = s32[8,1,16]{2,1,0:T(1,128)} copy-done((s32[8,1,16]{2,1,0:T(1,128)}, s32[8,1,16]{2,1,0:T(1,128)S(1)}, u32[]{:S(2)}) %copy-start.8) | copy-done | bytes 536
  23.6 1.9 %shard_map.91 = (f32[64,512]{1,0:T(8,128)}, bf16[64,128]{1,0:T(8,128)(2,1)}) custom-call(s32[8,16]{1,0:T(8,128)} %bitcast.2, s32[2]{0:T(128)} %pad_add_fusion.1.here.refs_1_, s32[64,512]{1,0:T(8,128)} %flags.1, bf16[512,512]{1,0:T(8,128)(2,1)} %constant.17.clone.order, bf16[2,64,128]{2,1,0:T(8,128)(2,1)} %constant.18.clone.back_rows), custom_call_target="tpu_custom_call" | custom-call | bytes 8388608 | tf_op jit(solution)/shard_map/pallas_call | solution.py:91
  25.5 0.0 collective-permute-done.4.refs_4_
  25.5 0.0 collective-permute-done.3.refs_3_
  25.6 0.6 %copy-done.5 = bf16[16,4096]{1,0:T(8,128)(2,1)} copy-done((bf16[16,4096]{1,0:T(8,128)(2,1)}, bf16[16,4096]{1,0:T(8,128)(2,1)S(1)}, u32[]{:S(2)}) %copy-start.5) | copy-done | bytes 131096
  26.2 0.0 copy-done.7
  26.2 7.2 %shard_map.92.refs_11_ = bf16[32,32,1024]{2,1,0:T(8,128)(2,1)} custom-call(s32[8,16]{1,0:T(8,128)} %bitcast.3, s32[2]{0:T(128)} %pad_add_fusion.1.here.refs_1_, bf16[16,4096]{1,0:T(8,128)(2,1)} %copy-done.1, bf16[16,4096]{1,0:T(8,128)(2,1)} %copy-done.7, bf16[16,4096]{1,0:T(8,128)(2,1)} %copy-done.5, bf16[16,4096]{1,0:T(8,128)(2,1)} %copy-done.4, ...), custom_call_target="tpu_custom_call" | custom-call | bytes 20971520 | tf_op jit(solution)/shard_map/pallas_call | solution.py:256
  33.6 0.6 %copy-done.2 = bf16[16,4096]{1,0:T(8,128)(2,1)} copy-done((bf16[16,4096]{1,0:T(8,128)(2,1)}, bf16[16,4096]{1,0:T(8,128)(2,1)S(1)}, u32[]{:S(2)}) %copy-start.2) | copy-done | bytes 131096
  34.2 0.0 copy-done.3
  34.2 0.6 %copy-done.6 = bf16[16,4096]{1,0:T(8,128)(2,1)} copy-done((bf16[16,4096]{1,0:T(8,128)(2,1)}, bf16[16,4096]{1,0:T(8,128)(2,1)S(1)}, u32[]{:S(2)}) %copy-start.6) | copy-done | bytes 131096
  34.9 7.2 %shard_map.93 = bf16[32,32,1024]{2,1,0:T(8,128)(2,1)} custom-call(s32[8,16]{1,0:T(8,128)} %bitcast.4, s32[2]{0:T(128)} %pad_add_fusion.1.here.refs_1_, bf16[16,4096]{1,0:T(8,128)(2,1)} %copy-done, bf16[16,4096]{1,0:T(8,128)(2,1)} %copy-done.6, bf16[16,4096]{1,0:T(8,128)(2,1)} %copy-done.3, ...), custom_call_target="tpu_custom_call", output_to_operand_aliasing={{}: (11, {})} | custom-call | bytes 20971520 | tf_op jit(solution)/shard_map/pallas_call | solution.py:256
  (15 shorter events, 0.0 us)
Async XLA Ops:
  1.0 24.6 %copy-start.1 = (bf16[16,4096]{1,0:T(8,128)(2,1)}, bf16[16,4096]{1,0:T(8,128)(2,1)S(1)}, u32[]{:S(2)}) copy-start(bf16[16,4096]{1,0:T(8,128)(2,1)S(1)} %get-tuple-element.9.refs_2_) | copy-start | bytes 393220
  1.0 32.5 %copy-start = (bf16[16,4096]{1,0:T(8,128)(2,1)}, bf16[16,4096]{1,0:T(8,128)(2,1)S(1)}, u32[]{:S(2)}) copy-start(bf16[16,4096]{1,0:T(8,128)(2,1)S(1)} %get-tuple-element.10.refs_2_) | copy-start | bytes 393220
  1.0 8.0 %collective-permute-start.5 = (bf16[16,4096]{1,0:T(8,128)(2,1)S(1)}, bf16[16,4096]{1,0:T(8,128)(2,1)S(1)}, u32[]{:S(2)}, u32[]{:S(2)}) collective-permute-start(bf16[16,4096]{1,0:T(8,128)(2,1)S(1)} %get-tuple-element.9.refs_2_), channel_id=1, source_target_pairs={{24,0},{16,8},{8,16},{0,24},{25,1},{17,9},{9,17},{1,25},{26,2},{18... | collective-permute-start | bytes 393224 | tf_op jit(solution)/shard_map/ppermute | solution.py:292
  5.0 20.6 %collective-permute-start.4 = (bf16[16,4096]{1,0:T(8,128)(2,1)S(1)}, bf16[16,4096]{1,0:T(8,128)(2,1)S(1)}, u32[]{:S(2)}, u32[]{:S(2)}) collective-permute-start(bf16[16,4096]{1,0:T(8,128)(2,1)S(1)} %get-tuple-element.9.refs_2_), channel_id=1, source_target_pairs={{16,0},{24,8},{0,16},{8,24},{17,1},{25,9},{1,17},{9,25},{18,2},{26... | collective-permute-start | bytes 393224 | tf_op jit(solution)/shard_map/ppermute | solution.py:292
  5.5 20.1 %collective-permute-start.3 = (bf16[16,4096]{1,0:T(8,128)(2,1)S(1)}, bf16[16,4096]{1,0:T(8,128)(2,1)S(1)}, u32[]{:S(2)}, u32[]{:S(2)}) collective-permute-start(bf16[16,4096]{1,0:T(8,128)(2,1)S(1)} %get-tuple-element.9.refs_2_), channel_id=1, source_target_pairs={{8,0},{0,8},{24,16},{16,24},{9,1},{1,9},{25,17},{17,25},{10,2},{2,... | collective-permute-start | bytes 393224 | tf_op jit(solution)/shard_map/ppermute | solution.py:292
  5.6 27.9 %collective-permute-start.2 = (bf16[16,4096]{1,0:T(8,128)(2,1)S(1)}, bf16[16,4096]{1,0:T(8,128)(2,1)S(1)}, u32[]{:S(2)}, u32[]{:S(2)}) collective-permute-start(bf16[16,4096]{1,0:T(8,128)(2,1)S(1)} %get-tuple-element.10.refs_2_), channel_id=1, source_target_pairs={{24,0},{16,8},{8,16},{0,24},{25,1},{17,9},{9,17},{1,25},{26,2},{18... | collective-permute-start | bytes 393224 | tf_op jit(solution)/shard_map/ppermute | solution.py:292
  8.5 25.1 %collective-permute-start.1 = (bf16[16,4096]{1,0:T(8,128)(2,1)S(1)}, bf16[16,4096]{1,0:T(8,128)(2,1)S(1)}, u32[]{:S(2)}, u32[]{:S(2)}) collective-permute-start(bf16[16,4096]{1,0:T(8,128)(2,1)S(1)} %get-tuple-element.10.refs_2_), channel_id=1, source_target_pairs={{16,0},{24,8},{0,16},{8,24},{17,1},{25,9},{1,17},{9,25},{18,2},{26... | collective-permute-start | bytes 393224 | tf_op jit(solution)/shard_map/ppermute | solution.py:292
  9.0 16.6 %copy-start.4 = (bf16[16,4096]{1,0:T(8,128)(2,1)}, bf16[16,4096]{1,0:T(8,128)(2,1)S(1)}, u32[]{:S(2)}) copy-start(bf16[16,4096]{1,0:T(8,128)(2,1)S(1)} %collective-permute-done.5.refs_5_) | copy-start | bytes 393220
  9.0 24.6 %collective-permute-start = (bf16[16,4096]{1,0:T(8,128)(2,1)S(1)}, bf16[16,4096]{1,0:T(8,128)(2,1)S(1)}, u32[]{:S(2)}, u32[]{:S(2)}) collective-permute-start(bf16[16,4096]{1,0:T(8,128)(2,1)S(1)} %get-tuple-element.10.refs_2_), channel_id=1, source_target_pairs={{8,0},{0,8},{24,16},{16,24},{9,1},{1,9},{25,17},{17,25},{10,2},{2,... | collective-permute-start | bytes 393224 | tf_op jit(solution)/shard_map/ppermute | solution.py:292
  12.6 10.4 %all-to-all-start = ((s32[8,1,16]{2,1,0:T(1,128)}), s32[8,1,16]{2,1,0:T(1,128)S(1)}, u32[]{:S(2)}, u32[]{:S(2)}) async-start(s32[8,1,16]{2,1,0:T(1,128)} %broadcast_in_dim.2), calls=%async_computation | async-start | bytes 8192 | tf_op jit(solution)/shard_map/all_to_all | solution.py:300
  23.0 0.6 %copy-start.8 = (s32[8,1,16]{2,1,0:T(1,128)}, s32[8,1,16]{2,1,0:T(1,128)S(1)}, u32[]{:S(2)}) copy-start(s32[8,1,16]{2,1,0:T(1,128)S(1)} %all-to-all-done) | copy-start | bytes 1540
  25.5 0.7 %copy-start.5 = (bf16[16,4096]{1,0:T(8,128)(2,1)}, bf16[16,4096]{1,0:T(8,128)(2,1)S(1)}, u32[]{:S(2)}) copy-start(bf16[16,4096]{1,0:T(8,128)(2,1)S(1)} %collective-permute-done.4.refs_4_) | copy-start | bytes 393220
  25.5 0.7 %copy-start.7 = (bf16[16,4096]{1,0:T(8,128)(2,1)}, bf16[16,4096]{1,0:T(8,128)(2,1)S(1)}, u32[]{:S(2)}) copy-start(bf16[16,4096]{1,0:T(8,128)(2,1)S(1)} %collective-permute-done.3.refs_3_) | copy-start | bytes 393220
  33.5 0.6 %copy-start.2 = (bf16[16,4096]{1,0:T(8,128)(2,1)}, bf16[16,4096]{1,0:T(8,128)(2,1)S(1)}, u32[]{:S(2)}) copy-start(bf16[16,4096]{1,0:T(8,128)(2,1)S(1)} %collective-permute-done.2.refs_5_) | copy-start | bytes 393220
  33.5 0.7 %copy-start.3 = (bf16[16,4096]{1,0:T(8,128)(2,1)}, bf16[16,4096]{1,0:T(8,128)(2,1)S(1)}, u32[]{:S(2)}) copy-start(bf16[16,4096]{1,0:T(8,128)(2,1)S(1)} %collective-permute-done.1.refs_4_) | copy-start | bytes 393220
  34.2 0.6 %copy-start.6 = (bf16[16,4096]{1,0:T(8,128)(2,1)}, bf16[16,4096]{1,0:T(8,128)(2,1)S(1)}, u32[]{:S(2)}) copy-start(bf16[16,4096]{1,0:T(8,128)(2,1)S(1)} %collective-permute-done.refs_3_) | copy-start | bytes 393220

commit v9 on v5

v9 whole, which is shorter than its diff:
```python
import functools
import math

import jax
import jax.numpy as jnp
import ml_dtypes
import numpy as np
from jax import lax
from jax.experimental import pallas as pl
from jax.experimental.pallas import tpu as pltpu
from jax.sharding import PartitionSpec as P

LANES = 128
BLOCK = 16


def make_tables(window, shots):
    half = window // 2
    quarter = half // 2
    times = np.arange(half)
    freqs = np.concatenate([np.arange(0, half, 2), np.arange(1, half, 2)])

    def waves(rows, columns, period):
        phase = (rows[:, None] * columns[None, :] % period) * (2.0 * math.pi / period)
        return np.cos(phase), np.sin(phase)

    bf16 = ml_dtypes.bfloat16
    cosine, sine = waves(times, freqs, window)
    forward = np.stack(
        [
            np.concatenate([cosine[:, cut], -sine[:, cut]], axis=1)
            for cut in (slice(0, quarter), slice(quarter, half))
        ]
    ).astype(bf16)
    gain = np.where(freqs == 0, 0.5, 1.0)[:, None] * (2.0 / (window * shots))
    inverse = np.stack(
        [
            np.concatenate([gain[cut] * cosine.T[cut], -gain[cut] * sine.T[cut]], axis=0)
            for cut in (slice(0, quarter), slice(quarter, half))
        ]
    ).astype(bf16)
    turn_cos, turn_sin = waves(np.arange(shots), np.arange(shots), shots)
    forward, inverse = [
        table.reshape(2, half, half // LANES, LANES).swapaxes(1, 2) for table in (forward, inverse)
    ]
    over_shots = np.block([[turn_cos, turn_sin], [-turn_sin, turn_cos]]).astype(bf16)
    back_rows = np.stack(
        [
            np.concatenate([turn_cos, -turn_sin], axis=1),
            np.concatenate([turn_sin, turn_cos], axis=1),
        ]
    ).astype(bf16)
    order = np.zeros((half, half), bf16)
    order[freqs, np.arange(half)] = 1
    return forward, inverse, over_shots, back_rows, order


def partner(index, away, count):
    if count & (count - 1) == 0:
        return index ^ away
    return (index + away) % count


def gather_kernel(peers, recs, *refs):
    ticks, places, *refs = refs
    share = ticks.shape[1]
    traces, refs = refs[:peers], refs[peers:]
    flags, over_shots, back_rows = refs[:3]
    table_refs, out = refs[3:6], refs[6]
    forward, inverse, order, tiles, folds, spectra, waved, mixed, swapped, ready = refs[7:17]
    table_sem, out_sem = refs[17:]
    rec_rows, block_len = traces[0].shape
    shots, half = flags.shape
    window = 2 * half
    slots = ready.shape[1]
    wide = window // LANES
    mid = wide // 2
    arms = mid // 2
    per_block = block_len // LANES
    f32, bf16 = jnp.float32, jnp.bfloat16
    here = lax.axis_index("tm")

    table_copies = [
        pltpu.make_async_copy(table, place, table_sem.at[index])
        for index, (table, place) in enumerate(zip(table_refs, (forward, inverse, order)))
    ]
    for index in (0, 2, 1):
        table_copies[index].start()

    for away, block in enumerate(traces):
        base = partner(here, away, peers) * per_block
        for tile in range(per_block):
            tiles[base + tile] = block[:, tile * LANES : (tile + 1) * LANES]
    for tile in range(wide):
        tiles[peers * per_block + tile] = jnp.zeros((rec_rows, LANES), bf16)

    lane = lax.broadcasted_iota(jnp.int16, (recs, LANES), 1)

    def cut(shot, rows):
        tick = ticks[shot // share, shot % share]
        first = lax.shift_right_logical(tick, LANES.bit_length() - 1)
        within = tick & (LANES - 1)
        piece = [tiles[first + tile, rows] for tile in range(wide + 1)]
        early = lane < within.astype(jnp.int16)
        piece = [jnp.where(early, piece[tile + 1], piece[tile]) for tile in range(wide)]
        turn = (LANES - within) & (LANES - 1)
        sums = [pltpu.roll(piece[tile] + piece[tile + mid], turn, 1) for tile in range(mid)]
        gaps = [pltpu.roll(piece[tile] - piece[tile + mid], turn, 1) for tile in range(mid)]
        return sums, gaps

    def cut_block(block, rows):
        cuts = [cut(shot, rows) for shot in range(block * BLOCK, (block + 1) * BLOCK)]
        for part in range(2):
            for tile in range(mid):
                panel = jnp.stack([cuts[item][part][tile] for item in range(BLOCK)])
                folds[block % 2, part, tile] = jnp.swapaxes(panel, 0, 1)

    def product(left, right, part):
        return jnp.dot(
            jnp.concatenate(left, axis=1),
            jnp.concatenate([right[part, tile] for tile in range(mid)], axis=1),
            preferred_element_type=f32,
        )

    def columns(tile):
        return slice(tile * LANES, (tile + 1) * LANES)

    def transform_block(block):
        for part in range(2):
            panel = [folds[block % 2, part, tile].reshape(recs * BLOCK, LANES) for tile in range(mid)]
            found = product(panel, forward, part).astype(bf16)
            for tile in range(mid):
                spectra[part, tile, :, block * BLOCK : (block + 1) * BLOCK] = found[
                    :, columns(tile)
                ].reshape(recs, BLOCK, LANES)

    def over(rec, keep):
        stacked = jnp.concatenate(
            [
                jnp.concatenate(
                    [spectra[part, tile, rec] for part in range(2) for tile in which], axis=1
                )
                for which in (range(arms), range(arms, mid))
            ],
            axis=0,
        )
        waves = jnp.dot(over_shots[...], stacked, preferred_element_type=f32)
        masked = jnp.concatenate([waves[:shots] * keep, waves[shots:] * keep], axis=0).astype(bf16)
        for tile in range(mid):
            waved[rec % 4, tile] = masked[:, columns(tile)]

    def under(rec, back):
        masked = jnp.concatenate([waved[rec % 4, tile] for tile in range(mid)], axis=1)
        again = jnp.dot(back, masked, preferred_element_type=f32).astype(bf16)
        for part in range(2):
            for arm in range(arms):
                at = columns(part * arms + arm)
                mixed[part, arm, rec] = again[:slots, at]
                mixed[part, arms + arm, rec] = again[slots:, at]

    group = 8

    def restore(first):
        even, odd = [
            product(
                [
                    mixed[part, tile, first : first + group].reshape(group * slots, LANES)
                    for tile in range(mid)
                ],
                inverse,
                part,
            )
            for part in range(2)
        ]
        early, late = (even + odd).astype(bf16), (even - odd).astype(bf16)
        for tile in range(mid):
            for to, found in ((tile, early), (tile + mid, late)):
                swapped[to, first : first + group] = found[:, columns(tile)].reshape(
                    group, slots, LANES
                )

    out_copies = []

    def send(chunk, first):
        base = chunk * recs + first
        for tile in range(wide):
            for slot in range(0, slots, BLOCK):
                ready[tile, slot : slot + BLOCK, base : base + BLOCK] = jnp.swapaxes(
                    swapped[tile, first : first + BLOCK, slot : slot + BLOCK], 0, 1
                )
        copies = [
            pltpu.make_async_copy(
                ready.at[tile, :, pl.ds(base, BLOCK)],
                out.at[:, pl.ds(base, BLOCK), pl.ds(tile * LANES, LANES)],
                out_sem.at[base // BLOCK, tile],
            )
            for tile in range(wide)
        ]
        for copy in copies:
            copy.start()
        out_copies.extend(copies)

    shot_lane = lax.broadcasted_iota(jnp.int32, (1, shots), 1)
    place_all = jnp.full((1, shots), -1, jnp.int32)
    for shot in range(shots):
        tick = ticks[shot // share, shot % share]
        mine = (tick >= here * block_len) & (tick < (here + 1) * block_len)
        place = jnp.where(mine, places[shot // share, shot % share], -1)
        place_all = jnp.where(shot_lane == shot, place, place_all)
    slot_row = lax.broadcasted_iota(jnp.int32, (slots, shots), 0)
    owned = (slot_row == place_all).astype(f32).astype(bf16)

    blocks = shots // BLOCK
    for chunk in range(rec_rows // recs):
        rows = slice(chunk * recs, (chunk + 1) * recs)
        cut_block(0, rows)
        if chunk == 0:
            back = jnp.concatenate(
                [jnp.dot(owned, back_rows[part], preferred_element_type=f32) for part in range(2)],
                axis=0,
            ).astype(bf16)
            table_copies[0].wait()
        for block in range(blocks):
            if block + 1 < blocks:
                cut_block(block + 1, rows)
            transform_block(block)
        if chunk == 0:
            table_copies[2].wait()
            keep = jnp.dot(
                flags[...].astype(f32).astype(bf16), order[...], preferred_element_type=f32
            )
        over(0, keep)
        for rec in range(recs):
            if rec + 1 < recs:
                over(rec + 1, keep)
            under(rec, back)
            if chunk == 0 and rec == group:
                table_copies[1].wait()
            if rec % group == 1 and rec > group:
                restore(rec - group - 1)
            if rec % BLOCK == 2 and rec > BLOCK:
                send(chunk, rec - BLOCK - 2)
        restore(recs - group)
        send(chunk, recs - BLOCK)
    for copy in out_copies:
        copy.wait()


def filter_gathers(codes, traces, flags, tables):
    forward, inverse, over_shots, back_rows, order = tables
    peers = len(traces)
    rec_rows, block_len = traces[0].shape
    shots, half = flags.shape
    window = 2 * half
    slots = 2 * shots // peers
    total = peers * block_len
    recs = rec_rows if shots * rec_rows * window <= 4 << 20 else BLOCK
    smem = pl.BlockSpec(memory_space=pltpu.SMEM)
    vmem = pl.BlockSpec(memory_space=pltpu.VMEM)
    anywhere = pl.BlockSpec(memory_space=pl.ANY)
    flops = 2 * rec_rows * (
        shots * window * half
        + slots * window * half
        + 4 * shots * shots * half
        + 4 * slots * shots * half
    )
    bf16 = jnp.bfloat16
    return pl.pallas_call(
        functools.partial(gather_kernel, peers, recs),
        out_shape=jax.ShapeDtypeStruct((slots, rec_rows, window), bf16),
        in_specs=[smem, smem] + [vmem] * (peers + 3) + [anywhere] * 3,
        out_specs=anywhere,
        scratch_shapes=[
            pltpu.VMEM(forward.shape, bf16),
            pltpu.VMEM(inverse.shape, bf16),
            pltpu.VMEM(order.shape, bf16),
            pltpu.VMEM(((total + window) // LANES, rec_rows, LANES), bf16),
            pltpu.VMEM((2, 2, half // LANES, recs, BLOCK, LANES), bf16),
            pltpu.VMEM((2, half // LANES, recs, shots, LANES), bf16),
            pltpu.VMEM((4, half // LANES, 2 * shots, LANES), bf16),
            pltpu.VMEM((2, half // LANES, recs, slots, LANES), bf16),
            pltpu.VMEM((window // LANES, recs, slots, LANES), bf16),
            pltpu.VMEM((window // LANES, slots, rec_rows, LANES), bf16),
            pltpu.SemaphoreType.DMA((3,)),
            pltpu.SemaphoreType.DMA((rec_rows // BLOCK, window // LANES)),
        ],
        compiler_params=pltpu.CompilerParams(vmem_limit_bytes=60 << 20),
        cost_estimate=pl.CostEstimate(
            flops=flops,
            bytes_accessed=2 * rec_rows * (total + slots * window),
            transcendentals=0,
        ),
    )(*codes, *traces, flags, over_shots, back_rows, forward, inverse, order)


def on_device(station_traces, shot_onset_ticks, span_place_index, spectral_keep_flags):
    shots, half = spectral_keep_flags.shape
    tables = make_tables(2 * half, shots)
    peers = lax.axis_size("tm")
    lines = lax.axis_size("line")
    traces = [station_traces] + [
        lax.ppermute(
            station_traces,
            "tm",
            [(partner(index, away, peers), index) for index in range(peers)],
        )
        for away in range(1, peers)
    ]
    share = shots // lines
    row = lax.broadcasted_iota(jnp.int32, (lines, share), 0)
    own = row == lax.axis_index("line")
    codes = lax.psum(
        [jnp.where(own, part[None], 0) for part in (shot_onset_ticks, span_place_index)], "line"
    )
    return filter_gathers(codes, traces, spectral_keep_flags, tables)


def solution(mesh):
    in_specs = (P("line", "tm"), P("line"), P("line"), P())
    out_specs = P("tm", "line", None)
    return jax.shard_map(
        on_device, mesh=mesh, in_specs=in_specs, out_specs=out_specs, check_vma=False
    )
```

time: 33.1 us -> 29.8 us (0.900)
  blocking collectives: 0 us -> 10.3 us
  starting transfers between devices: 9.81 us -> 4.46 us
  Pallas kernels: 15.3 us -> 12.6 us
  waiting for transfers between devices: 2.9 us -> 0.72 us
  matrix products: 1.98 us -> 0 us
  local copies, waits for them, and re-layouts: 1.46 us -> 0.69 us
  other arithmetic: 1.36 us -> 0.75 us
    psum x0 -> x1, blocking collectives: none -> 10.3 us  [on_device(): lax.psum([jnp.where(own, part[None], 0) for part in (shot_onset_ticks, sp...]
    all_to_all x1 -> x0, starting transfers between devices: 5.35 us -> none  [on_device(): lax.all_to_all(codes, 'line', split_axis=0, concat_axis=0, tiled=True)]
    all_to_all x1 -> x0, waiting for transfers between devices: 2.89 us -> none  [on_device(): lax.all_to_all(codes, 'line', split_axis=0, concat_axis=0, tiled=True)]
    pallas_call x1, Pallas kernels: 15.3 us -> 12.6 us  [filter_gathers(): pl.pallas_call(functools.partial(gather_kernel, peers, recs), out_shape=j...]
    dot_general x1 -> x0, matrix products: 1.98 us -> none  [on_device(): jnp.dot(spectral_keep_flags.astype(jnp.bfloat16), order, preferred_elemen...]
    concatenate x1 -> x0, other arithmetic: 0.75 us -> none  [on_device(): codes = jnp.concatenate([shot_onset_ticks, span_place_index])]
    select_n x0 -> x1, other arithmetic: none -> 0.74 us  [on_device(): jnp.where(own, part[None], 0)]
    ppermute x3, waiting for transfers between devices: 0.01 us -> 0.72 us  [on_device(): lax.ppermute(station_traces, 'tm', [(partner(index, away, peers), index)...]
  transfers between devices with their start and end apart: 4 -> 3, of which waited for: 1 -> 1; matrix products, arithmetic and copies ran while one was open for 12% -> 3% of each run, Pallas kernels for 0% -> 0%
where the time goes in v9:
time: 29.8 us; the launch traced here: 29.6 us
  Pallas kernels  12.6 us (42%)
  blocking collectives  10.3 us (35%)
  starting transfers between devices  4.46 us (15%)
  other arithmetic  0.75 us (3%)
  waiting for transfers between devices  0.72 us (2%)
  local copies, waits for them, and re-layouts  0.69 us (2%)
    pallas_call x1, Pallas kernels, filter_gathers(): pl.pallas_call(functools.partial(gather_kernel, peers, recs), out_shape=j...  12.6 us
    psum x1, blocking collectives, on_device(): lax.psum([jnp.where(own, part[None], 0) for part in (shot_onset_ticks, sp...  10.3 us
    ppermute x3, starting transfers between devices, on_device(): lax.ppermute(station_traces, 'tm', [(partner(index, away, peers), index)...  4.46 us
    select_n x1, other arithmetic, on_device(): jnp.where(own, part[None], 0)  0.74 us
    ppermute x3, waiting for transfers between devices, on_device(): lax.ppermute(station_traces, 'tm', [(partner(index, away, peers), index)...  0.72 us
    unnamed x6, local copies, waits for them, and re-layouts  0.69 us
  transfers between devices with their start and end apart: 3, of which 1 were waited for; matrix products, arithmetic and copies ran while one was open for 3% of the time, Pallas kernels for 0%

profile of v9, /device:TPU:0, one launch (start us, length us, event | category | flops | bytes accessed | tf_op | source)
XLA Modules:
  0.0 29.6 jit_solution(3338524748191066782)
XLA Ops:
  0.0 3.0 %collective-permute-start.1 = (bf16[32,4096]{1,0:T(8,128)(2,1)}, bf16[32,4096]{1,0:T(8,128)(2,1)S(1)}, u32[]{:S(2)}, u32[]{:S(2)}) collective-permute-start(bf16[32,4096]{1,0:T(8,128)(2,1)} %refs_2_.1), channel_id=1, source_target_pairs={{16,0},{24,8},{0,16},{8,24},{17,1},{25,9},{1,17},{9,25},{18,2},{26... | collective-permute-start | bytes 786440 | tf_op jit(solution)/shard_map/ppermute | solution.py:302
  3.0 1.5 %collective-permute-start = (bf16[32,4096]{1,0:T(8,128)(2,1)}, bf16[32,4096]{1,0:T(8,128)(2,1)S(1)}, u32[]{:S(2)}, u32[]{:S(2)}) collective-permute-start(bf16[32,4096]{1,0:T(8,128)(2,1)} %refs_2_.1), channel_id=1, source_target_pairs={{8,0},{0,8},{24,16},{16,24},{9,1},{1,9},{25,17},{17,25},{10,2},{2,... | collective-permute-start | bytes 786440 | tf_op jit(solution)/shard_map/ppermute | solution.py:302
  4.5 0.0 collective-permute-start.2
  4.5 0.7 %broadcast_select_fusion = (s32[8,8]{1,0:T(8,128)S(1)}, s32[8,8]{1,0:T(8,128)S(1)}) fusion(s32[8]{0:T(128)} %param.11, pred[8]{0:T(512)(128)(4,1)S(1)} %iota_compare_fusion, s32[8]{0:T(128)} %param.10), kind=kLoop, calls=%fused_computation | loop fusion | flops 128 | bytes 584 | tf_op jit(solution)/shard_map/jit(_where)/select_n | solution.py:313
  5.2 10.3 %all-reduce = (s32[8,8]{1,0:T(8,128)}, s32[8,8]{1,0:T(8,128)}) all-reduce(s32[8,8]{1,0:T(8,128)S(1)} %get-tuple-element.8, s32[8,8]{1,0:T(8,128)S(1)} %get-tuple-element.7), channel_id=1, replica_groups=mesh['tm'=4,'line'=8] {'line'}, use_global_device_ids=true, to_apply=%region_0.1 | all-reduce | flops 128 | bytes 1024 | tf_op jit(solution)/shard_map/psum | solution.py:312
  15.6 0.0 collective-permute-done.1.refs_4_
  15.6 0.0 copy-start
  15.6 0.0 collective-permute-done.refs_3_
  15.6 0.0 copy-start.1
  15.6 0.7 %collective-permute-done.2.refs_5_ = bf16[32,4096]{1,0:T(8,128)(2,1)S(1)} collective-permute-done((bf16[32,4096]{1,0:T(8,128)(2,1)}, bf16[32,4096]{1,0:T(8,128)(2,1)S(1)}, u32[]{:S(2)}, u32[]{:S(2)}) %collective-permute-start.2) | collective-permute-done | bytes 262176 | tf_op jit(solution)/shard_map/ppermute | solution.py:302
  16.3 0.0 copy-start.2
  16.3 0.0 copy-done
  16.3 0.1 copy-done.1
  16.4 0.6 %copy-done.2 = bf16[32,4096]{1,0:T(8,128)(2,1)} copy-done((bf16[32,4096]{1,0:T(8,128)(2,1)}, bf16[32,4096]{1,0:T(8,128)(2,1)S(1)}, u32[]{:S(2)}) %copy-start.2) | copy-done | bytes 262168
  17.0 12.6 %shard_map.91 = bf16[32,32,1024]{2,1,0:T(8,128)(2,1)} custom-call(s32[8,8]{1,0:T(8,128)} %get-tuple-element.5.refs_0_, s32[8,8]{1,0:T(8,128)} %get-tuple-element.6.refs_1_, bf16[32,4096]{1,0:T(8,128)(2,1)} %refs_2_.1, bf16[32,4096]{1,0:T(8,128)(2,1)} %copy-done.1, bf16[32,4096]{1,0:T(8,128)(2,1)} %copy-done, bf16[32,4096]{1,0:T(8,128)(2,1)} %copy-done.2, ...), custom_call_target="tpu_custom_call" | custom-call | flops 4026531840 | bytes 3145728 | tf_op jit(solution)/shard_map/pallas_call | solution.py:268
  (1 shorter events, 0.0 us)
Async XLA Ops:
  0.0 15.6 %collective-permute-start.1 = (bf16[32,4096]{1,0:T(8,128)(2,1)}, bf16[32,4096]{1,0:T(8,128)(2,1)S(1)}, u32[]{:S(2)}, u32[]{:S(2)}) collective-permute-start(bf16[32,4096]{1,0:T(8,128)(2,1)} %refs_2_.1), channel_id=1, source_target_pairs={{16,0},{24,8},{0,16},{8,24},{17,1},{25,9},{1,17},{9,25},{18,2},{26... | collective-permute-start | bytes 786440 | tf_op jit(solution)/shard_map/ppermute | solution.py:302
  3.0 12.6 %collective-permute-start = (bf16[32,4096]{1,0:T(8,128)(2,1)}, bf16[32,4096]{1,0:T(8,128)(2,1)S(1)}, u32[]{:S(2)}, u32[]{:S(2)}) collective-permute-start(bf16[32,4096]{1,0:T(8,128)(2,1)} %refs_2_.1), channel_id=1, source_target_pairs={{8,0},{0,8},{24,16},{16,24},{9,1},{1,9},{25,17},{17,25},{10,2},{2,... | collective-permute-start | bytes 786440 | tf_op jit(solution)/shard_map/ppermute | solution.py:302
  4.5 11.8 %collective-permute-start.2 = (bf16[32,4096]{1,0:T(8,128)(2,1)}, bf16[32,4096]{1,0:T(8,128)(2,1)S(1)}, u32[]{:S(2)}, u32[]{:S(2)}) collective-permute-start(bf16[32,4096]{1,0:T(8,128)(2,1)} %refs_2_.1), channel_id=1, source_target_pairs={{24,0},{16,8},{8,16},{0,24},{25,1},{17,9},{9,17},{1,25},{26,2},{18... | collective-permute-start | bytes 786440 | tf_op jit(solution)/shard_map/ppermute | solution.py:302
  15.6 0.7 %copy-start = (bf16[32,4096]{1,0:T(8,128)(2,1)}, bf16[32,4096]{1,0:T(8,128)(2,1)S(1)}, u32[]{:S(2)}) copy-start(bf16[32,4096]{1,0:T(8,128)(2,1)S(1)} %collective-permute-done.1.refs_4_) | copy-start | bytes 786436
  15.6 0.8 %copy-start.1 = (bf16[32,4096]{1,0:T(8,128)(2,1)}, bf16[32,4096]{1,0:T(8,128)(2,1)S(1)}, u32[]{:S(2)}) copy-start(bf16[32,4096]{1,0:T(8,128)(2,1)S(1)} %collective-permute-done.refs_3_) | copy-start | bytes 786436
  16.3 0.7 %copy-start.2 = (bf16[32,4096]{1,0:T(8,128)(2,1)}, bf16[32,4096]{1,0:T(8,128)(2,1)S(1)}, u32[]{:S(2)}) copy-start(bf16[32,4096]{1,0:T(8,128)(2,1)S(1)} %collective-permute-done.2.refs_5_) | copy-start | bytes 786436

commit v10 on v9

--- a/solution.py
+++ b/solution.py
@@ -65,10 +65,9 @@
     ticks, places, *refs = refs
     share = ticks.shape[1]
     traces, refs = refs[:peers], refs[peers:]
-    flags, over_shots, back_rows = refs[:3]
-    table_refs, out = refs[3:6], refs[6]
-    forward, inverse, order, tiles, folds, spectra, waved, mixed, swapped, ready = refs[7:17]
-    table_sem, out_sem = refs[17:]
+    table_refs, out, loaded, refs = refs[:6], refs[6], refs[7:14], refs[14:]
+    own, forward, inverse, order, flags, over_shots, back_rows = loaded
+    tiles, folds, spectra, waved, mixed, swapped, ready, table_sem, out_sem = refs
     rec_rows, block_len = traces[0].shape
     shots, half = flags.shape
     window = 2 * half
@@ -82,12 +81,13 @@
 
     table_copies = [
         pltpu.make_async_copy(table, place, table_sem.at[index])
-        for index, (table, place) in enumerate(zip(table_refs, (forward, inverse, order)))
+        for index, (table, place) in enumerate(zip((traces[0], *table_refs), loaded))
     ]
-    for index in (0, 2, 1):
+    for index in (0, 6, 1, 4, 3, 5, 2):
         table_copies[index].start()
 
-    for away, block in enumerate(traces):
+    table_copies[0].wait()
+    for away, block in enumerate((own, *traces[1:])):
         base = partner(here, away, peers) * per_block
         for tile in range(per_block):
             tiles[base + tile] = block[:, tile * LANES : (tile + 1) * LANES]
@@ -147,10 +147,10 @@
         waves = jnp.dot(over_shots[...], stacked, preferred_element_type=f32)
         masked = jnp.concatenate([waves[:shots] * keep, waves[shots:] * keep], axis=0).astype(bf16)
         for tile in range(mid):
-            waved[rec % 4, tile] = masked[:, columns(tile)]
+            waved[tile, rec] = masked[:, columns(tile)]
 
     def under(rec, back):
-        masked = jnp.concatenate([waved[rec % 4, tile] for tile in range(mid)], axis=1)
+        masked = jnp.concatenate([waved[tile, rec] for tile in range(mid)], axis=1)
         again = jnp.dot(back, masked, preferred_element_type=f32).astype(bf16)
         for part in range(2):
             for arm in range(arms):
@@ -215,33 +215,32 @@
         rows = slice(chunk * recs, (chunk + 1) * recs)
         cut_block(0, rows)
         if chunk == 0:
+            table_copies[6].wait()
             back = jnp.concatenate(
                 [jnp.dot(owned, back_rows[part], preferred_element_type=f32) for part in range(2)],
                 axis=0,
             ).astype(bf16)
-            table_copies[0].wait()
+            table_copies[1].wait()
         for block in range(blocks):
             if block + 1 < blocks:
                 cut_block(block + 1, rows)
             transform_block(block)
         if chunk == 0:
-            table_copies[2].wait()
+            for index in (3, 4, 5):
+                table_copies[index].wait()
             keep = jnp.dot(
                 flags[...].astype(f32).astype(bf16), order[...], preferred_element_type=f32
             )
-        over(0, keep)
         for rec in range(recs):
-            if rec + 1 < recs:
-                over(rec + 1, keep)
+            over(rec, keep)
+        for rec in range(recs):
             under(rec, back)
-            if chunk == 0 and rec == group:
-                table_copies[1].wait()
-            if rec % group == 1 and rec > group:
-                restore(rec - group - 1)
-            if rec % BLOCK == 2 and rec > BLOCK:
-                send(chunk, rec - BLOCK - 2)
-        restore(recs - group)
-        send(chunk, recs - BLOCK)
+        if chunk == 0:
+            table_copies[2].wait()
+        for first in range(0, recs, group):
+            restore(first)
+        for first in range(0, recs, BLOCK):
+            send(chunk, first)
     for copy in out_copies:
         copy.wait()
 
@@ -257,7 +256,7 @@
     recs = rec_rows if shots * rec_rows * window <= 4 << 20 else BLOCK
     smem = pl.BlockSpec(memory_space=pltpu.SMEM)
     vmem = pl.BlockSpec(memory_space=pltpu.VMEM)
-    anywhere = pl.BlockSpec(memory_space=pl.ANY)
+    hbm = pl.BlockSpec(memory_space=pltpu.HBM)
     flops = 2 * rec_rows * (
         shots * window * half
         + slots * window * half
@@ -265,23 +264,23 @@
         + 4 * slots * shots * half
     )
     bf16 = jnp.bfloat16
+    shared = [forward, inverse, order, flags, over_shots, back_rows]
     return pl.pallas_call(
         functools.partial(gather_kernel, peers, recs),
         out_shape=jax.ShapeDtypeStruct((slots, rec_rows, window), bf16),
-        in_specs=[smem, smem] + [vmem] * (peers + 3) + [anywhere] * 3,
-        out_specs=anywhere,
+        in_specs=[smem, smem, hbm] + [vmem] * (peers - 1) + [hbm] * 6,
+        out_specs=hbm,
         scratch_shapes=[
-            pltpu.VMEM(forward.shape, bf16),
-            pltpu.VMEM(inverse.shape, bf16),
-            pltpu.VMEM(order.shape, bf16),
+            pltpu.VMEM((rec_rows, block_len), bf16),
+            *[pltpu.VMEM(table.shape, table.dtype) for table in shared],
             pltpu.VMEM(((total + window) // LANES, rec_rows, LANES), bf16),
             pltpu.VMEM((2, 2, half // LANES, recs, BLOCK, LANES), bf16),
             pltpu.VMEM((2, half // LANES, recs, shots, LANES), bf16),
-            pltpu.VMEM((4, half // LANES, 2 * shots, LANES), bf16),
+            pltpu.VMEM((half // LANES, recs, 2 * shots, LANES), bf16),
             pltpu.VMEM((2, half // LANES, recs, slots, LANES), bf16),
             pltpu.VMEM((window // LANES, recs, slots, LANES), bf16),
             pltpu.VMEM((window // LANES, slots, rec_rows, LANES), bf16),
-            pltpu.SemaphoreType.DMA((3,)),
+            pltpu.SemaphoreType.DMA((7,)),
             pltpu.SemaphoreType.DMA((rec_rows // BLOCK, window // LANES)),
         ],
         compiler_params=pltpu.CompilerParams(vmem_limit_bytes=60 << 20),
@@ -290,7 +289,7 @@
             bytes_accessed=2 * rec_rows * (total + slots * window),
             transcendentals=0,
         ),
-    )(*codes, *traces, flags, over_shots, back_rows, forward, inverse, order)
+    )(*codes, *traces, *shared)
 
 
 def on_device(station_traces, shot_onset_ticks, span_place_index, spectral_keep_flags):

time: 29.8 us -> 27.7 us (0.930)
  Pallas kernels: 12.6 us -> 10.5 us
    pallas_call x1, Pallas kernels: 12.6 us -> 10.5 us  [filter_gathers(): pl.pallas_call(functools.partial(gather_kernel, peers, recs), out_shape=j...]
where the time goes in v10:
time: 27.7 us; the launch traced here: 27.5 us
  Pallas kernels  10.5 us (38%)
  blocking collectives  10.3 us (37%)
  starting transfers between devices  4.46 us (16%)
  other arithmetic  0.75 us (3%)
  waiting for transfers between devices  0.72 us (3%)
  local copies, waits for them, and re-layouts  0.69 us (2%)
    pallas_call x1, Pallas kernels, filter_gathers(): pl.pallas_call(functools.partial(gather_kernel, peers, recs), out_shape=j...  10.5 us
    psum x1, blocking collectives, on_device(): lax.psum([jnp.where(own, part[None], 0) for part in (shot_onset_ticks, sp...  10.3 us
    ppermute x3, starting transfers between devices, on_device(): lax.ppermute(station_traces, 'tm', [(partner(index, away, peers), index)...  4.46 us
    select_n x1, other arithmetic, on_device(): jnp.where(own, part[None], 0)  0.74 us
    ppermute x3, waiting for transfers between devices, on_device(): lax.ppermute(station_traces, 'tm', [(partner(index, away, peers), index)...  0.72 us
    unnamed x6, local copies, waits for them, and re-layouts  0.69 us
  transfers between devices with their start and end apart: 3, of which 1 were waited for; matrix products, arithmetic and copies ran while one was open for 3% of the time, Pallas kernels for 0%

profile of v10, /device:TPU:0, one launch (start us, length us, event | category | flops | bytes accessed | tf_op | source)
XLA Modules:
  0.0 27.5 jit_solution(1864917917238909749)
XLA Ops:
  0.0 3.0 %collective-permute-start.1 = (bf16[32,4096]{1,0:T(8,128)(2,1)}, bf16[32,4096]{1,0:T(8,128)(2,1)S(1)}, u32[]{:S(2)}, u32[]{:S(2)}) collective-permute-start(bf16[32,4096]{1,0:T(8,128)(2,1)} %refs_2_.1), channel_id=1, source_target_pairs={{16,0},{24,8},{0,16},{8,24},{17,1},{25,9},{1,17},{9,25},{18,2},{26... | collective-permute-start | bytes 786440 | tf_op jit(solution)/shard_map/ppermute | solution.py:301
  3.0 1.5 %collective-permute-start = (bf16[32,4096]{1,0:T(8,128)(2,1)}, bf16[32,4096]{1,0:T(8,128)(2,1)S(1)}, u32[]{:S(2)}, u32[]{:S(2)}) collective-permute-start(bf16[32,4096]{1,0:T(8,128)(2,1)} %refs_2_.1), channel_id=1, source_target_pairs={{8,0},{0,8},{24,16},{16,24},{9,1},{1,9},{25,17},{17,25},{10,2},{2,... | collective-permute-start | bytes 786440 | tf_op jit(solution)/shard_map/ppermute | solution.py:301
  4.5 0.0 collective-permute-start.2
  4.5 0.7 %broadcast_select_fusion = (s32[8,8]{1,0:T(8,128)S(1)}, s32[8,8]{1,0:T(8,128)S(1)}) fusion(s32[8]{0:T(128)} %param.11, pred[8]{0:T(512)(128)(4,1)S(1)} %iota_compare_fusion, s32[8]{0:T(128)} %param.10), kind=kLoop, calls=%fused_computation | loop fusion | flops 128 | bytes 584 | tf_op jit(solution)/shard_map/jit(_where)/select_n | solution.py:312
  5.2 10.3 %all-reduce = (s32[8,8]{1,0:T(8,128)}, s32[8,8]{1,0:T(8,128)}) all-reduce(s32[8,8]{1,0:T(8,128)S(1)} %get-tuple-element.8, s32[8,8]{1,0:T(8,128)S(1)} %get-tuple-element.7), channel_id=1, replica_groups=mesh['tm'=4,'line'=8] {'line'}, use_global_device_ids=true, to_apply=%region_0.1 | all-reduce | flops 128 | bytes 1024 | tf_op jit(solution)/shard_map/psum | solution.py:311
  15.6 0.0 collective-permute-done.1.refs_4_
  15.6 0.0 copy-start
  15.6 0.0 collective-permute-done.refs_3_
  15.6 0.0 copy-start.1
  15.6 0.7 %collective-permute-done.2.refs_5_ = bf16[32,4096]{1,0:T(8,128)(2,1)S(1)} collective-permute-done((bf16[32,4096]{1,0:T(8,128)(2,1)}, bf16[32,4096]{1,0:T(8,128)(2,1)S(1)}, u32[]{:S(2)}, u32[]{:S(2)}) %collective-permute-start.2) | collective-permute-done | bytes 262176 | tf_op jit(solution)/shard_map/ppermute | solution.py:301
  16.3 0.0 copy-start.2
  16.3 0.0 copy-done
  16.3 0.1 copy-done.1
  16.4 0.6 %copy-done.2 = bf16[32,4096]{1,0:T(8,128)(2,1)} copy-done((bf16[32,4096]{1,0:T(8,128)(2,1)}, bf16[32,4096]{1,0:T(8,128)(2,1)S(1)}, u32[]{:S(2)}) %copy-start.2) | copy-done | bytes 262168
  17.0 10.5 %shard_map.91 = bf16[32,32,1024]{2,1,0:T(8,128)(2,1)} custom-call(s32[8,8]{1,0:T(8,128)} %get-tuple-element.5.refs_0_, s32[8,8]{1,0:T(8,128)} %get-tuple-element.6.refs_1_, bf16[32,4096]{1,0:T(8,128)(2,1)} %refs_2_.1, bf16[32,4096]{1,0:T(8,128)(2,1)} %copy-done.1, bf16[32,4096]{1,0:T(8,128)(2,1)} %copy-done, bf16[32,4096]{1,0:T(8,128)(2,1)} %copy-done.2, ...), custom_call_target="tpu_custom_call" | custom-call | flops 4026531840 | bytes 3145728 | tf_op jit(solution)/shard_map/pallas_call | solution.py:268
  (1 shorter events, 0.0 us)
Async XLA Ops:
  0.0 15.6 %collective-permute-start.1 = (bf16[32,4096]{1,0:T(8,128)(2,1)}, bf16[32,4096]{1,0:T(8,128)(2,1)S(1)}, u32[]{:S(2)}, u32[]{:S(2)}) collective-permute-start(bf16[32,4096]{1,0:T(8,128)(2,1)} %refs_2_.1), channel_id=1, source_target_pairs={{16,0},{24,8},{0,16},{8,24},{17,1},{25,9},{1,17},{9,25},{18,2},{26... | collective-permute-start | bytes 786440 | tf_op jit(solution)/shard_map/ppermute | solution.py:301
  3.0 12.6 %collective-permute-start = (bf16[32,4096]{1,0:T(8,128)(2,1)}, bf16[32,4096]{1,0:T(8,128)(2,1)S(1)}, u32[]{:S(2)}, u32[]{:S(2)}) collective-permute-start(bf16[32,4096]{1,0:T(8,128)(2,1)} %refs_2_.1), channel_id=1, source_target_pairs={{8,0},{0,8},{24,16},{16,24},{9,1},{1,9},{25,17},{17,25},{10,2},{2,... | collective-permute-start | bytes 786440 | tf_op jit(solution)/shard_map/ppermute | solution.py:301
  4.5 11.8 %collective-permute-start.2 = (bf16[32,4096]{1,0:T(8,128)(2,1)}, bf16[32,4096]{1,0:T(8,128)(2,1)S(1)}, u32[]{:S(2)}, u32[]{:S(2)}) collective-permute-start(bf16[32,4096]{1,0:T(8,128)(2,1)} %refs_2_.1), channel_id=1, source_target_pairs={{24,0},{16,8},{8,16},{0,24},{25,1},{17,9},{9,17},{1,25},{26,2},{18... | collective-permute-start | bytes 786440 | tf_op jit(solution)/shard_map/ppermute | solution.py:301
  15.6 0.7 %copy-start = (bf16[32,4096]{1,0:T(8,128)(2,1)}, bf16[32,4096]{1,0:T(8,128)(2,1)S(1)}, u32[]{:S(2)}) copy-start(bf16[32,4096]{1,0:T(8,128)(2,1)S(1)} %collective-permute-done.1.refs_4_) | copy-start | bytes 786436
  15.6 0.8 %copy-start.1 = (bf16[32,4096]{1,0:T(8,128)(2,1)}, bf16[32,4096]{1,0:T(8,128)(2,1)S(1)}, u32[]{:S(2)}) copy-start(bf16[32,4096]{1,0:T(8,128)(2,1)S(1)} %collective-permute-done.refs_3_) | copy-start | bytes 786436
  16.3 0.7 %copy-start.2 = (bf16[32,4096]{1,0:T(8,128)(2,1)}, bf16[32,4096]{1,0:T(8,128)(2,1)S(1)}, u32[]{:S(2)}) copy-start(bf16[32,4096]{1,0:T(8,128)(2,1)S(1)} %collective-permute-done.2.refs_5_) | copy-start | bytes 786436

commit v11 on v10

--- a/solution.py
+++ b/solution.py
@@ -67,11 +67,12 @@
     traces, refs = refs[:peers], refs[peers:]
     table_refs, out, loaded, refs = refs[:6], refs[6], refs[7:14], refs[14:]
     own, forward, inverse, order, flags, over_shots, back_rows = loaded
-    tiles, folds, spectra, waved, mixed, swapped, ready, table_sem, out_sem = refs
+    tiles, folds, spectra, waved, mixed, ready, table_sem, out_sem = refs
     rec_rows, block_len = traces[0].shape
     shots, half = flags.shape
     window = 2 * half
-    slots = ready.shape[1]
+    slots = ready.shape[0]
+    pitch = recs + 1
     wide = window // LANES
     mid = wide // 2
     arms = mid // 2
@@ -109,11 +110,10 @@
         return sums, gaps
 
     def cut_block(block, rows):
-        cuts = [cut(shot, rows) for shot in range(block * BLOCK, (block + 1) * BLOCK)]
-        for part in range(2):
-            for tile in range(mid):
-                panel = jnp.stack([cuts[item][part][tile] for item in range(BLOCK)])
-                folds[block % 2, part, tile] = jnp.swapaxes(panel, 0, 1)
+        for item in range(BLOCK):
+            for part, tiles_of in enumerate(cut(block * BLOCK + item, rows)):
+                for tile in range(mid):
+                    folds[block % 2, part, tile, item * recs : (item + 1) * recs] = tiles_of[tile]
 
     def product(left, right, part):
         return jnp.dot(
@@ -127,18 +127,26 @@
 
     def transform_block(block):
         for part in range(2):
-            panel = [folds[block % 2, part, tile].reshape(recs * BLOCK, LANES) for tile in range(mid)]
-            found = product(panel, forward, part).astype(bf16)
-            for tile in range(mid):
-                spectra[part, tile, :, block * BLOCK : (block + 1) * BLOCK] = found[
-                    :, columns(tile)
-                ].reshape(recs, BLOCK, LANES)
+            panel = [folds[block % 2, part, tile] for tile in range(mid)]
+            found = product(panel, forward, part)
+            for item in range(BLOCK):
+                row = (block * BLOCK + item) * pitch
+                for tile in range(mid):
+                    spectra[part * mid + tile, row : row + recs] = found[
+                        item * recs : (item + 1) * recs, columns(tile)
+                    ]
 
     def over(rec, keep):
+        at = pl.ds(rec, shots, stride=pitch)
         stacked = jnp.concatenate(
             [
                 jnp.concatenate(
-                    [spectra[part, tile, rec] for part in range(2) for tile in which], axis=1
+                    [
+                        spectra[part * mid + tile, at].astype(bf16)
+                        for part in range(2)
+                        for tile in which
+                    ],
+                    axis=1,
                 )
                 for which in (range(arms), range(arms, mid))
             ],
@@ -151,20 +159,28 @@
 
     def under(rec, back):
         masked = jnp.concatenate([waved[tile, rec] for tile in range(mid)], axis=1)
-        again = jnp.dot(back, masked, preferred_element_type=f32).astype(bf16)
+        again = jnp.dot(back, masked, preferred_element_type=f32)
+        to = pl.ds(rec, slots, stride=pitch)
         for part in range(2):
             for arm in range(arms):
                 at = columns(part * arms + arm)
-                mixed[part, arm, rec] = again[:slots, at]
-                mixed[part, arms + arm, rec] = again[slots:, at]
-
-    group = 8
-
-    def restore(first):
+                mixed[part * mid + arm, to] = again[:slots, at]
+                mixed[part * mid + arms + arm, to] = again[slots:, at]
+
+    group = min(slots, 256 // recs)
+    out_copies = []
+
+    def restore(chunk, first):
         even, odd = [
             product(
                 [
-                    mixed[part, tile, first : first + group].reshape(group * slots, LANES)
+                    jnp.concatenate(
+                        [
+                            mixed[part * mid + tile, slot * pitch : slot * pitch + recs].astype(bf16)
+                            for slot in range(first, first + group)
+                        ],
+                        axis=0,
+                    )
                     for tile in range(mid)
                 ],
                 inverse,
@@ -172,33 +188,16 @@
             )
             for part in range(2)
         ]
+        rows = slice(chunk * recs, (chunk + 1) * recs)
         early, late = (even + odd).astype(bf16), (even - odd).astype(bf16)
-        for tile in range(mid):
-            for to, found in ((tile, early), (tile + mid, late)):
-                swapped[to, first : first + group] = found[:, columns(tile)].reshape(
-                    group, slots, LANES
-                )
-
-    out_copies = []
-
-    def send(chunk, first):
-        base = chunk * recs + first
-        for tile in range(wide):
-            for slot in range(0, slots, BLOCK):
-                ready[tile, slot : slot + BLOCK, base : base + BLOCK] = jnp.swapaxes(
-                    swapped[tile, first : first + BLOCK, slot : slot + BLOCK], 0, 1
-                )
-        copies = [
-            pltpu.make_async_copy(
-                ready.at[tile, :, pl.ds(base, BLOCK)],
-                out.at[:, pl.ds(base, BLOCK), pl.ds(tile * LANES, LANES)],
-                out_sem.at[base // BLOCK, tile],
-            )
-            for tile in range(wide)
-        ]
-        for copy in copies:
-            copy.start()
-        out_copies.extend(copies)
+        ready[first : first + group, rows, :half] = early.reshape(group, recs, half)
+        ready[first : first + group, rows, half:] = late.reshape(group, recs, half)
+        block = (pl.ds(first, group), pl.ds(chunk * recs, recs))
+        copy = pltpu.make_async_copy(
+            ready.at[block], out.at[block], out_sem.at[chunk, first // group]
+        )
+        copy.start()
+        out_copies.append(copy)
 
     shot_lane = lax.broadcasted_iota(jnp.int32, (1, shots), 1)
     place_all = jnp.full((1, shots), -1, jnp.int32)
@@ -237,10 +236,8 @@
             under(rec, back)
         if chunk == 0:
             table_copies[2].wait()
-        for first in range(0, recs, group):
-            restore(first)
-        for first in range(0, recs, BLOCK):
-            send(chunk, first)
+        for first in range(0, slots, group):
+            restore(chunk, first)
     for copy in out_copies:
         copy.wait()
 
@@ -274,14 +271,13 @@
             pltpu.VMEM((rec_rows, block_len), bf16),
             *[pltpu.VMEM(table.shape, table.dtype) for table in shared],
             pltpu.VMEM(((total + window) // LANES, rec_rows, LANES), bf16),
-            pltpu.VMEM((2, 2, half // LANES, recs, BLOCK, LANES), bf16),
-            pltpu.VMEM((2, half // LANES, recs, shots, LANES), bf16),
+            pltpu.VMEM((2, 2, half // LANES, BLOCK * recs, LANES), bf16),
+            pltpu.VMEM((window // LANES, shots * (recs + 1), LANES), jnp.float32),
             pltpu.VMEM((half // LANES, recs, 2 * shots, LANES), bf16),
-            pltpu.VMEM((2, half // LANES, recs, slots, LANES), bf16),
-            pltpu.VMEM((window // LANES, recs, slots, LANES), bf16),
-            pltpu.VMEM((window // LANES, slots, rec_rows, LANES), bf16),
+            pltpu.VMEM((window // LANES, slots * (recs + 1), LANES), jnp.float32),
+            pltpu.VMEM((slots, rec_rows, window), bf16),
             pltpu.SemaphoreType.DMA((7,)),
-            pltpu.SemaphoreType.DMA((rec_rows // BLOCK, window // LANES)),
+            pltpu.SemaphoreType.DMA((rec_rows // recs, slots)),
         ],
         compiler_params=pltpu.CompilerParams(vmem_limit_bytes=60 << 20),
         cost_estimate=pl.CostEstimate(

time: 27.7 us -> 26.6 us (0.960)
  Pallas kernels: 10.5 us -> 9.51 us
    pallas_call x1, Pallas kernels: 10.5 us -> 9.51 us  [filter_gathers(): pl.pallas_call(functools.partial(gather_kernel, peers, recs), out_shape=j...]
where the time goes in v11:
time: 26.6 us; the launch traced here: 26.5 us
  blocking collectives  10.3 us (39%)
  Pallas kernels  9.51 us (36%)
  starting transfers between devices  4.46 us (17%)
  other arithmetic  0.75 us (3%)
  waiting for transfers between devices  0.72 us (3%)
  local copies, waits for them, and re-layouts  0.69 us (3%)
    psum x1, blocking collectives, on_device(): lax.psum([jnp.where(own, part[None], 0) for part in (shot_onset_ticks, sp...  10.3 us
    pallas_call x1, Pallas kernels, filter_gathers(): pl.pallas_call(functools.partial(gather_kernel, peers, recs), out_shape=j...  9.51 us
    ppermute x3, starting transfers between devices, on_device(): lax.ppermute(station_traces, 'tm', [(partner(index, away, peers), index)...  4.46 us
    select_n x1, other arithmetic, on_device(): jnp.where(own, part[None], 0)  0.74 us
    ppermute x3, waiting for transfers between devices, on_device(): lax.ppermute(station_traces, 'tm', [(partner(index, away, peers), index)...  0.72 us
    unnamed x6, local copies, waits for them, and re-layouts  0.69 us
  transfers between devices with their start and end apart: 3, of which 1 were waited for; matrix products, arithmetic and copies ran while one was open for 3% of the time, Pallas kernels for 0%

profile of v11, /device:TPU:0, one launch (start us, length us, event | category | flops | bytes accessed | tf_op | source)
XLA Modules:
  0.0 26.5 jit_solution(13503962863929571981)
XLA Ops:
  0.0 3.0 %collective-permute-start.1 = (bf16[32,4096]{1,0:T(8,128)(2,1)}, bf16[32,4096]{1,0:T(8,128)(2,1)S(1)}, u32[]{:S(2)}, u32[]{:S(2)}) collective-permute-start(bf16[32,4096]{1,0:T(8,128)(2,1)} %refs_2_.1), channel_id=1, source_target_pairs={{16,0},{24,8},{0,16},{8,24},{17,1},{25,9},{1,17},{9,25},{18,2},{26... | collective-permute-start | bytes 786440 | tf_op jit(solution)/shard_map/ppermute | solution.py:297
  3.0 1.5 %collective-permute-start = (bf16[32,4096]{1,0:T(8,128)(2,1)}, bf16[32,4096]{1,0:T(8,128)(2,1)S(1)}, u32[]{:S(2)}, u32[]{:S(2)}) collective-permute-start(bf16[32,4096]{1,0:T(8,128)(2,1)} %refs_2_.1), channel_id=1, source_target_pairs={{8,0},{0,8},{24,16},{16,24},{9,1},{1,9},{25,17},{17,25},{10,2},{2,... | collective-permute-start | bytes 786440 | tf_op jit(solution)/shard_map/ppermute | solution.py:297
  4.5 0.0 collective-permute-start.2
  4.5 0.7 %broadcast_select_fusion = (s32[8,8]{1,0:T(8,128)S(1)}, s32[8,8]{1,0:T(8,128)S(1)}) fusion(s32[8]{0:T(128)} %param.11, pred[8]{0:T(512)(128)(4,1)S(1)} %iota_compare_fusion, s32[8]{0:T(128)} %param.10), kind=kLoop, calls=%fused_computation | loop fusion | flops 128 | bytes 584 | tf_op jit(solution)/shard_map/jit(_where)/select_n | solution.py:308
  5.2 10.3 %all-reduce = (s32[8,8]{1,0:T(8,128)}, s32[8,8]{1,0:T(8,128)}) all-reduce(s32[8,8]{1,0:T(8,128)S(1)} %get-tuple-element.8, s32[8,8]{1,0:T(8,128)S(1)} %get-tuple-element.7), channel_id=1, replica_groups=mesh['tm'=4,'line'=8] {'line'}, use_global_device_ids=true, to_apply=%region_0.1 | all-reduce | flops 128 | bytes 1024 | tf_op jit(solution)/shard_map/psum | solution.py:307
  15.6 0.0 collective-permute-done.1.refs_4_
  15.6 0.0 copy-start
  15.6 0.0 collective-permute-done.refs_3_
  15.6 0.0 copy-start.1
  15.6 0.7 %collective-permute-done.2.refs_5_ = bf16[32,4096]{1,0:T(8,128)(2,1)S(1)} collective-permute-done((bf16[32,4096]{1,0:T(8,128)(2,1)}, bf16[32,4096]{1,0:T(8,128)(2,1)S(1)}, u32[]{:S(2)}, u32[]{:S(2)}) %collective-permute-start.2) | collective-permute-done | bytes 262176 | tf_op jit(solution)/shard_map/ppermute | solution.py:297
  16.3 0.0 copy-start.2
  16.3 0.0 copy-done
  16.3 0.1 copy-done.1
  16.4 0.6 %copy-done.2 = bf16[32,4096]{1,0:T(8,128)(2,1)} copy-done((bf16[32,4096]{1,0:T(8,128)(2,1)}, bf16[32,4096]{1,0:T(8,128)(2,1)S(1)}, u32[]{:S(2)}) %copy-start.2) | copy-done | bytes 262168
  17.0 9.5 %shard_map.91 = bf16[32,32,1024]{2,1,0:T(8,128)(2,1)} custom-call(s32[8,8]{1,0:T(8,128)} %get-tuple-element.5.refs_0_, s32[8,8]{1,0:T(8,128)} %get-tuple-element.6.refs_1_, bf16[32,4096]{1,0:T(8,128)(2,1)} %refs_2_.1, bf16[32,4096]{1,0:T(8,128)(2,1)} %copy-done.1, bf16[32,4096]{1,0:T(8,128)(2,1)} %copy-done, bf16[32,4096]{1,0:T(8,128)(2,1)} %copy-done.2, ...), custom_call_target="tpu_custom_call" | custom-call | flops 4026531840 | bytes 3145728 | tf_op jit(solution)/shard_map/pallas_call | solution.py:265
  (1 shorter events, 0.0 us)
Async XLA Ops:
  0.0 15.6 %collective-permute-start.1 = (bf16[32,4096]{1,0:T(8,128)(2,1)}, bf16[32,4096]{1,0:T(8,128)(2,1)S(1)}, u32[]{:S(2)}, u32[]{:S(2)}) collective-permute-start(bf16[32,4096]{1,0:T(8,128)(2,1)} %refs_2_.1), channel_id=1, source_target_pairs={{16,0},{24,8},{0,16},{8,24},{17,1},{25,9},{1,17},{9,25},{18,2},{26... | collective-permute-start | bytes 786440 | tf_op jit(solution)/shard_map/ppermute | solution.py:297
  3.0 12.6 %collective-permute-start = (bf16[32,4096]{1,0:T(8,128)(2,1)}, bf16[32,4096]{1,0:T(8,128)(2,1)S(1)}, u32[]{:S(2)}, u32[]{:S(2)}) collective-permute-start(bf16[32,4096]{1,0:T(8,128)(2,1)} %refs_2_.1), channel_id=1, source_target_pairs={{8,0},{0,8},{24,16},{16,24},{9,1},{1,9},{25,17},{17,25},{10,2},{2,... | collective-permute-start | bytes 786440 | tf_op jit(solution)/shard_map/ppermute | solution.py:297
  4.5 11.8 %collective-permute-start.2 = (bf16[32,4096]{1,0:T(8,128)(2,1)}, bf16[32,4096]{1,0:T(8,128)(2,1)S(1)}, u32[]{:S(2)}, u32[]{:S(2)}) collective-permute-start(bf16[32,4096]{1,0:T(8,128)(2,1)} %refs_2_.1), channel_id=1, source_target_pairs={{24,0},{16,8},{8,16},{0,24},{25,1},{17,9},{9,17},{1,25},{26,2},{18... | collective-permute-start | bytes 786440 | tf_op jit(solution)/shard_map/ppermute | solution.py:297
  15.6 0.7 %copy-start = (bf16[32,4096]{1,0:T(8,128)(2,1)}, bf16[32,4096]{1,0:T(8,128)(2,1)S(1)}, u32[]{:S(2)}) copy-start(bf16[32,4096]{1,0:T(8,128)(2,1)S(1)} %collective-permute-done.1.refs_4_) | copy-start | bytes 786436
  15.6 0.8 %copy-start.1 = (bf16[32,4096]{1,0:T(8,128)(2,1)}, bf16[32,4096]{1,0:T(8,128)(2,1)S(1)}, u32[]{:S(2)}) copy-start(bf16[32,4096]{1,0:T(8,128)(2,1)S(1)} %collective-permute-done.refs_3_) | copy-start | bytes 786436
  16.3 0.7 %copy-start.2 = (bf16[32,4096]{1,0:T(8,128)(2,1)}, bf16[32,4096]{1,0:T(8,128)(2,1)S(1)}, u32[]{:S(2)}) copy-start(bf16[32,4096]{1,0:T(8,128)(2,1)S(1)} %collective-permute-done.2.refs_5_) | copy-start | bytes 786436

commit v12 on v11

--- a/solution.py
+++ b/solution.py
@@ -16,33 +16,40 @@
 
 def make_tables(window, shots):
     half = window // 2
-    quarter = half // 2
-    times = np.arange(half)
-    freqs = np.concatenate([np.arange(0, half, 2), np.arange(1, half, 2)])
+    quarter, eighth = window // 4, window // 8
+    bf16 = ml_dtypes.bfloat16
 
     def waves(rows, columns, period):
         phase = (rows[:, None] * columns[None, :] % period) * (2.0 * math.pi / period)
         return np.cos(phase), np.sin(phase)
 
-    bf16 = ml_dtypes.bfloat16
-    cosine, sine = waves(times, freqs, window)
-    forward = np.stack(
-        [
-            np.concatenate([cosine[:, cut], -sine[:, cut]], axis=1)
-            for cut in (slice(0, quarter), slice(quarter, half))
-        ]
-    ).astype(bf16)
-    gain = np.where(freqs == 0, 0.5, 1.0)[:, None] * (2.0 / (window * shots))
-    inverse = np.stack(
-        [
-            np.concatenate([gain[cut] * cosine.T[cut], -gain[cut] * sine.T[cut]], axis=0)
-            for cut in (slice(0, quarter), slice(quarter, half))
-        ]
-    ).astype(bf16)
+    classes = [np.arange(first, half, 4) for first in (0, 2)]
+    classes += [
+        np.concatenate([np.arange(first, half, 8) for first in pair]) for pair in ((1, 7), (3, 5))
+    ]
+    freqs = np.concatenate(classes)
+    forward, inverse = [], []
+    for part, found in enumerate(classes):
+        gain = np.where(found == 0, 0.5, 1.0)[:, None] * (2.0 / (window * shots))
+        if part < 2:
+            cosine, sine = waves(np.arange(quarter), found, window)
+            forward.append(np.concatenate([cosine, -sine], axis=1))
+            inverse.append(np.concatenate([gain * cosine.T, -gain * sine.T], axis=0))
+            continue
+        cosine, sine = waves(np.arange(eighth), found, window)
+        turn = np.where(found % 8 < 4, 1.0, -1.0)
+        way = -turn if part == 2 else turn
+        forward.append(np.block([[cosine, -sine], [way * sine, way * cosine]]))
+        inverse.append(
+            np.block(
+                [
+                    [gain * cosine.T, turn[:, None] * gain * sine.T],
+                    [-gain * sine.T, turn[:, None] * gain * cosine.T],
+                ]
+            )
+        )
+    forward, inverse = np.stack(forward).astype(bf16), np.stack(inverse).astype(bf16)
     turn_cos, turn_sin = waves(np.arange(shots), np.arange(shots), shots)
-    forward, inverse = [
-        table.reshape(2, half, half // LANES, LANES).swapaxes(1, 2) for table in (forward, inverse)
-    ]
     over_shots = np.block([[turn_cos, turn_sin], [-turn_sin, turn_cos]]).astype(bf16)
     back_rows = np.stack(
         [
@@ -61,9 +68,10 @@
     return (index + away) % count
 
 
-def gather_kernel(peers, recs, *refs):
+def gather_kernel(aways, recs, *refs):
     ticks, places, *refs = refs
     share = ticks.shape[1]
+    peers = len(aways)
     traces, refs = refs[:peers], refs[peers:]
     table_refs, out, loaded, refs = refs[:6], refs[6], refs[7:14], refs[14:]
     own, forward, inverse, order, flags, over_shots, back_rows = loaded
@@ -75,7 +83,8 @@
     pitch = recs + 1
     wide = window // LANES
     mid = wide // 2
-    arms = mid // 2
+    parts = range(mid)
+    side = math.sqrt(0.5)
     per_block = block_len // LANES
     f32, bf16 = jnp.float32, jnp.bfloat16
     here = lax.axis_index("tm")
@@ -88,7 +97,7 @@
         table_copies[index].start()
 
     table_copies[0].wait()
-    for away, block in enumerate((own, *traces[1:])):
+    for away, block in zip(aways, (own, *traces[1:])):
         base = partner(here, away, peers) * per_block
         for tile in range(per_block):
             tiles[base + tile] = block[:, tile * LANES : (tile + 1) * LANES]
@@ -105,93 +114,97 @@
         early = lane < within.astype(jnp.int16)
         piece = [jnp.where(early, piece[tile + 1], piece[tile]) for tile in range(wide)]
         turn = (LANES - within) & (LANES - 1)
-        sums = [pltpu.roll(piece[tile] + piece[tile + mid], turn, 1) for tile in range(mid)]
-        gaps = [pltpu.roll(piece[tile] - piece[tile + mid], turn, 1) for tile in range(mid)]
-        return sums, gaps
+        sums = [piece[tile] + piece[tile + mid] for tile in range(mid)]
+        gaps = [piece[tile] - piece[tile + mid] for tile in range(mid)]
+        near = (gaps[1] - gaps[3]) * bf16(side)
+        far = (gaps[1] + gaps[3]) * bf16(side)
+        pairs = [
+            (sums[0] + sums[2], sums[1] + sums[3]),
+            (sums[0] - sums[2], sums[1] - sums[3]),
+            (gaps[0] + near, gaps[2] + far),
+            (gaps[0] - near, gaps[2] - far),
+        ]
+        return [[pltpu.roll(tile, turn, 1) for tile in pair] for pair in pairs]
 
     def cut_block(block, rows):
         for item in range(BLOCK):
-            for part, tiles_of in enumerate(cut(block * BLOCK + item, rows)):
-                for tile in range(mid):
-                    folds[block % 2, part, tile, item * recs : (item + 1) * recs] = tiles_of[tile]
-
-    def product(left, right, part):
-        return jnp.dot(
-            jnp.concatenate(left, axis=1),
-            jnp.concatenate([right[part, tile] for tile in range(mid)], axis=1),
-            preferred_element_type=f32,
-        )
+            for part, pair in enumerate(cut(block * BLOCK + item, rows)):
+                for side_of, tile in enumerate(pair):
+                    folds[block % 2, part, side_of, item * recs : (item + 1) * recs] = tile
 
     def columns(tile):
         return slice(tile * LANES, (tile + 1) * LANES)
 
     def transform_block(block):
-        for part in range(2):
-            panel = [folds[block % 2, part, tile] for tile in range(mid)]
-            found = product(panel, forward, part)
+        for part in parts:
+            panel = jnp.concatenate([folds[block % 2, part, side_of] for side_of in range(2)], axis=1)
+            found = jnp.dot(panel, forward[part], preferred_element_type=f32)
             for item in range(BLOCK):
                 row = (block * BLOCK + item) * pitch
-                for tile in range(mid):
-                    spectra[part * mid + tile, row : row + recs] = found[
-                        item * recs : (item + 1) * recs, columns(tile)
+                for side_of in range(2):
+                    spectra[2 * part + side_of, row : row + recs] = found[
+                        item * recs : (item + 1) * recs, columns(side_of)
                     ]
 
     def over(rec, keep):
         at = pl.ds(rec, shots, stride=pitch)
         stacked = jnp.concatenate(
             [
-                jnp.concatenate(
-                    [
-                        spectra[part * mid + tile, at].astype(bf16)
-                        for part in range(2)
-                        for tile in which
-                    ],
-                    axis=1,
-                )
-                for which in (range(arms), range(arms, mid))
+                jnp.concatenate([spectra[2 * part + side_of, at].astype(bf16) for part in parts], axis=1)
+                for side_of in range(2)
             ],
             axis=0,
         )
         waves = jnp.dot(over_shots[...], stacked, preferred_element_type=f32)
         masked = jnp.concatenate([waves[:shots] * keep, waves[shots:] * keep], axis=0).astype(bf16)
-        for tile in range(mid):
-            waved[tile, rec] = masked[:, columns(tile)]
+        for part in parts:
+            waved[part, rec] = masked[:, columns(part)]
 
     def under(rec, back):
-        masked = jnp.concatenate([waved[tile, rec] for tile in range(mid)], axis=1)
+        masked = jnp.concatenate([waved[part, rec] for part in parts], axis=1)
         again = jnp.dot(back, masked, preferred_element_type=f32)
         to = pl.ds(rec, slots, stride=pitch)
-        for part in range(2):
-            for arm in range(arms):
-                at = columns(part * arms + arm)
-                mixed[part * mid + arm, to] = again[:slots, at]
-                mixed[part * mid + arms + arm, to] = again[slots:, at]
+        for part in parts:
+            mixed[2 * part, to] = again[:slots, columns(part)]
+            mixed[2 * part + 1, to] = again[slots:, columns(part)]
 
     group = min(slots, 256 // recs)
     out_copies = []
 
     def restore(chunk, first):
-        even, odd = [
-            product(
-                [
-                    jnp.concatenate(
-                        [
-                            mixed[part * mid + tile, slot * pitch : slot * pitch + recs].astype(bf16)
-                            for slot in range(first, first + group)
-                        ],
-                        axis=0,
-                    )
-                    for tile in range(mid)
-                ],
-                inverse,
-                part,
+        found = []
+        for part in parts:
+            panel = [
+                jnp.concatenate(
+                    [
+                        mixed[2 * part + side_of, slot * pitch : slot * pitch + recs].astype(bf16)
+                        for slot in range(first, first + group)
+                    ],
+                    axis=0,
+                )
+                for side_of in range(2)
+            ]
+            found.append(
+                jnp.dot(
+                    jnp.concatenate(panel, axis=1), inverse[part], preferred_element_type=f32
+                )
             )
-            for part in range(2)
+        plus, minus = found[0] + found[1], found[0] - found[1]
+        even = [plus[:, :LANES], plus[:, LANES:], minus[:, :LANES], minus[:, LANES:]]
+        total, gap = found[2] + found[3], found[2] - found[3]
+        real_gap, imag_sum = gap[:, :LANES], total[:, LANES:]
+        odd = [
+            total[:, :LANES],
+            (real_gap - imag_sum) * side,
+            -gap[:, LANES:],
+            (real_gap + imag_sum) * -side,
         ]
         rows = slice(chunk * recs, (chunk + 1) * recs)
-        early, late = (even + odd).astype(bf16), (even - odd).astype(bf16)
-        ready[first : first + group, rows, :half] = early.reshape(group, recs, half)
-        ready[first : first + group, rows, half:] = late.reshape(group, recs, half)
+        for tile in range(mid):
+            for to, value in ((tile, even[tile] + odd[tile]), (tile + mid, even[tile] - odd[tile])):
+                ready[first : first + group, rows, columns(to)] = value.astype(bf16).reshape(
+                    group, recs, LANES
+                )
         block = (pl.ds(first, group), pl.ds(chunk * recs, recs))
         copy = pltpu.make_async_copy(
             ready.at[block], out.at[block], out_sem.at[chunk, first // group]
@@ -242,7 +255,7 @@
         copy.wait()
 
 
-def filter_gathers(codes, traces, flags, tables):
+def filter_gathers(codes, traces, aways, flags, tables):
     forward, inverse, over_shots, back_rows, order = tables
     peers = len(traces)
     rec_rows, block_len = traces[0].shape
@@ -263,7 +276,7 @@
     bf16 = jnp.bfloat16
     shared = [forward, inverse, order, flags, over_shots, back_rows]
     return pl.pallas_call(
-        functools.partial(gather_kernel, peers, recs),
+        functools.partial(gather_kernel, aways, recs),
         out_shape=jax.ShapeDtypeStruct((slots, rec_rows, window), bf16),
         in_specs=[smem, smem, hbm] + [vmem] * (peers - 1) + [hbm] * 6,
         out_specs=hbm,
@@ -271,7 +284,7 @@
             pltpu.VMEM((rec_rows, block_len), bf16),
             *[pltpu.VMEM(table.shape, table.dtype) for table in shared],
             pltpu.VMEM(((total + window) // LANES, rec_rows, LANES), bf16),
-            pltpu.VMEM((2, 2, half // LANES, BLOCK * recs, LANES), bf16),
+            pltpu.VMEM((2, half // LANES, 2, BLOCK * recs, LANES), bf16),
             pltpu.VMEM((window // LANES, shots * (recs + 1), LANES), jnp.float32),
             pltpu.VMEM((half // LANES, recs, 2 * shots, LANES), bf16),
             pltpu.VMEM((window // LANES, slots * (recs + 1), LANES), jnp.float32),
@@ -293,13 +306,15 @@
     tables = make_tables(2 * half, shots)
     peers = lax.axis_size("tm")
     lines = lax.axis_size("line")
+    farthest = list(range(peers - 1, 0, -1))
+    aways = [0, *farthest[1::-1], *farthest[2:]]
     traces = [station_traces] + [
         lax.ppermute(
             station_traces,
             "tm",
             [(partner(index, away, peers), index) for index in range(peers)],
         )
-        for away in range(1, peers)
+        for away in aways[1:]
     ]
     share = shots // lines
     row = lax.broadcasted_iota(jnp.int32, (lines, share), 0)
@@ -307,7 +322,7 @@
     codes = lax.psum(
         [jnp.where(own, part[None], 0) for part in (shot_onset_ticks, span_place_index)], "line"
     )
-    return filter_gathers(codes, traces, spectral_keep_flags, tables)
+    return filter_gathers(codes, traces, aways, spectral_keep_flags, tables)
 
 
 def solution(mesh):

time: 26.6 us -> 25.6 us (0.962)
  Pallas kernels: 9.51 us -> 8.45 us
    pallas_call x1, Pallas kernels: 9.51 us -> 8.45 us  [filter_gathers(): pl.pallas_call(functools.partial(gather_kernel, aways, recs), out_shape=j...]
  transfers between devices with their start and end apart: 3 -> 3, of which waited for: 1 -> 2; matrix products, arithmetic and copies ran while one was open for 3% -> 3% of each run, Pallas kernels for 0% -> 0%
where the time goes in v12:
time: 25.6 us; the launch traced here: 25.5 us
  blocking collectives  10.3 us (40%)
  Pallas kernels  8.45 us (33%)
  starting transfers between devices  4.46 us (17%)
  waiting for transfers between devices  0.76 us (3%)
  other arithmetic  0.75 us (3%)
  local copies, waits for them, and re-layouts  0.69 us (3%)
    psum x1, blocking collectives, on_device(): lax.psum([jnp.where(own, part[None], 0) for part in (shot_onset_ticks, sp...  10.3 us
    pallas_call x1, Pallas kernels, filter_gathers(): pl.pallas_call(functools.partial(gather_kernel, aways, recs), out_shape=j...  8.45 us
    ppermute x3, starting transfers between devices, on_device(): lax.ppermute(station_traces, 'tm', [(partner(index, away, peers), index)...  4.46 us
    ppermute x3, waiting for transfers between devices, on_device(): lax.ppermute(station_traces, 'tm', [(partner(index, away, peers), index)...  0.76 us
    select_n x1, other arithmetic, on_device(): jnp.where(own, part[None], 0)  0.74 us
    unnamed x6, local copies, waits for them, and re-layouts  0.69 us
  transfers between devices with their start and end apart: 3, of which 2 were waited for; matrix products, arithmetic and copies ran while one was open for 3% of the time, Pallas kernels for 0%

profile of v12, /device:TPU:0, one launch (start us, length us, event | category | flops | bytes accessed | tf_op | source)
XLA Modules:
  0.0 25.5 jit_solution(10828422433344276663)
XLA Ops:
  0.0 3.9 %collective-permute-start.1 = (bf16[32,4096]{1,0:T(8,128)(2,1)}, bf16[32,4096]{1,0:T(8,128)(2,1)S(1)}, u32[]{:S(2)}, u32[]{:S(2)}) collective-permute-start(bf16[32,4096]{1,0:T(8,128)(2,1)} %refs_2_.1), channel_id=1, source_target_pairs={{24,0},{16,8},{8,16},{0,24},{25,1},{17,9},{9,17},{1,25},{26,2},{18... | collective-permute-start | bytes 786440 | tf_op jit(solution)/shard_map/ppermute | solution.py:312
  3.9 0.5 %collective-permute-start = (bf16[32,4096]{1,0:T(8,128)(2,1)}, bf16[32,4096]{1,0:T(8,128)(2,1)S(1)}, u32[]{:S(2)}, u32[]{:S(2)}) collective-permute-start(bf16[32,4096]{1,0:T(8,128)(2,1)} %refs_2_.1), channel_id=1, source_target_pairs={{16,0},{24,8},{0,16},{8,24},{17,1},{25,9},{1,17},{9,25},{18,2},{26... | collective-permute-start | bytes 786440 | tf_op jit(solution)/shard_map/ppermute | solution.py:312
  4.4 0.1 collective-permute-start.2
  4.5 0.7 %broadcast_select_fusion = (s32[8,8]{1,0:T(8,128)S(1)}, s32[8,8]{1,0:T(8,128)S(1)}) fusion(s32[8]{0:T(128)} %param.11, pred[8]{0:T(512)(128)(4,1)S(1)} %iota_compare_fusion, s32[8]{0:T(128)} %param.10), kind=kLoop, calls=%fused_computation | loop fusion | flops 128 | bytes 584 | tf_op jit(solution)/shard_map/jit(_where)/select_n | solution.py:323
  5.2 10.3 %all-reduce = (s32[8,8]{1,0:T(8,128)}, s32[8,8]{1,0:T(8,128)}) all-reduce(s32[8,8]{1,0:T(8,128)S(1)} %get-tuple-element.8, s32[8,8]{1,0:T(8,128)S(1)} %get-tuple-element.7), channel_id=1, replica_groups=mesh['tm'=4,'line'=8] {'line'}, use_global_device_ids=true, to_apply=%region_0.1 | all-reduce | flops 128 | bytes 1024 | tf_op jit(solution)/shard_map/psum | solution.py:322
  15.6 0.0 collective-permute-done.1.refs_4_
  15.6 0.0 copy-start
  15.6 0.5 %collective-permute-done.refs_3_ = bf16[32,4096]{1,0:T(8,128)(2,1)S(1)} collective-permute-done((bf16[32,4096]{1,0:T(8,128)(2,1)}, bf16[32,4096]{1,0:T(8,128)(2,1)S(1)}, u32[]{:S(2)}, u32[]{:S(2)}) %collective-permute-start) | collective-permute-done | bytes 262176 | tf_op jit(solution)/shard_map/ppermute | solution.py:312
  16.0 0.0 copy-start.1
  16.0 0.3 %collective-permute-done.2.refs_5_ = bf16[32,4096]{1,0:T(8,128)(2,1)S(1)} collective-permute-done((bf16[32,4096]{1,0:T(8,128)(2,1)}, bf16[32,4096]{1,0:T(8,128)(2,1)S(1)}, u32[]{:S(2)}, u32[]{:S(2)}) %collective-permute-start.2) | collective-permute-done | bytes 262176 | tf_op jit(solution)/shard_map/ppermute | solution.py:312
  16.3 0.0 copy-start.2
  16.3 0.0 copy-done
  16.3 0.4 %copy-done.1 = bf16[32,4096]{1,0:T(8,128)(2,1)} copy-done((bf16[32,4096]{1,0:T(8,128)(2,1)}, bf16[32,4096]{1,0:T(8,128)(2,1)S(1)}, u32[]{:S(2)}) %copy-start.1) | copy-done | bytes 262168
  16.7 0.3 %copy-done.2 = bf16[32,4096]{1,0:T(8,128)(2,1)} copy-done((bf16[32,4096]{1,0:T(8,128)(2,1)}, bf16[32,4096]{1,0:T(8,128)(2,1)S(1)}, u32[]{:S(2)}) %copy-start.2) | copy-done | bytes 262168
  17.0 8.5 %shard_map.91 = bf16[32,32,1024]{2,1,0:T(8,128)(2,1)} custom-call(s32[8,8]{1,0:T(8,128)} %get-tuple-element.5.refs_0_, s32[8,8]{1,0:T(8,128)} %get-tuple-element.6.refs_1_, bf16[32,4096]{1,0:T(8,128)(2,1)} %refs_2_.1, bf16[32,4096]{1,0:T(8,128)(2,1)} %copy-done.1, bf16[32,4096]{1,0:T(8,128)(2,1)} %copy-done, bf16[32,4096]{1,0:T(8,128)(2,1)} %copy-done.2, ...), custom_call_target="tpu_custom_call" | custom-call | flops 4026531840 | bytes 3145728 | tf_op jit(solution)/shard_map/pallas_call | solution.py:278
  (1 shorter events, 0.0 us)
Async XLA Ops:
  0.0 15.6 %collective-permute-start.1 = (bf16[32,4096]{1,0:T(8,128)(2,1)}, bf16[32,4096]{1,0:T(8,128)(2,1)S(1)}, u32[]{:S(2)}, u32[]{:S(2)}) collective-permute-start(bf16[32,4096]{1,0:T(8,128)(2,1)} %refs_2_.1), channel_id=1, source_target_pairs={{24,0},{16,8},{8,16},{0,24},{25,1},{17,9},{9,17},{1,25},{26,2},{18... | collective-permute-start | bytes 786440 | tf_op jit(solution)/shard_map/ppermute | solution.py:312
  3.9 12.1 %collective-permute-start = (bf16[32,4096]{1,0:T(8,128)(2,1)}, bf16[32,4096]{1,0:T(8,128)(2,1)S(1)}, u32[]{:S(2)}, u32[]{:S(2)}) collective-permute-start(bf16[32,4096]{1,0:T(8,128)(2,1)} %refs_2_.1), channel_id=1, source_target_pairs={{16,0},{24,8},{0,16},{8,24},{17,1},{25,9},{1,17},{9,25},{18,2},{26... | collective-permute-start | bytes 786440 | tf_op jit(solution)/shard_map/ppermute | solution.py:312
  4.4 11.9 %collective-permute-start.2 = (bf16[32,4096]{1,0:T(8,128)(2,1)}, bf16[32,4096]{1,0:T(8,128)(2,1)S(1)}, u32[]{:S(2)}, u32[]{:S(2)}) collective-permute-start(bf16[32,4096]{1,0:T(8,128)(2,1)} %refs_2_.1), channel_id=1, source_target_pairs={{8,0},{0,8},{24,16},{16,24},{9,1},{1,9},{25,17},{17,25},{10,2},{2,... | collective-permute-start | bytes 786440 | tf_op jit(solution)/shard_map/ppermute | solution.py:312
  15.6 0.8 %copy-start = (bf16[32,4096]{1,0:T(8,128)(2,1)}, bf16[32,4096]{1,0:T(8,128)(2,1)S(1)}, u32[]{:S(2)}) copy-start(bf16[32,4096]{1,0:T(8,128)(2,1)S(1)} %collective-permute-done.1.refs_4_) | copy-start | bytes 786436
  16.0 0.7 %copy-start.1 = (bf16[32,4096]{1,0:T(8,128)(2,1)}, bf16[32,4096]{1,0:T(8,128)(2,1)S(1)}, u32[]{:S(2)}) copy-start(bf16[32,4096]{1,0:T(8,128)(2,1)S(1)} %collective-permute-done.refs_3_) | copy-start | bytes 786436
  16.3 0.7 %copy-start.2 = (bf16[32,4096]{1,0:T(8,128)(2,1)}, bf16[32,4096]{1,0:T(8,128)(2,1)S(1)}, u32[]{:S(2)}) copy-start(bf16[32,4096]{1,0:T(8,128)(2,1)S(1)} %collective-permute-done.2.refs_5_) | copy-start | bytes 786436

commit v13 on v12

--- a/solution.py
+++ b/solution.py
@@ -69,8 +69,8 @@
 
 
 def gather_kernel(aways, recs, *refs):
-    ticks, places, *refs = refs
-    share = ticks.shape[1]
+    codes, *refs = refs
+    share = codes.shape[2]
     peers = len(aways)
     traces, refs = refs[:peers], refs[peers:]
     table_refs, out, loaded, refs = refs[:6], refs[6], refs[7:14], refs[14:]
@@ -96,8 +96,9 @@
     for index in (0, 6, 1, 4, 3, 5, 2):
         table_copies[index].start()
 
-    table_copies[0].wait()
-    for away, block in zip(aways, (own, *traces[1:])):
+    for away, block in [*zip(aways[1:], traces[1:]), (0, own)]:
+        if away == 0:
+            table_copies[0].wait()
         base = partner(here, away, peers) * per_block
         for tile in range(per_block):
             tiles[base + tile] = block[:, tile * LANES : (tile + 1) * LANES]
@@ -107,7 +108,7 @@
     lane = lax.broadcasted_iota(jnp.int16, (recs, LANES), 1)
 
     def cut(shot, rows):
-        tick = ticks[shot // share, shot % share]
+        tick = codes[0, shot // share, shot % share]
         first = lax.shift_right_logical(tick, LANES.bit_length() - 1)
         within = tick & (LANES - 1)
         piece = [tiles[first + tile, rows] for tile in range(wide + 1)]
@@ -156,7 +157,7 @@
             axis=0,
         )
         waves = jnp.dot(over_shots[...], stacked, preferred_element_type=f32)
-        masked = jnp.concatenate([waves[:shots] * keep, waves[shots:] * keep], axis=0).astype(bf16)
+        masked = waves.astype(bf16) * keep
         for part in parts:
             waved[part, rec] = masked[:, columns(part)]
 
@@ -215,9 +216,9 @@
     shot_lane = lax.broadcasted_iota(jnp.int32, (1, shots), 1)
     place_all = jnp.full((1, shots), -1, jnp.int32)
     for shot in range(shots):
-        tick = ticks[shot // share, shot % share]
+        tick = codes[0, shot // share, shot % share]
         mine = (tick >= here * block_len) & (tick < (here + 1) * block_len)
-        place = jnp.where(mine, places[shot // share, shot % share], -1)
+        place = jnp.where(mine, codes[1, shot // share, shot % share], -1)
         place_all = jnp.where(shot_lane == shot, place, place_all)
     slot_row = lax.broadcasted_iota(jnp.int32, (slots, shots), 0)
     owned = (slot_row == place_all).astype(f32).astype(bf16)
@@ -237,12 +238,13 @@
             if block + 1 < blocks:
                 cut_block(block + 1, rows)
             transform_block(block)
-        if chunk == 0:
-            for index in (3, 4, 5):
-                table_copies[index].wait()
-            keep = jnp.dot(
-                flags[...].astype(f32).astype(bf16), order[...], preferred_element_type=f32
-            )
+            if chunk == 0 and block == 0:
+                for index in (3, 4, 5):
+                    table_copies[index].wait()
+                kept = jnp.dot(
+                    flags[...].astype(f32).astype(bf16), order[...], preferred_element_type=f32
+                ).astype(bf16)
+                keep = jnp.concatenate([kept, kept], axis=0)
         for rec in range(recs):
             over(rec, keep)
         for rec in range(recs):
@@ -278,7 +280,7 @@
     return pl.pallas_call(
         functools.partial(gather_kernel, aways, recs),
         out_shape=jax.ShapeDtypeStruct((slots, rec_rows, window), bf16),
-        in_specs=[smem, smem, hbm] + [vmem] * (peers - 1) + [hbm] * 6,
+        in_specs=[smem, hbm] + [vmem] * (peers - 1) + [hbm] * 6,
         out_specs=hbm,
         scratch_shapes=[
             pltpu.VMEM((rec_rows, block_len), bf16),
@@ -298,7 +300,7 @@
             bytes_accessed=2 * rec_rows * (total + slots * window),
             transcendentals=0,
         ),
-    )(*codes, *traces, *shared)
+    )(codes, *traces, *shared)
 
 
 def on_device(station_traces, shot_onset_ticks, span_place_index, spectral_keep_flags):
@@ -306,8 +308,7 @@
     tables = make_tables(2 * half, shots)
     peers = lax.axis_size("tm")
     lines = lax.axis_size("line")
-    farthest = list(range(peers - 1, 0, -1))
-    aways = [0, *farthest[1::-1], *farthest[2:]]
+    aways = list(range(peers))
     traces = [station_traces] + [
         lax.ppermute(
             station_traces,
@@ -316,12 +317,11 @@
         )
         for away in aways[1:]
     ]
-    share = shots // lines
-    row = lax.broadcasted_iota(jnp.int32, (lines, share), 0)
-    own = row == lax.axis_index("line")
-    codes = lax.psum(
-        [jnp.where(own, part[None], 0) for part in (shot_onset_ticks, span_place_index)], "line"
-    )
+    shape = (2, lines, shots // lines)
+    which = lax.broadcasted_iota(jnp.int32, shape, 0)
+    line = lax.broadcasted_iota(jnp.int32, shape, 1)
+    both = jnp.where(which == 0, shot_onset_ticks, span_place_index)
+    codes = lax.psum(jnp.where(line == lax.axis_index("line"), both, 0), "line")
     return filter_gathers(codes, traces, aways, spectral_keep_flags, tables)
 
 

time: 25.6 us -> 25.6 us (level)
  transfers between devices with their start and end apart: 3 -> 3, of which waited for: 2 -> 1; matrix products, arithmetic and copies ran while one was open for 3% -> 3% of each run, Pallas kernels for 0% -> 0%
where the time goes in v13:
time: 25.6 us; the launch traced here: 25.4 us
  blocking collectives  10.4 us (41%)
  Pallas kernels  8.33 us (33%)
  starting transfers between devices  4.46 us (17%)
  local copies, waits for them, and re-layouts  0.78 us (3%)
  other arithmetic  0.76 us (3%)
  waiting for transfers between devices  0.69 us (3%)
    psum x1, blocking collectives, on_device(): codes = lax.psum(jnp.where(line == lax.axis_index('line'), both, 0), 'line')  10.4 us
    pallas_call x1, Pallas kernels, filter_gathers(): pl.pallas_call(functools.partial(gather_kernel, aways, recs), out_shape=j...  8.33 us
    ppermute x3, starting transfers between devices, on_device(): lax.ppermute(station_traces, 'tm', [(partner(index, away, peers), index)...  4.46 us
    unnamed x6, local copies, waits for them, and re-layouts  0.78 us
    select_n x1, other arithmetic, on_device(): codes = lax.psum(jnp.where(line == lax.axis_index('line'), both, 0), 'line')  0.75 us
    ppermute x3, waiting for transfers between devices, on_device(): lax.ppermute(station_traces, 'tm', [(partner(index, away, peers), index)...  0.69 us
  transfers between devices with their start and end apart: 3, of which 1 were waited for; matrix products, arithmetic and copies ran while one was open for 3% of the time, Pallas kernels for 0%

profile of v13, /device:TPU:0, one launch (start us, length us, event | category | flops | bytes accessed | tf_op | source)
XLA Modules:
  0.0 25.4 jit_solution(14465303739126240289)
XLA Ops:
  0.0 3.0 %collective-permute-start.1 = (bf16[32,4096]{1,0:T(8,128)(2,1)}, bf16[32,4096]{1,0:T(8,128)(2,1)S(1)}, u32[]{:S(2)}, u32[]{:S(2)}) collective-permute-start(bf16[32,4096]{1,0:T(8,128)(2,1)} %refs_1_.1), channel_id=1, source_target_pairs={{16,0},{24,8},{0,16},{8,24},{17,1},{25,9},{1,17},{9,25},{18,2},{26... | collective-permute-start | bytes 786440 | tf_op jit(solution)/shard_map/ppermute | solution.py:313
  3.0 1.5 %collective-permute-start = (bf16[32,4096]{1,0:T(8,128)(2,1)}, bf16[32,4096]{1,0:T(8,128)(2,1)S(1)}, u32[]{:S(2)}, u32[]{:S(2)}) collective-permute-start(bf16[32,4096]{1,0:T(8,128)(2,1)} %refs_1_.1), channel_id=1, source_target_pairs={{8,0},{0,8},{24,16},{16,24},{9,1},{1,9},{25,17},{17,25},{10,2},{2,... | collective-permute-start | bytes 786440 | tf_op jit(solution)/shard_map/ppermute | solution.py:313
  4.5 0.0 collective-permute-start.2
  4.5 0.7 %select_select_fusion = s32[2,8,8]{2,1,0:T(8,128)S(1)} fusion(s32[8]{0:T(128)} %param.11, s32[8]{0:T(128)} %param.10, pred[2]{0:T(512)(128)(4,1)S(1)} %iota_compare_fusion, pred[8]{0:T(512)(128)(4,1)S(1)} %iota_compare_fusion.1), kind=kLoop, calls=%fused_computation | loop fusion | flops 256 | bytes 586 | tf_op jit(solution)/shard_map/jit(_where)/select_n | solution.py:324
  5.2 10.4 %psum.7.refs_0_ = s32[2,8,8]{2,1,0:T(8,128)} all-reduce(s32[2,8,8]{2,1,0:T(8,128)S(1)} %select_select_fusion), channel_id=1, replica_groups=mesh['tm'=4,'line'=8] {'line'}, use_global_device_ids=true, to_apply=%region_0.1 | all-reduce | flops 128 | bytes 1024 | tf_op jit(solution)/shard_map/psum | solution.py:324
  15.6 0.0 collective-permute-done.1.refs_3_
  15.6 0.0 copy-start
  15.6 0.0 collective-permute-done.refs_2_
  15.6 0.0 copy-start.1
  15.6 0.7 %collective-permute-done.2.refs_4_ = bf16[32,4096]{1,0:T(8,128)(2,1)S(1)} collective-permute-done((bf16[32,4096]{1,0:T(8,128)(2,1)}, bf16[32,4096]{1,0:T(8,128)(2,1)S(1)}, u32[]{:S(2)}, u32[]{:S(2)}) %collective-permute-start.2) | collective-permute-done | bytes 262176 | tf_op jit(solution)/shard_map/ppermute | solution.py:313
  16.3 0.0 copy-done
  16.3 0.1 copy-done.1
  16.4 0.0 copy-start.2
  16.4 0.7 %copy-done.2 = bf16[32,4096]{1,0:T(8,128)(2,1)} copy-done((bf16[32,4096]{1,0:T(8,128)(2,1)}, bf16[32,4096]{1,0:T(8,128)(2,1)S(1)}, u32[]{:S(2)}) %copy-start.2) | copy-done | bytes 262168
  17.1 8.3 %shard_map.91 = bf16[32,32,1024]{2,1,0:T(8,128)(2,1)} custom-call(s32[2,8,8]{2,1,0:T(8,128)} %psum.7.refs_0_, bf16[32,4096]{1,0:T(8,128)(2,1)} %refs_1_.1, bf16[32,4096]{1,0:T(8,128)(2,1)} %copy-done.1, bf16[32,4096]{1,0:T(8,128)(2,1)} %copy-done, bf16[32,4096]{1,0:T(8,128)(2,1)} %copy-done.2, bf16[4,256,256]{2,1,0:T(8,128)(2,1)} %constant.6.clone.refs_5_, ...), custom_call_target="tpu_custom_call" | custom-call | flops 4026531840 | bytes 3145728 | tf_op jit(solution)/shard_map/pallas_call | solution.py:280
  (2 shorter events, 0.0 us)
Async XLA Ops:
  0.0 15.6 %collective-permute-start.1 = (bf16[32,4096]{1,0:T(8,128)(2,1)}, bf16[32,4096]{1,0:T(8,128)(2,1)S(1)}, u32[]{:S(2)}, u32[]{:S(2)}) collective-permute-start(bf16[32,4096]{1,0:T(8,128)(2,1)} %refs_1_.1), channel_id=1, source_target_pairs={{16,0},{24,8},{0,16},{8,24},{17,1},{25,9},{1,17},{9,25},{18,2},{26... | collective-permute-start | bytes 786440 | tf_op jit(solution)/shard_map/ppermute | solution.py:313
  3.0 12.6 %collective-permute-start = (bf16[32,4096]{1,0:T(8,128)(2,1)}, bf16[32,4096]{1,0:T(8,128)(2,1)S(1)}, u32[]{:S(2)}, u32[]{:S(2)}) collective-permute-start(bf16[32,4096]{1,0:T(8,128)(2,1)} %refs_1_.1), channel_id=1, source_target_pairs={{8,0},{0,8},{24,16},{16,24},{9,1},{1,9},{25,17},{17,25},{10,2},{2,... | collective-permute-start | bytes 786440 | tf_op jit(solution)/shard_map/ppermute | solution.py:313
  4.5 11.8 %collective-permute-start.2 = (bf16[32,4096]{1,0:T(8,128)(2,1)}, bf16[32,4096]{1,0:T(8,128)(2,1)S(1)}, u32[]{:S(2)}, u32[]{:S(2)}) collective-permute-start(bf16[32,4096]{1,0:T(8,128)(2,1)} %refs_1_.1), channel_id=1, source_target_pairs={{24,0},{16,8},{8,16},{0,24},{25,1},{17,9},{9,17},{1,25},{26,2},{18... | collective-permute-start | bytes 786440 | tf_op jit(solution)/shard_map/ppermute | solution.py:313
  15.6 0.7 %copy-start = (bf16[32,4096]{1,0:T(8,128)(2,1)}, bf16[32,4096]{1,0:T(8,128)(2,1)S(1)}, u32[]{:S(2)}) copy-start(bf16[32,4096]{1,0:T(8,128)(2,1)S(1)} %collective-permute-done.1.refs_3_) | copy-start | bytes 786436
  15.6 0.8 %copy-start.1 = (bf16[32,4096]{1,0:T(8,128)(2,1)}, bf16[32,4096]{1,0:T(8,128)(2,1)S(1)}, u32[]{:S(2)}) copy-start(bf16[32,4096]{1,0:T(8,128)(2,1)S(1)} %collective-permute-done.refs_2_) | copy-start | bytes 786436
  16.4 0.7 %copy-start.2 = (bf16[32,4096]{1,0:T(8,128)(2,1)}, bf16[32,4096]{1,0:T(8,128)(2,1)S(1)}, u32[]{:S(2)}) copy-start(bf16[32,4096]{1,0:T(8,128)(2,1)S(1)} %collective-permute-done.2.refs_4_) | copy-start | bytes 786436

commit v14 on v13

--- a/solution.py
+++ b/solution.py
@@ -69,13 +69,15 @@
 
 
 def gather_kernel(aways, recs, *refs):
-    codes, *refs = refs
-    share = codes.shape[2]
+    codes_ref, *refs = refs
     peers = len(aways)
     traces, refs = refs[:peers], refs[peers:]
-    table_refs, out, loaded, refs = refs[:6], refs[6], refs[7:14], refs[14:]
-    own, forward, inverse, order, flags, over_shots, back_rows = loaded
-    tiles, folds, spectra, waved, mixed, ready, table_sem, out_sem = refs
+    table_refs, out, codes, records, loaded, refs = (
+        refs[:6], refs[6], refs[7], refs[8], refs[9:15], refs[15:]
+    )
+    share = codes.shape[2]
+    forward, inverse, order, flags, over_shots, back_rows = loaded
+    tiles, folds, spectra, waved, mixed, ready, codes_sem, record_sem, table_sem, out_sem = refs
     rec_rows, block_len = traces[0].shape
     shots, half = flags.shape
     window = 2 * half
@@ -89,19 +91,27 @@
     f32, bf16 = jnp.float32, jnp.bfloat16
     here = lax.axis_index("tm")
 
+    codes_copy = pltpu.make_async_copy(codes_ref, codes, codes_sem)
+    record_copies = [
+        pltpu.make_async_copy(block, records.at[index], record_sem.at[index])
+        for index, block in enumerate(traces)
+    ]
     table_copies = [
         pltpu.make_async_copy(table, place, table_sem.at[index])
-        for index, (table, place) in enumerate(zip((traces[0], *table_refs), loaded))
+        for index, (table, place) in enumerate(zip(table_refs, loaded))
     ]
-    for index in (0, 6, 1, 4, 3, 5, 2):
+    codes_copy.start()
+    for copy in record_copies:
+        copy.start()
+    for index in (5, 0, 3, 2, 4, 1):
         table_copies[index].start()
 
-    for away, block in [*zip(aways[1:], traces[1:]), (0, own)]:
-        if away == 0:
-            table_copies[0].wait()
+    for index, away in enumerate(aways):
+        record_copies[index].wait()
         base = partner(here, away, peers) * per_block
         for tile in range(per_block):
-            tiles[base + tile] = block[:, tile * LANES : (tile + 1) * LANES]
+            tiles[base + tile] = records[index, :, tile * LANES : (tile + 1) * LANES]
+    codes_copy.wait()
     for tile in range(wide):
         tiles[peers * per_block + tile] = jnp.zeros((rec_rows, LANES), bf16)
 
@@ -127,8 +137,8 @@
         ]
         return [[pltpu.roll(tile, turn, 1) for tile in pair] for pair in pairs]
 
-    def cut_block(block, rows):
-        for item in range(BLOCK):
+    def cut_block(block, rows, items=range(BLOCK)):
+        for item in items:
             for part, pair in enumerate(cut(block * BLOCK + item, rows)):
                 for side_of, tile in enumerate(pair):
                     folds[block % 2, part, side_of, item * recs : (item + 1) * recs] = tile
@@ -136,16 +146,15 @@
     def columns(tile):
         return slice(tile * LANES, (tile + 1) * LANES)
 
-    def transform_block(block):
-        for part in parts:
-            panel = jnp.concatenate([folds[block % 2, part, side_of] for side_of in range(2)], axis=1)
-            found = jnp.dot(panel, forward[part], preferred_element_type=f32)
-            for item in range(BLOCK):
-                row = (block * BLOCK + item) * pitch
-                for side_of in range(2):
-                    spectra[2 * part + side_of, row : row + recs] = found[
-                        item * recs : (item + 1) * recs, columns(side_of)
-                    ]
+    def transform_block(block, part):
+        panel = jnp.concatenate([folds[block % 2, part, side_of] for side_of in range(2)], axis=1)
+        found = jnp.dot(panel, forward[part], preferred_element_type=f32)
+        for item in range(BLOCK):
+            row = (block * BLOCK + item) * pitch
+            for side_of in range(2):
+                spectra[2 * part + side_of, row : row + recs] = found[
+                    item * recs : (item + 1) * recs, columns(side_of)
+                ]
 
     def over(rec, keep):
         at = pl.ds(rec, shots, stride=pitch)
@@ -228,18 +237,19 @@
         rows = slice(chunk * recs, (chunk + 1) * recs)
         cut_block(0, rows)
         if chunk == 0:
-            table_copies[6].wait()
+            table_copies[5].wait()
             back = jnp.concatenate(
                 [jnp.dot(owned, back_rows[part], preferred_element_type=f32) for part in range(2)],
                 axis=0,
             ).astype(bf16)
-            table_copies[1].wait()
+            table_copies[0].wait()
         for block in range(blocks):
-            if block + 1 < blocks:
-                cut_block(block + 1, rows)
-            transform_block(block)
+            for part in parts:
+                transform_block(block, part)
+                if block + 1 < blocks:
+                    cut_block(block + 1, rows, range(part * BLOCK // mid, (part + 1) * BLOCK // mid))
             if chunk == 0 and block == 0:
-                for index in (3, 4, 5):
+                for index in (2, 3, 4):
                     table_copies[index].wait()
                 kept = jnp.dot(
                     flags[...].astype(f32).astype(bf16), order[...], preferred_element_type=f32
@@ -250,7 +260,7 @@
         for rec in range(recs):
             under(rec, back)
         if chunk == 0:
-            table_copies[2].wait()
+            table_copies[1].wait()
         for first in range(0, slots, group):
             restore(chunk, first)
     for copy in out_copies:
@@ -266,8 +276,6 @@
     slots = 2 * shots // peers
     total = peers * block_len
     recs = rec_rows if shots * rec_rows * window <= 4 << 20 else BLOCK
-    smem = pl.BlockSpec(memory_space=pltpu.SMEM)
-    vmem = pl.BlockSpec(memory_space=pltpu.VMEM)
     hbm = pl.BlockSpec(memory_space=pltpu.HBM)
     flops = 2 * rec_rows * (
         shots * window * half
@@ -280,10 +288,11 @@
     return pl.pallas_call(
         functools.partial(gather_kernel, aways, recs),
         out_shape=jax.ShapeDtypeStruct((slots, rec_rows, window), bf16),
-        in_specs=[smem, hbm] + [vmem] * (peers - 1) + [hbm] * 6,
+        in_specs=[hbm] * (1 + peers + len(shared)),
         out_specs=hbm,
         scratch_shapes=[
-            pltpu.VMEM((rec_rows, block_len), bf16),
+            pltpu.SMEM(codes.shape, jnp.int32),
+            pltpu.VMEM((peers, rec_rows, block_len), bf16),
             *[pltpu.VMEM(table.shape, table.dtype) for table in shared],
             pltpu.VMEM(((total + window) // LANES, rec_rows, LANES), bf16),
             pltpu.VMEM((2, half // LANES, 2, BLOCK * recs, LANES), bf16),
@@ -291,7 +300,9 @@
             pltpu.VMEM((half // LANES, recs, 2 * shots, LANES), bf16),
             pltpu.VMEM((window // LANES, slots * (recs + 1), LANES), jnp.float32),
             pltpu.VMEM((slots, rec_rows, window), bf16),
-            pltpu.SemaphoreType.DMA((7,)),
+            pltpu.SemaphoreType.DMA,
+            pltpu.SemaphoreType.DMA((peers,)),
+            pltpu.SemaphoreType.DMA((len(shared),)),
             pltpu.SemaphoreType.DMA((rec_rows // recs, slots)),
         ],
         compiler_params=pltpu.CompilerParams(vmem_limit_bytes=60 << 20),

time: 25.6 us -> 25.1 us (0.980)
  Pallas kernels: 8.33 us -> 7.86 us
    pallas_call x1, Pallas kernels: 8.33 us -> 7.86 us  [filter_gathers(): pl.pallas_call(functools.partial(gather_kernel, aways, recs), out_shape=j...]
where the time goes in v14:
time: 25.1 us; the launch traced here: 24.9 us
  blocking collectives  10.4 us (41%)
  Pallas kernels  7.86 us (31%)
  starting transfers between devices  4.46 us (18%)
  local copies, waits for them, and re-layouts  0.78 us (3%)
  other arithmetic  0.76 us (3%)
  waiting for transfers between devices  0.69 us (3%)
    psum x1, blocking collectives, on_device(): codes = lax.psum(jnp.where(line == lax.axis_index('line'), both, 0), 'line')  10.4 us
    pallas_call x1, Pallas kernels, filter_gathers(): pl.pallas_call(functools.partial(gather_kernel, aways, recs), out_shape=j...  7.86 us
    ppermute x3, starting transfers between devices, on_device(): lax.ppermute(station_traces, 'tm', [(partner(index, away, peers), index)...  4.46 us
    unnamed x6, local copies, waits for them, and re-layouts  0.78 us
    select_n x1, other arithmetic, on_device(): codes = lax.psum(jnp.where(line == lax.axis_index('line'), both, 0), 'line')  0.75 us
    ppermute x3, waiting for transfers between devices, on_device(): lax.ppermute(station_traces, 'tm', [(partner(index, away, peers), index)...  0.69 us
  transfers between devices with their start and end apart: 3, of which 1 were waited for; matrix products, arithmetic and copies ran while one was open for 3% of the time, Pallas kernels for 0%

profile of v14, /device:TPU:0, one launch (start us, length us, event | category | flops | bytes accessed | tf_op | source)
XLA Modules:
  0.0 24.9 jit_solution(2327121308174174926)
XLA Ops:
  0.0 3.0 %collective-permute-start.1 = (bf16[32,4096]{1,0:T(8,128)(2,1)}, bf16[32,4096]{1,0:T(8,128)(2,1)S(1)}, u32[]{:S(2)}, u32[]{:S(2)}) collective-permute-start(bf16[32,4096]{1,0:T(8,128)(2,1)} %refs_1_.1), channel_id=1, source_target_pairs={{16,0},{24,8},{0,16},{8,24},{17,1},{25,9},{1,17},{9,25},{18,2},{26... | collective-permute-start | bytes 786440 | tf_op jit(solution)/shard_map/ppermute | solution.py:324
  3.0 1.5 %collective-permute-start = (bf16[32,4096]{1,0:T(8,128)(2,1)}, bf16[32,4096]{1,0:T(8,128)(2,1)S(1)}, u32[]{:S(2)}, u32[]{:S(2)}) collective-permute-start(bf16[32,4096]{1,0:T(8,128)(2,1)} %refs_1_.1), channel_id=1, source_target_pairs={{8,0},{0,8},{24,16},{16,24},{9,1},{1,9},{25,17},{17,25},{10,2},{2,... | collective-permute-start | bytes 786440 | tf_op jit(solution)/shard_map/ppermute | solution.py:324
  4.5 0.0 collective-permute-start.2
  4.5 0.7 %select_select_fusion = s32[2,8,8]{2,1,0:T(8,128)S(1)} fusion(s32[8]{0:T(128)} %param.11, s32[8]{0:T(128)} %param.10, pred[2]{0:T(512)(128)(4,1)S(1)} %iota_compare_fusion, pred[8]{0:T(512)(128)(4,1)S(1)} %iota_compare_fusion.1), kind=kLoop, calls=%fused_computation | loop fusion | flops 256 | bytes 586 | tf_op jit(solution)/shard_map/jit(_where)/select_n | solution.py:335
  5.2 10.4 %psum.7.refs_0_ = s32[2,8,8]{2,1,0:T(8,128)} all-reduce(s32[2,8,8]{2,1,0:T(8,128)S(1)} %select_select_fusion), channel_id=1, replica_groups=mesh['tm'=4,'line'=8] {'line'}, use_global_device_ids=true, to_apply=%region_0.1 | all-reduce | flops 128 | bytes 1024 | tf_op jit(solution)/shard_map/psum | solution.py:335
  15.6 0.0 collective-permute-done.1.refs_3_
  15.6 0.0 copy-start
  15.6 0.0 collective-permute-done.refs_2_
  15.6 0.0 copy-start.1
  15.6 0.7 %collective-permute-done.2.refs_4_ = bf16[32,4096]{1,0:T(8,128)(2,1)S(1)} collective-permute-done((bf16[32,4096]{1,0:T(8,128)(2,1)}, bf16[32,4096]{1,0:T(8,128)(2,1)S(1)}, u32[]{:S(2)}, u32[]{:S(2)}) %collective-permute-start.2) | collective-permute-done | bytes 262176 | tf_op jit(solution)/shard_map/ppermute | solution.py:324
  16.3 0.0 copy-done
  16.3 0.1 copy-done.1
  16.4 0.0 copy-start.2
  16.4 0.7 %copy-done.2 = bf16[32,4096]{1,0:T(8,128)(2,1)} copy-done((bf16[32,4096]{1,0:T(8,128)(2,1)}, bf16[32,4096]{1,0:T(8,128)(2,1)S(1)}, u32[]{:S(2)}) %copy-start.2) | copy-done | bytes 262168
  17.1 7.9 %shard_map.91 = bf16[32,32,1024]{2,1,0:T(8,128)(2,1)} custom-call(s32[2,8,8]{2,1,0:T(8,128)} %psum.7.refs_0_, bf16[32,4096]{1,0:T(8,128)(2,1)} %refs_1_.1, bf16[32,4096]{1,0:T(8,128)(2,1)} %copy-done.1, bf16[32,4096]{1,0:T(8,128)(2,1)} %copy-done, bf16[32,4096]{1,0:T(8,128)(2,1)} %copy-done.2, bf16[4,256,256]{2,1,0:T(8,128)(2,1)} %constant.6.clone.refs_5_, ...), custom_call_target="tpu_custom_call" | custom-call | flops 4026531840 | bytes 3145728 | tf_op jit(solution)/shard_map/pallas_call | solution.py:288
  (2 shorter events, 0.0 us)
Async XLA Ops:
  0.0 15.6 %collective-permute-start.1 = (bf16[32,4096]{1,0:T(8,128)(2,1)}, bf16[32,4096]{1,0:T(8,128)(2,1)S(1)}, u32[]{:S(2)}, u32[]{:S(2)}) collective-permute-start(bf16[32,4096]{1,0:T(8,128)(2,1)} %refs_1_.1), channel_id=1, source_target_pairs={{16,0},{24,8},{0,16},{8,24},{17,1},{25,9},{1,17},{9,25},{18,2},{26... | collective-permute-start | bytes 786440 | tf_op jit(solution)/shard_map/ppermute | solution.py:324
  3.0 12.6 %collective-permute-start = (bf16[32,4096]{1,0:T(8,128)(2,1)}, bf16[32,4096]{1,0:T(8,128)(2,1)S(1)}, u32[]{:S(2)}, u32[]{:S(2)}) collective-permute-start(bf16[32,4096]{1,0:T(8,128)(2,1)} %refs_1_.1), channel_id=1, source_target_pairs={{8,0},{0,8},{24,16},{16,24},{9,1},{1,9},{25,17},{17,25},{10,2},{2,... | collective-permute-start | bytes 786440 | tf_op jit(solution)/shard_map/ppermute | solution.py:324
  4.5 11.8 %collective-permute-start.2 = (bf16[32,4096]{1,0:T(8,128)(2,1)}, bf16[32,4096]{1,0:T(8,128)(2,1)S(1)}, u32[]{:S(2)}, u32[]{:S(2)}) collective-permute-start(bf16[32,4096]{1,0:T(8,128)(2,1)} %refs_1_.1), channel_id=1, source_target_pairs={{24,0},{16,8},{8,16},{0,24},{25,1},{17,9},{9,17},{1,25},{26,2},{18... | collective-permute-start | bytes 786440 | tf_op jit(solution)/shard_map/ppermute | solution.py:324
  15.6 0.7 %copy-start = (bf16[32,4096]{1,0:T(8,128)(2,1)}, bf16[32,4096]{1,0:T(8,128)(2,1)S(1)}, u32[]{:S(2)}) copy-start(bf16[32,4096]{1,0:T(8,128)(2,1)S(1)} %collective-permute-done.1.refs_3_) | copy-start | bytes 786436
  15.6 0.8 %copy-start.1 = (bf16[32,4096]{1,0:T(8,128)(2,1)}, bf16[32,4096]{1,0:T(8,128)(2,1)S(1)}, u32[]{:S(2)}) copy-start(bf16[32,4096]{1,0:T(8,128)(2,1)S(1)} %collective-permute-done.refs_2_) | copy-start | bytes 786436
  16.4 0.7 %copy-start.2 = (bf16[32,4096]{1,0:T(8,128)(2,1)}, bf16[32,4096]{1,0:T(8,128)(2,1)S(1)}, u32[]{:S(2)}) copy-start(bf16[32,4096]{1,0:T(8,128)(2,1)S(1)} %collective-permute-done.2.refs_4_) | copy-start | bytes 786436

commit v15 on v14

--- a/solution.py
+++ b/solution.py
@@ -255,10 +255,12 @@
                     flags[...].astype(f32).astype(bf16), order[...], preferred_element_type=f32
                 ).astype(bf16)
                 keep = jnp.concatenate([kept, kept], axis=0)
-        for rec in range(recs):
-            over(rec, keep)
-        for rec in range(recs):
-            under(rec, back)
+        lag = recs // 2
+        for rec in range(recs + lag):
+            if rec < recs:
+                over(rec, keep)
+            if rec >= lag:
+                under(rec - lag, back)
         if chunk == 0:
             table_copies[1].wait()
         for first in range(0, slots, group):

time: 25.1 us -> 25.1 us (level)
  no operation moved by 1% of the time
where the time goes in v15:
time: 25.1 us; the launch traced here: 24.9 us
  blocking collectives  10.4 us (41%)
  Pallas kernels  7.86 us (31%)
  starting transfers between devices  4.46 us (18%)
  local copies, waits for them, and re-layouts  0.78 us (3%)
  other arithmetic  0.76 us (3%)
  waiting for transfers between devices  0.69 us (3%)
    psum x1, blocking collectives, on_device(): codes = lax.psum(jnp.where(line == lax.axis_index('line'), both, 0), 'line')  10.4 us
    pallas_call x1, Pallas kernels, filter_gathers(): pl.pallas_call(functools.partial(gather_kernel, aways, recs), out_shape=j...  7.86 us
    ppermute x3, starting transfers between devices, on_device(): lax.ppermute(station_traces, 'tm', [(partner(index, away, peers), index)...  4.46 us
    unnamed x6, local copies, waits for them, and re-layouts  0.78 us
    select_n x1, other arithmetic, on_device(): codes = lax.psum(jnp.where(line == lax.axis_index('line'), both, 0), 'line')  0.75 us
    ppermute x3, waiting for transfers between devices, on_device(): lax.ppermute(station_traces, 'tm', [(partner(index, away, peers), index)...  0.69 us
  transfers between devices with their start and end apart: 3, of which 1 were waited for; matrix products, arithmetic and copies ran while one was open for 3% of the time, Pallas kernels for 0%

profile of v15, /device:TPU:0, one launch (start us, length us, event | category | flops | bytes accessed | tf_op | source)
XLA Modules:
  0.0 24.9 jit_solution(5483547059821018957)
XLA Ops:
  0.0 3.0 %collective-permute-start.1 = (bf16[32,4096]{1,0:T(8,128)(2,1)}, bf16[32,4096]{1,0:T(8,128)(2,1)S(1)}, u32[]{:S(2)}, u32[]{:S(2)}) collective-permute-start(bf16[32,4096]{1,0:T(8,128)(2,1)} %refs_1_.1), channel_id=1, source_target_pairs={{16,0},{24,8},{0,16},{8,24},{17,1},{25,9},{1,17},{9,25},{18,2},{26... | collective-permute-start | bytes 786440 | tf_op jit(solution)/shard_map/ppermute | solution.py:326
  3.0 1.5 %collective-permute-start = (bf16[32,4096]{1,0:T(8,128)(2,1)}, bf16[32,4096]{1,0:T(8,128)(2,1)S(1)}, u32[]{:S(2)}, u32[]{:S(2)}) collective-permute-start(bf16[32,4096]{1,0:T(8,128)(2,1)} %refs_1_.1), channel_id=1, source_target_pairs={{8,0},{0,8},{24,16},{16,24},{9,1},{1,9},{25,17},{17,25},{10,2},{2,... | collective-permute-start | bytes 786440 | tf_op jit(solution)/shard_map/ppermute | solution.py:326
  4.5 0.0 collective-permute-start.2
  4.5 0.7 %select_select_fusion = s32[2,8,8]{2,1,0:T(8,128)S(1)} fusion(s32[8]{0:T(128)} %param.11, s32[8]{0:T(128)} %param.10, pred[2]{0:T(512)(128)(4,1)S(1)} %iota_compare_fusion, pred[8]{0:T(512)(128)(4,1)S(1)} %iota_compare_fusion.1), kind=kLoop, calls=%fused_computation | loop fusion | flops 256 | bytes 586 | tf_op jit(solution)/shard_map/jit(_where)/select_n | solution.py:337
  5.2 10.4 %psum.7.refs_0_ = s32[2,8,8]{2,1,0:T(8,128)} all-reduce(s32[2,8,8]{2,1,0:T(8,128)S(1)} %select_select_fusion), channel_id=1, replica_groups=mesh['tm'=4,'line'=8] {'line'}, use_global_device_ids=true, to_apply=%region_0.1 | all-reduce | flops 128 | bytes 1024 | tf_op jit(solution)/shard_map/psum | solution.py:337
  15.6 0.0 collective-permute-done.1.refs_3_
  15.6 0.0 copy-start
  15.6 0.0 collective-permute-done.refs_2_
  15.6 0.0 copy-start.1
  15.6 0.7 %collective-permute-done.2.refs_4_ = bf16[32,4096]{1,0:T(8,128)(2,1)S(1)} collective-permute-done((bf16[32,4096]{1,0:T(8,128)(2,1)}, bf16[32,4096]{1,0:T(8,128)(2,1)S(1)}, u32[]{:S(2)}, u32[]{:S(2)}) %collective-permute-start.2) | collective-permute-done | bytes 262176 | tf_op jit(solution)/shard_map/ppermute | solution.py:326
  16.3 0.0 copy-done
  16.3 0.1 copy-done.1
  16.4 0.0 copy-start.2
  16.4 0.7 %copy-done.2 = bf16[32,4096]{1,0:T(8,128)(2,1)} copy-done((bf16[32,4096]{1,0:T(8,128)(2,1)}, bf16[32,4096]{1,0:T(8,128)(2,1)S(1)}, u32[]{:S(2)}) %copy-start.2) | copy-done | bytes 262168
  17.1 7.9 %shard_map.91 = bf16[32,32,1024]{2,1,0:T(8,128)(2,1)} custom-call(s32[2,8,8]{2,1,0:T(8,128)} %psum.7.refs_0_, bf16[32,4096]{1,0:T(8,128)(2,1)} %refs_1_.1, bf16[32,4096]{1,0:T(8,128)(2,1)} %copy-done.1, bf16[32,4096]{1,0:T(8,128)(2,1)} %copy-done, bf16[32,4096]{1,0:T(8,128)(2,1)} %copy-done.2, bf16[4,256,256]{2,1,0:T(8,128)(2,1)} %constant.6.clone.refs_5_, ...), custom_call_target="tpu_custom_call" | custom-call | flops 4026531840 | bytes 3145728 | tf_op jit(solution)/shard_map/pallas_call | solution.py:290
  (2 shorter events, 0.0 us)
Async XLA Ops:
  0.0 15.6 %collective-permute-start.1 = (bf16[32,4096]{1,0:T(8,128)(2,1)}, bf16[32,4096]{1,0:T(8,128)(2,1)S(1)}, u32[]{:S(2)}, u32[]{:S(2)}) collective-permute-start(bf16[32,4096]{1,0:T(8,128)(2,1)} %refs_1_.1), channel_id=1, source_target_pairs={{16,0},{24,8},{0,16},{8,24},{17,1},{25,9},{1,17},{9,25},{18,2},{26... | collective-permute-start | bytes 786440 | tf_op jit(solution)/shard_map/ppermute | solution.py:326
  3.0 12.6 %collective-permute-start = (bf16[32,4096]{1,0:T(8,128)(2,1)}, bf16[32,4096]{1,0:T(8,128)(2,1)S(1)}, u32[]{:S(2)}, u32[]{:S(2)}) collective-permute-start(bf16[32,4096]{1,0:T(8,128)(2,1)} %refs_1_.1), channel_id=1, source_target_pairs={{8,0},{0,8},{24,16},{16,24},{9,1},{1,9},{25,17},{17,25},{10,2},{2,... | collective-permute-start | bytes 786440 | tf_op jit(solution)/shard_map/ppermute | solution.py:326
  4.5 11.8 %collective-permute-start.2 = (bf16[32,4096]{1,0:T(8,128)(2,1)}, bf16[32,4096]{1,0:T(8,128)(2,1)S(1)}, u32[]{:S(2)}, u32[]{:S(2)}) collective-permute-start(bf16[32,4096]{1,0:T(8,128)(2,1)} %refs_1_.1), channel_id=1, source_target_pairs={{24,0},{16,8},{8,16},{0,24},{25,1},{17,9},{9,17},{1,25},{26,2},{18... | collective-permute-start | bytes 786440 | tf_op jit(solution)/shard_map/ppermute | solution.py:326
  15.6 0.7 %copy-start = (bf16[32,4096]{1,0:T(8,128)(2,1)}, bf16[32,4096]{1,0:T(8,128)(2,1)S(1)}, u32[]{:S(2)}) copy-start(bf16[32,4096]{1,0:T(8,128)(2,1)S(1)} %collective-permute-done.1.refs_3_) | copy-start | bytes 786436
  15.6 0.8 %copy-start.1 = (bf16[32,4096]{1,0:T(8,128)(2,1)}, bf16[32,4096]{1,0:T(8,128)(2,1)S(1)}, u32[]{:S(2)}) copy-start(bf16[32,4096]{1,0:T(8,128)(2,1)S(1)} %collective-permute-done.refs_2_) | copy-start | bytes 786436
  16.4 0.7 %copy-start.2 = (bf16[32,4096]{1,0:T(8,128)(2,1)}, bf16[32,4096]{1,0:T(8,128)(2,1)S(1)}, u32[]{:S(2)}) copy-start(bf16[32,4096]{1,0:T(8,128)(2,1)S(1)} %collective-permute-done.2.refs_4_) | copy-start | bytes 786436

commit v16 on v15

--- a/solution.py
+++ b/solution.py
@@ -101,17 +101,33 @@
         for index, (table, place) in enumerate(zip(table_refs, loaded))
     ]
     codes_copy.start()
+    table_copies[5].start()
     for copy in record_copies:
         copy.start()
-    for index in (5, 0, 3, 2, 4, 1):
+    for index in (0, 3, 2, 4, 1):
         table_copies[index].start()
+
+    codes_copy.wait()
+    shot_lane = lax.broadcasted_iota(jnp.int32, (1, shots), 1)
+    place_all = jnp.full((1, shots), -1, jnp.int32)
+    for shot in range(shots):
+        tick = codes[0, shot // share, shot % share]
+        mine = (tick >= here * block_len) & (tick < (here + 1) * block_len)
+        place = jnp.where(mine, codes[1, shot // share, shot % share], -1)
+        place_all = jnp.where(shot_lane == shot, place, place_all)
+    slot_row = lax.broadcasted_iota(jnp.int32, (slots, shots), 0)
+    owned = (slot_row == place_all).astype(f32).astype(bf16)
+
+    table_copies[5].wait()
+    back = jnp.concatenate(
+        [jnp.dot(owned, back_rows[part], preferred_element_type=f32) for part in range(2)], axis=0
+    ).astype(bf16)
 
     for index, away in enumerate(aways):
         record_copies[index].wait()
         base = partner(here, away, peers) * per_block
         for tile in range(per_block):
             tiles[base + tile] = records[index, :, tile * LANES : (tile + 1) * LANES]
-    codes_copy.wait()
     for tile in range(wide):
         tiles[peers * per_block + tile] = jnp.zeros((rec_rows, LANES), bf16)
 
@@ -178,20 +194,20 @@
             mixed[2 * part, to] = again[:slots, columns(part)]
             mixed[2 * part + 1, to] = again[slots:, columns(part)]
 
-    group = min(slots, 256 // recs)
+    group = BLOCK
     out_copies = []
 
-    def restore(chunk, first):
+    def restore(chunk, start, first):
         found = []
         for part in parts:
             panel = [
                 jnp.concatenate(
                     [
-                        mixed[2 * part + side_of, slot * pitch : slot * pitch + recs].astype(bf16)
+                        mixed[2 * part + side_of, slot * pitch + start : slot * pitch + start + BLOCK]
                         for slot in range(first, first + group)
                     ],
                     axis=0,
-                )
+                ).astype(bf16)
                 for side_of in range(2)
             ]
             found.append(
@@ -209,39 +225,25 @@
             -gap[:, LANES:],
             (real_gap + imag_sum) * -side,
         ]
-        rows = slice(chunk * recs, (chunk + 1) * recs)
+        base = chunk * recs + start
+        rows = slice(base, base + BLOCK)
         for tile in range(mid):
             for to, value in ((tile, even[tile] + odd[tile]), (tile + mid, even[tile] - odd[tile])):
                 ready[first : first + group, rows, columns(to)] = value.astype(bf16).reshape(
-                    group, recs, LANES
+                    group, BLOCK, LANES
                 )
-        block = (pl.ds(first, group), pl.ds(chunk * recs, recs))
+        block = (pl.ds(first, group), pl.ds(base, BLOCK))
         copy = pltpu.make_async_copy(
-            ready.at[block], out.at[block], out_sem.at[chunk, first // group]
+            ready.at[block], out.at[block], out_sem.at[base // BLOCK, first // group]
         )
         copy.start()
         out_copies.append(copy)
-
-    shot_lane = lax.broadcasted_iota(jnp.int32, (1, shots), 1)
-    place_all = jnp.full((1, shots), -1, jnp.int32)
-    for shot in range(shots):
-        tick = codes[0, shot // share, shot % share]
-        mine = (tick >= here * block_len) & (tick < (here + 1) * block_len)
-        place = jnp.where(mine, codes[1, shot // share, shot % share], -1)
-        place_all = jnp.where(shot_lane == shot, place, place_all)
-    slot_row = lax.broadcasted_iota(jnp.int32, (slots, shots), 0)
-    owned = (slot_row == place_all).astype(f32).astype(bf16)
 
     blocks = shots // BLOCK
     for chunk in range(rec_rows // recs):
         rows = slice(chunk * recs, (chunk + 1) * recs)
         cut_block(0, rows)
         if chunk == 0:
-            table_copies[5].wait()
-            back = jnp.concatenate(
-                [jnp.dot(owned, back_rows[part], preferred_element_type=f32) for part in range(2)],
-                axis=0,
-            ).astype(bf16)
             table_copies[0].wait()
         for block in range(blocks):
             for part in parts:
@@ -255,16 +257,20 @@
                     flags[...].astype(f32).astype(bf16), order[...], preferred_element_type=f32
                 ).astype(bf16)
                 keep = jnp.concatenate([kept, kept], axis=0)
+        if chunk == 0:
+            table_copies[1].wait()
         lag = recs // 2
+        wanted = [(start, first) for start in range(0, recs, BLOCK) for first in range(0, slots, group)]
         for rec in range(recs + lag):
             if rec < recs:
                 over(rec, keep)
-            if rec >= lag:
-                under(rec - lag, back)
-        if chunk == 0:
-            table_copies[1].wait()
-        for first in range(0, slots, group):
-            restore(chunk, first)
+            done = rec - lag
+            if done >= 0:
+                under(done, back)
+                if wanted[0][0] + BLOCK + 4 <= done and done % 5 == 0:
+                    restore(chunk, *wanted.pop(0))
+        for start, first in wanted:
+            restore(chunk, start, first)
     for copy in out_copies:
         copy.wait()
 
@@ -305,7 +311,7 @@
             pltpu.SemaphoreType.DMA,
             pltpu.SemaphoreType.DMA((peers,)),
             pltpu.SemaphoreType.DMA((len(shared),)),
-            pltpu.SemaphoreType.DMA((rec_rows // recs, slots)),
+            pltpu.SemaphoreType.DMA((rec_rows // BLOCK, slots // BLOCK)),
         ],
         compiler_params=pltpu.CompilerParams(vmem_limit_bytes=60 << 20),
         cost_estimate=pl.CostEstimate(

time: 25.1 us -> 24.7 us (0.984)
  Pallas kernels: 7.86 us -> 7.47 us
    pallas_call x1, Pallas kernels: 7.86 us -> 7.47 us  [filter_gathers(): pl.pallas_call(functools.partial(gather_kernel, aways, recs), out_shape=j...]
where the time goes in v16:
time: 24.7 us; the launch traced here: 24.5 us
  blocking collectives  10.4 us (42%)
  Pallas kernels  7.47 us (30%)
  starting transfers between devices  4.46 us (18%)
  local copies, waits for them, and re-layouts  0.78 us (3%)
  other arithmetic  0.76 us (3%)
  waiting for transfers between devices  0.69 us (3%)
    psum x1, blocking collectives, on_device(): codes = lax.psum(jnp.where(line == lax.axis_index('line'), both, 0), 'line')  10.4 us
    pallas_call x1, Pallas kernels, filter_gathers(): pl.pallas_call(functools.partial(gather_kernel, aways, recs), out_shape=j...  7.47 us
    ppermute x3, starting transfers between devices, on_device(): lax.ppermute(station_traces, 'tm', [(partner(index, away, peers), index)...  4.46 us
    unnamed x6, local copies, waits for them, and re-layouts  0.78 us
    select_n x1, other arithmetic, on_device(): codes = lax.psum(jnp.where(line == lax.axis_index('line'), both, 0), 'line')  0.75 us
    ppermute x3, waiting for transfers between devices, on_device(): lax.ppermute(station_traces, 'tm', [(partner(index, away, peers), index)...  0.69 us
  transfers between devices with their start and end apart: 3, of which 1 were waited for; matrix products, arithmetic and copies ran while one was open for 3% of the time, Pallas kernels for 0%

profile of v16, /device:TPU:0, one launch (start us, length us, event | category | flops | bytes accessed | tf_op | source)
XLA Modules:
  0.0 24.5 jit_solution(5289522174060442384)
XLA Ops:
  0.0 3.0 %collective-permute-start.1 = (bf16[32,4096]{1,0:T(8,128)(2,1)}, bf16[32,4096]{1,0:T(8,128)(2,1)S(1)}, u32[]{:S(2)}, u32[]{:S(2)}) collective-permute-start(bf16[32,4096]{1,0:T(8,128)(2,1)} %refs_1_.1), channel_id=1, source_target_pairs={{16,0},{24,8},{0,16},{8,24},{17,1},{25,9},{1,17},{9,25},{18,2},{26... | collective-permute-start | bytes 786440 | tf_op jit(solution)/shard_map/ppermute | solution.py:332
  3.0 1.5 %collective-permute-start = (bf16[32,4096]{1,0:T(8,128)(2,1)}, bf16[32,4096]{1,0:T(8,128)(2,1)S(1)}, u32[]{:S(2)}, u32[]{:S(2)}) collective-permute-start(bf16[32,4096]{1,0:T(8,128)(2,1)} %refs_1_.1), channel_id=1, source_target_pairs={{8,0},{0,8},{24,16},{16,24},{9,1},{1,9},{25,17},{17,25},{10,2},{2,... | collective-permute-start | bytes 786440 | tf_op jit(solution)/shard_map/ppermute | solution.py:332
  4.5 0.0 collective-permute-start.2
  4.5 0.7 %select_select_fusion = s32[2,8,8]{2,1,0:T(8,128)S(1)} fusion(s32[8]{0:T(128)} %param.11, s32[8]{0:T(128)} %param.10, pred[2]{0:T(512)(128)(4,1)S(1)} %iota_compare_fusion, pred[8]{0:T(512)(128)(4,1)S(1)} %iota_compare_fusion.1), kind=kLoop, calls=%fused_computation | loop fusion | flops 256 | bytes 586 | tf_op jit(solution)/shard_map/jit(_where)/select_n | solution.py:343
  5.2 10.4 %psum.7.refs_0_ = s32[2,8,8]{2,1,0:T(8,128)} all-reduce(s32[2,8,8]{2,1,0:T(8,128)S(1)} %select_select_fusion), channel_id=1, replica_groups=mesh['tm'=4,'line'=8] {'line'}, use_global_device_ids=true, to_apply=%region_0.1 | all-reduce | flops 128 | bytes 1024 | tf_op jit(solution)/shard_map/psum | solution.py:343
  15.6 0.0 collective-permute-done.1.refs_3_
  15.6 0.0 copy-start
  15.6 0.0 collective-permute-done.refs_2_
  15.6 0.0 copy-start.1
  15.6 0.7 %collective-permute-done.2.refs_4_ = bf16[32,4096]{1,0:T(8,128)(2,1)S(1)} collective-permute-done((bf16[32,4096]{1,0:T(8,128)(2,1)}, bf16[32,4096]{1,0:T(8,128)(2,1)S(1)}, u32[]{:S(2)}, u32[]{:S(2)}) %collective-permute-start.2) | collective-permute-done | bytes 262176 | tf_op jit(solution)/shard_map/ppermute | solution.py:332
  16.3 0.0 copy-done
  16.3 0.1 copy-done.1
  16.4 0.0 copy-start.2
  16.4 0.7 %copy-done.2 = bf16[32,4096]{1,0:T(8,128)(2,1)} copy-done((bf16[32,4096]{1,0:T(8,128)(2,1)}, bf16[32,4096]{1,0:T(8,128)(2,1)S(1)}, u32[]{:S(2)}) %copy-start.2) | copy-done | bytes 262168
  17.1 7.5 %shard_map.91 = bf16[32,32,1024]{2,1,0:T(8,128)(2,1)} custom-call(s32[2,8,8]{2,1,0:T(8,128)} %psum.7.refs_0_, bf16[32,4096]{1,0:T(8,128)(2,1)} %refs_1_.1, bf16[32,4096]{1,0:T(8,128)(2,1)} %copy-done.1, bf16[32,4096]{1,0:T(8,128)(2,1)} %copy-done, bf16[32,4096]{1,0:T(8,128)(2,1)} %copy-done.2, bf16[4,256,256]{2,1,0:T(8,128)(2,1)} %constant.6.clone.refs_5_, ...), custom_call_target="tpu_custom_call" | custom-call | flops 4026531840 | bytes 3145728 | tf_op jit(solution)/shard_map/pallas_call | solution.py:296
  (2 shorter events, 0.0 us)
Async XLA Ops:
  0.0 15.6 %collective-permute-start.1 = (bf16[32,4096]{1,0:T(8,128)(2,1)}, bf16[32,4096]{1,0:T(8,128)(2,1)S(1)}, u32[]{:S(2)}, u32[]{:S(2)}) collective-permute-start(bf16[32,4096]{1,0:T(8,128)(2,1)} %refs_1_.1), channel_id=1, source_target_pairs={{16,0},{24,8},{0,16},{8,24},{17,1},{25,9},{1,17},{9,25},{18,2},{26... | collective-permute-start | bytes 786440 | tf_op jit(solution)/shard_map/ppermute | solution.py:332
  3.0 12.6 %collective-permute-start = (bf16[32,4096]{1,0:T(8,128)(2,1)}, bf16[32,4096]{1,0:T(8,128)(2,1)S(1)}, u32[]{:S(2)}, u32[]{:S(2)}) collective-permute-start(bf16[32,4096]{1,0:T(8,128)(2,1)} %refs_1_.1), channel_id=1, source_target_pairs={{8,0},{0,8},{24,16},{16,24},{9,1},{1,9},{25,17},{17,25},{10,2},{2,... | collective-permute-start | bytes 786440 | tf_op jit(solution)/shard_map/ppermute | solution.py:332
  4.5 11.8 %collective-permute-start.2 = (bf16[32,4096]{1,0:T(8,128)(2,1)}, bf16[32,4096]{1,0:T(8,128)(2,1)S(1)}, u32[]{:S(2)}, u32[]{:S(2)}) collective-permute-start(bf16[32,4096]{1,0:T(8,128)(2,1)} %refs_1_.1), channel_id=1, source_target_pairs={{24,0},{16,8},{8,16},{0,24},{25,1},{17,9},{9,17},{1,25},{26,2},{18... | collective-permute-start | bytes 786440 | tf_op jit(solution)/shard_map/ppermute | solution.py:332
  15.6 0.7 %copy-start = (bf16[32,4096]{1,0:T(8,128)(2,1)}, bf16[32,4096]{1,0:T(8,128)(2,1)S(1)}, u32[]{:S(2)}) copy-start(bf16[32,4096]{1,0:T(8,128)(2,1)S(1)} %collective-permute-done.1.refs_3_) | copy-start | bytes 786436
  15.6 0.8 %copy-start.1 = (bf16[32,4096]{1,0:T(8,128)(2,1)}, bf16[32,4096]{1,0:T(8,128)(2,1)S(1)}, u32[]{:S(2)}) copy-start(bf16[32,4096]{1,0:T(8,128)(2,1)S(1)} %collective-permute-done.refs_2_) | copy-start | bytes 786436
  16.4 0.7 %copy-start.2 = (bf16[32,4096]{1,0:T(8,128)(2,1)}, bf16[32,4096]{1,0:T(8,128)(2,1)S(1)}, u32[]{:S(2)}) copy-start(bf16[32,4096]{1,0:T(8,128)(2,1)S(1)} %collective-permute-done.2.refs_4_) | copy-start | bytes 786436

commit v17 on v16

--- a/solution.py
+++ b/solution.py
@@ -327,7 +327,7 @@
     tables = make_tables(2 * half, shots)
     peers = lax.axis_size("tm")
     lines = lax.axis_size("line")
-    aways = list(range(peers))
+    aways = [0, *range(2, peers)[:1], 1, *range(3, peers)]
     traces = [station_traces] + [
         lax.ppermute(
             station_traces,

time: 24.7 us -> 25.6 us (1.036)
  local copies, waits for them, and re-layouts: 0.78 us -> 1.38 us
  waiting for transfers between devices: 0.69 us -> 0.95 us
    unnamed x6, local copies, waits for them, and re-layouts: 0.78 us -> 1.38 us
    ppermute x3, waiting for transfers between devices: 0.69 us -> 0.95 us  [on_device(): lax.ppermute(station_traces, 'tm', [(partner(index, away, peers), index)...]
where the time goes in v17:
time: 25.6 us; the launch traced here: 25.4 us
  blocking collectives  10.4 us (41%)
  Pallas kernels  7.47 us (29%)
  starting transfers between devices  4.46 us (17%)
  local copies, waits for them, and re-layouts  1.38 us (5%)
  waiting for transfers between devices  0.95 us (4%)
  other arithmetic  0.76 us (3%)
    psum x1, blocking collectives, on_device(): codes = lax.psum(jnp.where(line == lax.axis_index('line'), both, 0), 'line')  10.4 us
    pallas_call x1, Pallas kernels, filter_gathers(): pl.pallas_call(functools.partial(gather_kernel, aways, recs), out_shape=j...  7.47 us
    ppermute x3, starting transfers between devices, on_device(): lax.ppermute(station_traces, 'tm', [(partner(index, away, peers), index)...  4.46 us
    unnamed x6, local copies, waits for them, and re-layouts  1.38 us
    ppermute x3, waiting for transfers between devices, on_device(): lax.ppermute(station_traces, 'tm', [(partner(index, away, peers), index)...  0.95 us
    select_n x1, other arithmetic, on_device(): codes = lax.psum(jnp.where(line == lax.axis_index('line'), both, 0), 'line')  0.75 us
  transfers between devices with their start and end apart: 3, of which 1 were waited for; matrix products, arithmetic and copies ran while one was open for 3% of the time, Pallas kernels for 0%

profile of v17, /device:TPU:0, one launch (start us, length us, event | category | flops | bytes accessed | tf_op | source)
XLA Modules:
  0.0 25.4 jit_solution(1629994852030423048)
XLA Ops:
  0.0 2.9 %collective-permute-start.1 = (bf16[32,4096]{1,0:T(8,128)(2,1)}, bf16[32,4096]{1,0:T(8,128)(2,1)S(1)}, u32[]{:S(2)}, u32[]{:S(2)}) collective-permute-start(bf16[32,4096]{1,0:T(8,128)(2,1)} %refs_1_.1), channel_id=1, source_target_pairs={{8,0},{0,8},{24,16},{16,24},{9,1},{1,9},{25,17},{17,25},{10,2},{2,... | collective-permute-start | bytes 786440 | tf_op jit(solution)/shard_map/ppermute | solution.py:332
  2.9 1.5 %collective-permute-start = (bf16[32,4096]{1,0:T(8,128)(2,1)}, bf16[32,4096]{1,0:T(8,128)(2,1)S(1)}, u32[]{:S(2)}, u32[]{:S(2)}) collective-permute-start(bf16[32,4096]{1,0:T(8,128)(2,1)} %refs_1_.1), channel_id=1, source_target_pairs={{16,0},{24,8},{0,16},{8,24},{17,1},{25,9},{1,17},{9,25},{18,2},{26... | collective-permute-start | bytes 786440 | tf_op jit(solution)/shard_map/ppermute | solution.py:332
  4.5 0.0 collective-permute-start.2
  4.5 0.7 %select_select_fusion = s32[2,8,8]{2,1,0:T(8,128)S(1)} fusion(s32[8]{0:T(128)} %param.11, s32[8]{0:T(128)} %param.10, pred[2]{0:T(512)(128)(4,1)S(1)} %iota_compare_fusion, pred[8]{0:T(512)(128)(4,1)S(1)} %iota_compare_fusion.1), kind=kLoop, calls=%fused_computation | loop fusion | flops 256 | bytes 586 | tf_op jit(solution)/shard_map/jit(_where)/select_n | solution.py:343
  5.2 10.4 %psum.7.refs_0_ = s32[2,8,8]{2,1,0:T(8,128)} all-reduce(s32[2,8,8]{2,1,0:T(8,128)S(1)} %select_select_fusion), channel_id=1, replica_groups=mesh['tm'=4,'line'=8] {'line'}, use_global_device_ids=true, to_apply=%region_0.1 | all-reduce | flops 128 | bytes 1024 | tf_op jit(solution)/shard_map/psum | solution.py:343
  15.6 0.0 collective-permute-done.1.refs_3_
  15.6 0.0 copy-start
  15.6 0.9 %collective-permute-done.refs_2_ = bf16[32,4096]{1,0:T(8,128)(2,1)S(1)} collective-permute-done((bf16[32,4096]{1,0:T(8,128)(2,1)}, bf16[32,4096]{1,0:T(8,128)(2,1)S(1)}, u32[]{:S(2)}, u32[]{:S(2)}) %collective-permute-start) | collective-permute-done | bytes 262176 | tf_op jit(solution)/shard_map/ppermute | solution.py:332
  16.5 0.0 copy-start.1
  16.5 0.0 collective-permute-done.2.refs_4_
  16.5 0.0 copy-done
  16.5 0.7 %copy-done.1 = bf16[32,4096]{1,0:T(8,128)(2,1)} copy-done((bf16[32,4096]{1,0:T(8,128)(2,1)}, bf16[32,4096]{1,0:T(8,128)(2,1)S(1)}, u32[]{:S(2)}) %copy-start.1) | copy-done | bytes 262168
  17.2 0.0 copy-start.2
  17.2 0.7 %copy-done.2 = bf16[32,4096]{1,0:T(8,128)(2,1)} copy-done((bf16[32,4096]{1,0:T(8,128)(2,1)}, bf16[32,4096]{1,0:T(8,128)(2,1)S(1)}, u32[]{:S(2)}) %copy-start.2) | copy-done | bytes 262168
  17.9 7.5 %shard_map.91 = bf16[32,32,1024]{2,1,0:T(8,128)(2,1)} custom-call(s32[2,8,8]{2,1,0:T(8,128)} %psum.7.refs_0_, bf16[32,4096]{1,0:T(8,128)(2,1)} %refs_1_.1, bf16[32,4096]{1,0:T(8,128)(2,1)} %copy-done.1, bf16[32,4096]{1,0:T(8,128)(2,1)} %copy-done, bf16[32,4096]{1,0:T(8,128)(2,1)} %copy-done.2, bf16[4,256,256]{2,1,0:T(8,128)(2,1)} %constant.6.clone.refs_5_, ...), custom_call_target="tpu_custom_call" | custom-call | flops 4026531840 | bytes 3145728 | tf_op jit(solution)/shard_map/pallas_call | solution.py:296
  (2 shorter events, 0.0 us)
Async XLA Ops:
  0.0 15.6 %collective-permute-start.1 = (bf16[32,4096]{1,0:T(8,128)(2,1)}, bf16[32,4096]{1,0:T(8,128)(2,1)S(1)}, u32[]{:S(2)}, u32[]{:S(2)}) collective-permute-start(bf16[32,4096]{1,0:T(8,128)(2,1)} %refs_1_.1), channel_id=1, source_target_pairs={{8,0},{0,8},{24,16},{16,24},{9,1},{1,9},{25,17},{17,25},{10,2},{2,... | collective-permute-start | bytes 786440 | tf_op jit(solution)/shard_map/ppermute | solution.py:332
  2.9 13.6 %collective-permute-start = (bf16[32,4096]{1,0:T(8,128)(2,1)}, bf16[32,4096]{1,0:T(8,128)(2,1)S(1)}, u32[]{:S(2)}, u32[]{:S(2)}) collective-permute-start(bf16[32,4096]{1,0:T(8,128)(2,1)} %refs_1_.1), channel_id=1, source_target_pairs={{16,0},{24,8},{0,16},{8,24},{17,1},{25,9},{1,17},{9,25},{18,2},{26... | collective-permute-start | bytes 786440 | tf_op jit(solution)/shard_map/ppermute | solution.py:332
  4.5 12.1 %collective-permute-start.2 = (bf16[32,4096]{1,0:T(8,128)(2,1)}, bf16[32,4096]{1,0:T(8,128)(2,1)S(1)}, u32[]{:S(2)}, u32[]{:S(2)}) collective-permute-start(bf16[32,4096]{1,0:T(8,128)(2,1)} %refs_1_.1), channel_id=1, source_target_pairs={{24,0},{16,8},{8,16},{0,24},{25,1},{17,9},{9,17},{1,25},{26,2},{18... | collective-permute-start | bytes 786440 | tf_op jit(solution)/shard_map/ppermute | solution.py:332
  15.6 1.0 %copy-start = (bf16[32,4096]{1,0:T(8,128)(2,1)}, bf16[32,4096]{1,0:T(8,128)(2,1)S(1)}, u32[]{:S(2)}) copy-start(bf16[32,4096]{1,0:T(8,128)(2,1)S(1)} %collective-permute-done.1.refs_3_) | copy-start | bytes 786436
  16.5 0.7 %copy-start.1 = (bf16[32,4096]{1,0:T(8,128)(2,1)}, bf16[32,4096]{1,0:T(8,128)(2,1)S(1)}, u32[]{:S(2)}) copy-start(bf16[32,4096]{1,0:T(8,128)(2,1)S(1)} %collective-permute-done.refs_2_) | copy-start | bytes 786436
  17.2 0.7 %copy-start.2 = (bf16[32,4096]{1,0:T(8,128)(2,1)}, bf16[32,4096]{1,0:T(8,128)(2,1)S(1)}, u32[]{:S(2)}) copy-start(bf16[32,4096]{1,0:T(8,128)(2,1)S(1)} %collective-permute-done.2.refs_4_) | copy-start | bytes 786436

commit v18 on v16

--- a/solution.py
+++ b/solution.py
@@ -162,14 +162,15 @@
     def columns(tile):
         return slice(tile * LANES, (tile + 1) * LANES)
 
-    def transform_block(block, part):
-        panel = jnp.concatenate([folds[block % 2, part, side_of] for side_of in range(2)], axis=1)
+    def transform_block(block, part, items):
+        at = slice(items[0] * recs, (items[-1] + 1) * recs)
+        panel = jnp.concatenate([folds[block % 2, part, side_of, at] for side_of in range(2)], axis=1)
         found = jnp.dot(panel, forward[part], preferred_element_type=f32)
-        for item in range(BLOCK):
+        for place, item in enumerate(items):
             row = (block * BLOCK + item) * pitch
             for side_of in range(2):
                 spectra[2 * part + side_of, row : row + recs] = found[
-                    item * recs : (item + 1) * recs, columns(side_of)
+                    place * recs : (place + 1) * recs, columns(side_of)
                 ]
 
     def over(rec, keep):
@@ -246,10 +247,10 @@
         if chunk == 0:
             table_copies[0].wait()
         for block in range(blocks):
-            for part in parts:
-                transform_block(block, part)
+            for turn, (part, start) in enumerate((p, q) for p in parts for q in (0, BLOCK // 2)):
+                transform_block(block, part, range(start, start + BLOCK // 2))
                 if block + 1 < blocks:
-                    cut_block(block + 1, rows, range(part * BLOCK // mid, (part + 1) * BLOCK // mid))
+                    cut_block(block + 1, rows, range(2 * turn, 2 * turn + 2))
             if chunk == 0 and block == 0:
                 for index in (2, 3, 4):
                     table_copies[index].wait()

time: 24.7 us -> 24.9 us (level)
  no operation moved by 1% of the time
where the time goes in v18:
time: 24.9 us; the launch traced here: 24.7 us
  blocking collectives  10.4 us (42%)
  Pallas kernels  7.63 us (31%)
  starting transfers between devices  4.46 us (18%)
  local copies, waits for them, and re-layouts  0.78 us (3%)
  other arithmetic  0.76 us (3%)
  waiting for transfers between devices  0.69 us (3%)
    psum x1, blocking collectives, on_device(): codes = lax.psum(jnp.where(line == lax.axis_index('line'), both, 0), 'line')  10.4 us
    pallas_call x1, Pallas kernels, filter_gathers(): pl.pallas_call(functools.partial(gather_kernel, aways, recs), out_shape=j...  7.63 us
    ppermute x3, starting transfers between devices, on_device(): lax.ppermute(station_traces, 'tm', [(partner(index, away, peers), index)...  4.46 us
    unnamed x6, local copies, waits for them, and re-layouts  0.78 us
    select_n x1, other arithmetic, on_device(): codes = lax.psum(jnp.where(line == lax.axis_index('line'), both, 0), 'line')  0.75 us
    ppermute x3, waiting for transfers between devices, on_device(): lax.ppermute(station_traces, 'tm', [(partner(index, away, peers), index)...  0.69 us
  transfers between devices with their start and end apart: 3, of which 1 were waited for; matrix products, arithmetic and copies ran while one was open for 3% of the time, Pallas kernels for 0%

profile of v18, /device:TPU:0, one launch (start us, length us, event | category | flops | bytes accessed | tf_op | source)
XLA Modules:
  0.0 24.7 jit_solution(12687511871152381341)
XLA Ops:
  0.0 3.0 %collective-permute-start.1 = (bf16[32,4096]{1,0:T(8,128)(2,1)}, bf16[32,4096]{1,0:T(8,128)(2,1)S(1)}, u32[]{:S(2)}, u32[]{:S(2)}) collective-permute-start(bf16[32,4096]{1,0:T(8,128)(2,1)} %refs_1_.1), channel_id=1, source_target_pairs={{16,0},{24,8},{0,16},{8,24},{17,1},{25,9},{1,17},{9,25},{18,2},{26... | collective-permute-start | bytes 786440 | tf_op jit(solution)/shard_map/ppermute | solution.py:333
  3.0 1.5 %collective-permute-start = (bf16[32,4096]{1,0:T(8,128)(2,1)}, bf16[32,4096]{1,0:T(8,128)(2,1)S(1)}, u32[]{:S(2)}, u32[]{:S(2)}) collective-permute-start(bf16[32,4096]{1,0:T(8,128)(2,1)} %refs_1_.1), channel_id=1, source_target_pairs={{8,0},{0,8},{24,16},{16,24},{9,1},{1,9},{25,17},{17,25},{10,2},{2,... | collective-permute-start | bytes 786440 | tf_op jit(solution)/shard_map/ppermute | solution.py:333
  4.5 0.0 collective-permute-start.2
  4.5 0.7 %select_select_fusion = s32[2,8,8]{2,1,0:T(8,128)S(1)} fusion(s32[8]{0:T(128)} %param.11, s32[8]{0:T(128)} %param.10, pred[2]{0:T(512)(128)(4,1)S(1)} %iota_compare_fusion, pred[8]{0:T(512)(128)(4,1)S(1)} %iota_compare_fusion.1), kind=kLoop, calls=%fused_computation | loop fusion | flops 256 | bytes 586 | tf_op jit(solution)/shard_map/jit(_where)/select_n | solution.py:344
  5.2 10.4 %psum.7.refs_0_ = s32[2,8,8]{2,1,0:T(8,128)} all-reduce(s32[2,8,8]{2,1,0:T(8,128)S(1)} %select_select_fusion), channel_id=1, replica_groups=mesh['tm'=4,'line'=8] {'line'}, use_global_device_ids=true, to_apply=%region_0.1 | all-reduce | flops 128 | bytes 1024 | tf_op jit(solution)/shard_map/psum | solution.py:344
  15.6 0.0 collective-permute-done.1.refs_3_
  15.6 0.0 copy-start
  15.6 0.0 collective-permute-done.refs_2_
  15.6 0.0 copy-start.1
  15.6 0.7 %collective-permute-done.2.refs_4_ = bf16[32,4096]{1,0:T(8,128)(2,1)S(1)} collective-permute-done((bf16[32,4096]{1,0:T(8,128)(2,1)}, bf16[32,4096]{1,0:T(8,128)(2,1)S(1)}, u32[]{:S(2)}, u32[]{:S(2)}) %collective-permute-start.2) | collective-permute-done | bytes 262176 | tf_op jit(solution)/shard_map/ppermute | solution.py:333
  16.3 0.0 copy-done
  16.3 0.1 copy-done.1
  16.4 0.0 copy-start.2
  16.4 0.7 %copy-done.2 = bf16[32,4096]{1,0:T(8,128)(2,1)} copy-done((bf16[32,4096]{1,0:T(8,128)(2,1)}, bf16[32,4096]{1,0:T(8,128)(2,1)S(1)}, u32[]{:S(2)}) %copy-start.2) | copy-done | bytes 262168
  17.1 7.6 %shard_map.91 = bf16[32,32,1024]{2,1,0:T(8,128)(2,1)} custom-call(s32[2,8,8]{2,1,0:T(8,128)} %psum.7.refs_0_, bf16[32,4096]{1,0:T(8,128)(2,1)} %refs_1_.1, bf16[32,4096]{1,0:T(8,128)(2,1)} %copy-done.1, bf16[32,4096]{1,0:T(8,128)(2,1)} %copy-done, bf16[32,4096]{1,0:T(8,128)(2,1)} %copy-done.2, bf16[4,256,256]{2,1,0:T(8,128)(2,1)} %constant.6.clone.refs_5_, ...), custom_call_target="tpu_custom_call" | custom-call | flops 4026531840 | bytes 3145728 | tf_op jit(solution)/shard_map/pallas_call | solution.py:297
  (2 shorter events, 0.0 us)
Async XLA Ops:
  0.0 15.6 %collective-permute-start.1 = (bf16[32,4096]{1,0:T(8,128)(2,1)}, bf16[32,4096]{1,0:T(8,128)(2,1)S(1)}, u32[]{:S(2)}, u32[]{:S(2)}) collective-permute-start(bf16[32,4096]{1,0:T(8,128)(2,1)} %refs_1_.1), channel_id=1, source_target_pairs={{16,0},{24,8},{0,16},{8,24},{17,1},{25,9},{1,17},{9,25},{18,2},{26... | collective-permute-start | bytes 786440 | tf_op jit(solution)/shard_map/ppermute | solution.py:333
  3.0 12.6 %collective-permute-start = (bf16[32,4096]{1,0:T(8,128)(2,1)}, bf16[32,4096]{1,0:T(8,128)(2,1)S(1)}, u32[]{:S(2)}, u32[]{:S(2)}) collective-permute-start(bf16[32,4096]{1,0:T(8,128)(2,1)} %refs_1_.1), channel_id=1, source_target_pairs={{8,0},{0,8},{24,16},{16,24},{9,1},{1,9},{25,17},{17,25},{10,2},{2,... | collective-permute-start | bytes 786440 | tf_op jit(solution)/shard_map/ppermute | solution.py:333
  4.5 11.8 %collective-permute-start.2 = (bf16[32,4096]{1,0:T(8,128)(2,1)}, bf16[32,4096]{1,0:T(8,128)(2,1)S(1)}, u32[]{:S(2)}, u32[]{:S(2)}) collective-permute-start(bf16[32,4096]{1,0:T(8,128)(2,1)} %refs_1_.1), channel_id=1, source_target_pairs={{24,0},{16,8},{8,16},{0,24},{25,1},{17,9},{9,17},{1,25},{26,2},{18... | collective-permute-start | bytes 786440 | tf_op jit(solution)/shard_map/ppermute | solution.py:333
  15.6 0.7 %copy-start = (bf16[32,4096]{1,0:T(8,128)(2,1)}, bf16[32,4096]{1,0:T(8,128)(2,1)S(1)}, u32[]{:S(2)}) copy-start(bf16[32,4096]{1,0:T(8,128)(2,1)S(1)} %collective-permute-done.1.refs_3_) | copy-start | bytes 786436
  15.6 0.8 %copy-start.1 = (bf16[32,4096]{1,0:T(8,128)(2,1)}, bf16[32,4096]{1,0:T(8,128)(2,1)S(1)}, u32[]{:S(2)}) copy-start(bf16[32,4096]{1,0:T(8,128)(2,1)S(1)} %collective-permute-done.refs_2_) | copy-start | bytes 786436
  16.4 0.7 %copy-start.2 = (bf16[32,4096]{1,0:T(8,128)(2,1)}, bf16[32,4096]{1,0:T(8,128)(2,1)S(1)}, u32[]{:S(2)}) copy-start(bf16[32,4096]{1,0:T(8,128)(2,1)S(1)} %collective-permute-done.2.refs_4_) | copy-start | bytes 786436
